TPU v7x, 512 devices: a whole 4x4x16 slice. The times are simulated.
512 devices in a mesh: src: 16 (over y_hi, x, core), dst: 32 (over z, y_lo).
Axes of the slice: x: 4, y: 4 (y_hi: 2, y_lo: 2; y = y_hi * 2 + y_lo), z: 16, core: 2. Of those that a mesh axis runs over, the one named last changes fastest.
Arguments:
- features: bfloat16 [98304, 256], P(('src', 'dst')), may hold values from -6 to 6
- weight: bfloat16 [256, 256], replicated, may hold values from -0.375 to 0.375
- values: bfloat16 [16, 32, 144, 128, 128], P('src', 'dst'), may hold values from -0.109375 to 0.109375
- coords: int32 [16, 32, 144, 2], P('src', 'dst'), may hold values from 0 to 47, as said below
- counts: int32 [16, 32], P('src', 'dst'), may hold values from 1 to 144, as said below
- cotangent: bfloat16 [32, 3072, 256], P('dst', 'src'), may hold values from -6 to 6
Outputs:
- activations: bfloat16 [32, 3072, 256], P('dst', 'src')
- input_grad: bfloat16 [98304, 256], P(('src', 'dst'))
- weight_grad: float32 [256, 256], replicated
Inputs may be any that keep to these rules, and one draw needn't show every extreme that they name: coords[s, d, k, 0] is below 48 and coords[s, d, k, 1] below 24; the 144 slots of one tile name distinct blocks; slots from counts[s, d] on are not part of the graph. `counts`: some tile holds exactly 144 blocks.
All inputs are finite; a program needn't handle non-finite values.
Results may differ from a plain program's by a relative error of at most 0.03.
Values may be sent and summed in bfloat16 or wider, within the bound.
No kernel may reach another device: no remote copies, remote signals or barrier semaphores. Data moves between devices by JAX's collectives and lax.ppermute only.
A program may use at most 128 MiB of HBM per device.

v0:
```python
import math

import jax
import jax.numpy as jnp
from jax import lax
from jax.sharding import PartitionSpec as P


def sum_blocks(block_values, block_coords, stop_slot, block_rows, backward, places):
    slots = block_values.shape[0]
    group = math.gcd(16, slots)
    side = block_values.shape[1]
    width = block_rows.shape[2]
    pick_ids = block_coords[:, 1] if backward else block_coords[:, 0]
    place_ids = block_coords[:, 0] if backward else block_coords[:, 1]

    def one_group(turn_index, running):
        first_slot = turn_index * group
        group_values = lax.dynamic_slice_in_dim(block_values, first_slot, group, 0)
        group_picks = lax.dynamic_slice_in_dim(pick_ids, first_slot, group, 0)
        group_places = lax.dynamic_slice_in_dim(place_ids, first_slot, group, 0)
        picked = jnp.take(block_rows, group_picks, axis=0)
        if backward:
            products = jnp.einsum(
                "gij,gjf->gif", group_values, picked, preferred_element_type=jnp.float32
            )
        else:
            products = jnp.einsum(
                "gij,gif->gjf", group_values, picked, preferred_element_type=jnp.float32
            )
        is_live = first_slot + jnp.arange(group, dtype=jnp.int32) < stop_slot
        kept = jnp.where(is_live[:, None, None], products, 0.0)
        return running.at[group_places].add(kept)

    turns = (stop_slot + group - 1) // group
    return lax.fori_loop(0, turns, one_group, jnp.zeros((places, side, width), jnp.float32))


def shards(features, weight, values, coords, counts, cotangent):
    tile_values = values[0, 0]
    tile_coords = coords[0, 0]
    tile_count = counts[0, 0]
    side = tile_values.shape[1]
    width = features.shape[1]
    dest_places = cotangent.shape[1] * lax.axis_size("src") // side
    gathered = lax.all_gather(features, "dst", axis=0, tiled=True)
    source_blocks = gathered.reshape(-1, side, width)
    source_places = source_blocks.shape[0]
    forward_terms = sum_blocks(
        tile_values, tile_coords, tile_count, source_blocks, False, dest_places
    )
    aggregated = lax.psum_scatter(
        forward_terms.reshape(-1, width).astype(jnp.bfloat16),
        "src",
        scatter_dimension=0,
        tiled=True,
    )
    preact = jnp.dot(aggregated, weight, preferred_element_type=jnp.float32)
    sigma = jax.nn.sigmoid(preact)
    activations = (preact * sigma).astype(jnp.bfloat16)
    slope = sigma * (1.0 + preact * (1.0 - sigma))
    delta = (cotangent[0].astype(jnp.float32) * slope).astype(jnp.bfloat16)
    local_grad = jnp.einsum("nf,ng->fg", aggregated, delta, preferred_element_type=jnp.float32)
    weight_grad = lax.psum(local_grad, ("src", "dst"))
    grad_agg = jnp.dot(delta, weight.T, preferred_element_type=jnp.float32).astype(jnp.bfloat16)
    dest_rows = lax.all_gather(grad_agg, "src", axis=0, tiled=True).reshape(-1, side, width)
    backward_terms = sum_blocks(
        tile_values, tile_coords, tile_count, dest_rows, True, source_places
    )
    input_grad = lax.psum_scatter(
        backward_terms.reshape(-1, width).astype(jnp.bfloat16),
        "dst",
        scatter_dimension=0,
        tiled=True,
    )
    return (activations.reshape(1, -1, width), input_grad, weight_grad)


def solution(mesh):
    in_specs = (
        P(("src", "dst"), None),
        P(),
        P("src", "dst", None, None, None),
        P("src", "dst", None, None),
        P("src", "dst"),
        P("dst", "src", None),
    )
    out_specs = (P("dst", "src", None), P(("src", "dst"), None), P())
    return jax.shard_map(shards, mesh=mesh, in_specs=in_specs, out_specs=out_specs, check_vma=False)
```

profile of v0, /device:TPU:2, one launch (start us, length us, event | category | flops | bytes accessed | tf_op | source)
XLA Modules:
  0.0 1006.1 jit_solution(14542213289443175228)
XLA Ops:
  8.6 0.8 fusion.14
  9.4 141.9 %all-gather.3.cloned.1.call-done = bf16[6144,256]{1,0:T(8,128)(2,1)} async-done(((bf16[192,256]{1,0:T(8,128)(2,1)}), bf16[6144,256]{1,0:T(8,128)(2,1)}) %all-gather.3.cloned.1.call-update) | async-done | bytes 3145744 | tf_op jit(solution)/shard_map/all_gather | solution.py:46
  151.3 2.0 broadcast_in_dim.58
  153.3 9.3 while.20
  153.4 0.7 compare_and_fusion.4
  154.1 2.5 gather_fusion
  156.7 1.6 convolution_select_fusion.4
  158.2 4.4 scatter_fusion
  162.7 3.3 convert_element_type.27
  166.0 163.0 %reduce-scatter.3.cloned.1.call-done = bf16[192,256]{1,0:T(8,128)(2,1)} async-done(((bf16[3072,256]{1,0:T(8,128)(2,1)}), bf16[192,256]{1,0:T(8,128)(2,1)}) %reduce-scatter.3.cloned.1.call-update) | async-done | bytes 98320 | tf_op jit(solution)/shard_map/reduce_scatter | solution.py:52
  329.0 1.8 fusion.12
  330.8 0.9 convolution_convert_fusion
  331.7 1.8 fusion.15
  333.6 60.6 %all-gather.5.cloned.1.call-done = bf16[3072,256]{1,0:T(8,128)(2,1)} async-done(((bf16[192,256]{1,0:T(8,128)(2,1)}), bf16[3072,256]{1,0:T(8,128)(2,1)}) %all-gather.5.cloned.1.call-update) | async-done | bytes 1572880 | tf_op jit(solution)/shard_map/all_gather | solution.py:66
  394.2 3.4 broadcast_in_dim.59
  397.6 8.9 while.21
  397.7 0.7 compare_and_fusion.5
  398.4 2.0 gather_fusion.1
  400.5 1.6 convolution_select_fusion.5
  402.0 4.5 scatter_fusion.1
  406.6 4.9 convert_element_type.34
  411.5 445.0 %all-reduce.2.cloned.1.call-done = f32[256,256]{1,0:T(8,128)} async-done(((f32[256,256]{1,0:T(8,128)}), f32[256,256]{1,0:T(8,128)}) %all-reduce.2.cloned.1.call-update) | async-done | bytes 262160 | tf_op jit(solution)/shard_map/psum | solution.py:64
  856.5 141.4 %reduce-scatter.5.cloned.1.call-done = bf16[192,256]{1,0:T(8,128)(2,1)} async-done(((bf16[6144,256]{1,0:T(8,128)(2,1)}), bf16[192,256]{1,0:T(8,128)(2,1)}) %reduce-scatter.5.cloned.1.call-update) | async-done | bytes 98320 | tf_op jit(solution)/shard_map/reduce_scatter | solution.py:70
  997.9 1.7 copy.27
  (18 shorter events, 1.1 us)
Async XLA Ops:
  7.2 321.9 %copy-start = (bf16[256,256]{1,0:T(8,128)(2,1)S(1)}, bf16[256,256]{1,0:T(8,128)(2,1)}, u32[]{:S(2)}) copy-start(bf16[256,256]{1,0:T(8,128)(2,1)} %param.11) | copy-start | bytes 393220
  7.2 144.1 %all-gather.3.cloned.1.call-start = ((), (), s32[]{:S(2)}) async-start(), calls=%async_computation.2 | async-start | bytes 3244032 | tf_op jit(solution)/shard_map/all_gather | solution.py:46
  7.9 321.1 %reduce-scatter.3.cloned.1.call-start = ((), (), s32[]{:S(2)}) async-start(), calls=%async_computation.3 | async-start | bytes 1671168 | tf_op jit(solution)/shard_map/reduce_scatter | solution.py:52
  162.7 166.4 %copy-start.1 = (bf16[1,192,256]{2,1,0:T(8,128)(2,1)S(1)}, bf16[1,192,256]{2,1,0:T(8,128)(2,1)}, u32[]{:S(2)}) copy-start(bf16[1,192,256]{2,1,0:T(8,128)(2,1)} %param.15) | copy-start | bytes 294916
  166.0 228.2 %all-gather.5.cloned.1.call-start = ((), (), s32[]{:S(2)}) async-start(), calls=%async_computation.4 | async-start | bytes 1671168 | tf_op jit(solution)/shard_map/all_gather | solution.py:66
  331.7 524.8 %all-reduce.2.cloned.1.call-start = ((), (), s32[]{:S(2)}) async-start(), calls=%async_computation.6 | async-start | bytes 524288 | tf_op jit(solution)/shard_map/psum | solution.py:64
  333.6 664.3 %reduce-scatter.5.cloned.1.call-start = ((), (), s32[]{:S(2)}) async-start(), calls=%async_computation.5 | async-start | bytes 3244032 | tf_op jit(solution)/shard_map/reduce_scatter | solution.py:70
Sparse Core Ops, SparseCore 0:
  10.1 141.1 all-gather.2
  166.1 162.8 reduce-scatter.2
  332.9 61.2 all-gather.4
  400.1 456.3 all-reduce.1
  860.0 137.8 reduce-scatter.4
where the time goes:
time: 1010 us
  waiting for transfers between devices  953 us (94%)
  other arithmetic  18.8 us (2%)
  between operations  14.5 us (1%)
  local copies, waits for them, and re-layouts  12.4 us (1%)
    psum x1, waiting for transfers between devices, shards(): weight_grad = lax.psum(local_grad, ('src', 'dst'))  445 us
    reduce_scatter x1, waiting for transfers between devices, shards(): lax.psum_scatter(forward_terms.reshape(-1, width).astype(jnp.bfloat16), '...  163 us
    all_gather x1, waiting for transfers between devices, shards(): gathered = lax.all_gather(features, 'dst', axis=0, tiled=True)  142 us
    reduce_scatter x1, waiting for transfers between devices, shards(): lax.psum_scatter(backward_terms.reshape(-1, width).astype(jnp.bfloat16),...  141 us
    all_gather x1, waiting for transfers between devices, shards(): lax.all_gather(grad_agg, 'src', axis=0, tiled=True).reshape(-1, side, width)  60.6 us
  transfers between devices with their start and end apart: 5, of which 5 were waited for; matrix products, arithmetic and copies ran while one was open for 2% of the time, Pallas kernels for 0%

commit v1 on v0

v1 whole, which is shorter than its diff:
```python
import functools

import jax
import jax.numpy as jnp
from jax import lax
from jax.experimental import pallas as pl
from jax.experimental.pallas import tpu as pltpu
from jax.sharding import PartitionSpec as P

BF16 = jnp.bfloat16
F32 = jnp.float32
NZ, NY = 16, 2
N_SRC = 16
SIDE = 128
WIDTH = 256
ROWS = 192
PAIR = NY * ROWS
GROUP = 16
VMEM_LIMIT = 40 * 1024 * 1024

STRIDE_GROUPS = [[2 * z + y for z in range(q, NZ, 4)] for q in range(4) for y in range(NY)]
Y_GROUPS = [[2 * z, 2 * z + 1] for z in range(NZ)]


def from_z(step):
    return [(((z + step) % NZ) * NY + y, z * NY + y) for z in range(NZ) for y in range(NY)]


Y_SWAP = [(d, d ^ 1) for d in range(NZ * NY)]


def live_slots(slot_count, values_ref, held, sems, one_slot):
    slots = values_ref.shape[0]
    groups = slots // GROUP

    def copy(g):
        span = pl.ds(g * GROUP, GROUP)
        return pltpu.make_async_copy(values_ref.at[span], held.at[span], sems.at[g])

    def start():
        for g in range(groups):

            @pl.when(g * GROUP < slot_count)
            def _():
                copy(g).start()

    def run():
        for g in range(groups):

            @pl.when(g * GROUP < slot_count)
            def _():
                copy(g).wait()
                live = jnp.minimum(slot_count - g * GROUP, GROUP)

                def four(i, carry):
                    one_slot([g * GROUP + 4 * i + u for u in range(4)])
                    return carry

                def single(i, carry):
                    one_slot([g * GROUP + i])
                    return carry

                lax.fori_loop(0, live // 4, four, 0)
                lax.fori_loop((live // 4) * 4, live, single, 0)

    return start, run


def block_of(ref, index):
    return ref[pl.ds(pl.multiple_of(index * SIDE, SIDE), SIDE), :]


def add_block(ref, index, term):
    span = pl.ds(pl.multiple_of(index * SIDE, SIDE), SIDE)
    ref[span, :] = ref[span, :] + term


def forward_kernel(
    meta, coords, values_ref, g0, g1, g2a, g2b, g3, out_ref, held, rows, total, value_sems, row_sems
):
    slot_count, z = meta[0], meta[1]
    slots = values_ref.shape[0]

    def one_slot(ks):
        terms = [
            lax.dot_general(
                held[k], block_of(rows, coords[k]), (((0,), (0,)), ((), ())), preferred_element_type=F32
            )
            for k in ks
        ]
        for k, term in zip(ks, terms):
            add_block(total, coords[slots + k], term)

    start, run = live_slots(slot_count, values_ref, held, value_sems, one_slot)
    copies = []
    for offset, ref, first in ((0, g0, 0), (1, g1, 0), (3, g3, 0), (2, g2a, 0), (2, g2b, 2)):
        residue = lax.rem(z + offset, 4)
        for i in range(ref.shape[0]):
            place = (residue + 4 * (first + i)) * PAIR
            copies.append(
                pltpu.make_async_copy(
                    ref.at[i],
                    rows.at[pl.ds(pl.multiple_of(place, PAIR), PAIR)],
                    row_sems.at[len(copies)],
                )
            )
    for copy in copies:
        copy.start()
    start()
    total[...] = jnp.zeros_like(total)
    for copy in copies:
        copy.wait()
    run()
    out_ref[...] = total[...].astype(BF16)


def forward_sums(meta, coords, values, parts, dest_rows):
    slots = values.shape[0]
    source_rows = NZ * PAIR
    smem = pl.BlockSpec(memory_space=pltpu.SMEM)
    anywhere = pl.BlockSpec(memory_space=pl.ANY)
    return pl.pallas_call(
        forward_kernel,
        out_shape=jax.ShapeDtypeStruct((dest_rows, WIDTH), BF16),
        in_specs=[smem, smem] + [anywhere] * 6,
        out_specs=pl.BlockSpec(memory_space=pltpu.VMEM),
        scratch_shapes=[
            pltpu.VMEM(values.shape, BF16),
            pltpu.VMEM((source_rows, WIDTH), BF16),
            pltpu.VMEM((dest_rows, WIDTH), F32),
            pltpu.SemaphoreType.DMA((slots // GROUP,)),
            pltpu.SemaphoreType.DMA((NZ,)),
        ],
        compiler_params=pltpu.CompilerParams(vmem_limit_bytes=VMEM_LIMIT),
        name="forward_sums",
    )(meta, coords, values, *parts)


def middle_kernel(terms, weight, cotangent, act_ref, message):
    agg = jnp.sum(terms[...].astype(F32), axis=0).astype(BF16)
    w = weight[...]
    preact = jnp.dot(agg, w, preferred_element_type=F32)
    sigma = jax.nn.sigmoid(preact)
    act_ref[...] = (preact * sigma).astype(BF16)
    slope = sigma * (1.0 + preact * (1.0 - sigma))
    delta = (cotangent[...].astype(F32) * slope).astype(BF16)
    grad_agg = lax.dot_general(
        delta, w, (((1,), (1,)), ((), ())), preferred_element_type=F32
    ).astype(BF16)
    local = lax.dot_general(agg, delta, (((0,), (0,)), ((), ())), preferred_element_type=F32)
    share = WIDTH // N_SRC
    for s in range(N_SRC):
        message[s, :ROWS, :] = grad_agg
        message[s, ROWS:, :] = local[s * share : (s + 1) * share, :].astype(BF16)


def middle(terms, weight, cotangent):
    share = WIDTH // N_SRC
    vmem = pl.BlockSpec(memory_space=pltpu.VMEM)
    return pl.pallas_call(
        middle_kernel,
        out_shape=(
            jax.ShapeDtypeStruct((ROWS, WIDTH), BF16),
            jax.ShapeDtypeStruct((N_SRC, ROWS + share, WIDTH), BF16),
        ),
        in_specs=[vmem] * 3,
        out_specs=(vmem, vmem),
        compiler_params=pltpu.CompilerParams(vmem_limit_bytes=VMEM_LIMIT),
        name="middle",
    )(terms, weight, cotangent)


def backward_kernel(
    meta, coords, values_ref, message, p0, p1a, p1b, p3a, p3b, p2a, p2b, wsum,
    held, rows, total, tail, value_sems, row_sems, tail_sem,
):
    slot_count, z, y = meta[0], meta[1], meta[2]
    slots = values_ref.shape[0]

    def one_slot(ks):
        terms = [
            jnp.dot(held[k], block_of(rows, coords[slots + k]), preferred_element_type=F32)
            for k in ks
        ]
        for k, term in zip(ks, terms):
            add_block(total, coords[k], term)

    start, run = live_slots(slot_count, values_ref, held, value_sems, one_slot)
    copies = [
        pltpu.make_async_copy(
            message.at[s, pl.ds(0, ROWS)], rows.at[pl.ds(s * ROWS, ROWS)], row_sems.at[s]
        )
        for s in range(N_SRC)
    ]
    share = message.shape[1] - ROWS
    tail_copy = pltpu.make_async_copy(message.at[:, pl.ds(ROWS, share)], tail, tail_sem)
    for copy in copies:
        copy.start()
    tail_copy.start()
    start()
    total[...] = jnp.zeros_like(total)
    for copy in copies:
        copy.wait()
    tail_copy.wait()
    run()
    summed = jnp.sum(tail[...].astype(F32), axis=0)
    wsum[...] = summed
    p2b[4 * ROWS :, :] = summed.astype(BF16)

    def put(ref, first_row, offset, member, other):
        place = (lax.rem(z + offset, 4) + 4 * member) * PAIR + (y if other == 0 else 1 - y) * ROWS
        chunk = total[pl.ds(pl.multiple_of(place, ROWS), ROWS), :]
        ref[first_row : first_row + ROWS, :] = chunk.astype(BF16)

    for other in range(2):
        for member in range(4):
            put(p0, (other * 4 + member) * ROWS, 0, member, other)
        for i in range(2):
            place = (other * 2 + i) * ROWS
            put(p1a, place, 1, i, other)
            put(p1b, place, 1, 2 + i, other)
            put(p3a, place, 3, i, other)
            put(p3b, place, 3, 2 + i, other)
            put(p2a, place, 2, i, other)
            put(p2b, place, 2, 2 + i, other)


def backward_sums(meta, coords, values, message):
    slots = values.shape[0]
    share = message.shape[1] - ROWS
    dest_rows = N_SRC * ROWS
    source_rows = NZ * PAIR
    smem = pl.BlockSpec(memory_space=pltpu.SMEM)
    anywhere = pl.BlockSpec(memory_space=pl.ANY)
    vmem = pl.BlockSpec(memory_space=pltpu.VMEM)
    half = jax.ShapeDtypeStruct((4 * ROWS, WIDTH), BF16)
    return pl.pallas_call(
        backward_kernel,
        out_shape=(
            jax.ShapeDtypeStruct((8 * ROWS, WIDTH), BF16),
            half, half, half, half, half,
            jax.ShapeDtypeStruct((4 * ROWS + share, WIDTH), BF16),
            jax.ShapeDtypeStruct((share, WIDTH), F32),
        ),
        in_specs=[smem, smem, anywhere, anywhere],
        out_specs=(vmem,) * 8,
        scratch_shapes=[
            pltpu.VMEM(values.shape, BF16),
            pltpu.VMEM((dest_rows, WIDTH), BF16),
            pltpu.VMEM((source_rows, WIDTH), F32),
            pltpu.VMEM((N_SRC, share, WIDTH), BF16),
            pltpu.SemaphoreType.DMA((slots // GROUP,)),
            pltpu.SemaphoreType.DMA((N_SRC,)),
            pltpu.SemaphoreType.DMA,
        ],
        compiler_params=pltpu.CompilerParams(vmem_limit_bytes=VMEM_LIMIT),
        name="backward_sums",
    )(meta, coords, values, message)


def shift(array, step):
    return lax.ppermute(array, "dst", from_z(step))


def gather_sources(features):
    own = lax.all_gather(features, "dst", axis=0, axis_index_groups=STRIDE_GROUPS)
    own = lax.all_gather(own, "dst", axis=1, tiled=True, axis_index_groups=Y_GROUPS)
    right = shift(own, 1)
    left = shift(own, -1)
    far_low = shift(right[:2], 1)
    far_high = shift(left[2:], -1)
    return own, right, far_low, far_high, left


def scatter_sources(p0, p1a, p1b, p3a, p3b, p2a, p2b, wsum):
    half = 4 * ROWS
    low = shift(p2a, -1)
    high = shift(p2b, 1)
    w1 = wsum + high[half:].astype(F32)
    w1_sent = w1.astype(BF16)
    up = jnp.concatenate([(p1a.astype(F32) + low.astype(F32)).astype(BF16), p1b, w1_sent], 0)
    down = jnp.concatenate([p3a, (p3b.astype(F32) + high[:half].astype(F32)).astype(BF16), w1_sent], 0)
    from_below = shift(up, -1)
    from_above = shift(down, 1)
    w2 = from_below[2 * half :].astype(F32) + from_above[2 * half :].astype(F32)

    def both(span):
        return from_below[span].astype(F32) + from_above[span].astype(F32)

    quarter = half // 2
    near = jnp.concatenate([both(slice(0, quarter)), both(slice(half, half + quarter))], 0)
    away = jnp.concatenate([both(slice(quarter, half)), both(slice(half + quarter, 2 * half))], 0)
    kept = p0[:half].astype(F32) + near
    sent = (p0[half:].astype(F32) + away).astype(BF16)
    sent = jnp.concatenate([sent, w2.astype(BF16)], 0)
    got = lax.ppermute(sent, "dst", Y_SWAP)
    w3 = (w2 + got[half:].astype(F32)).astype(BF16)
    mine = (kept + got[:half].astype(F32)).astype(BF16).reshape(4, ROWS, WIDTH)
    message = jnp.concatenate([mine, jnp.broadcast_to(w3, (4,) + w3.shape)], 1)
    last = lax.all_to_all(message, "dst", 0, 0, tiled=True, axis_index_groups=STRIDE_GROUPS)
    last = jnp.sum(last.astype(F32), axis=0)
    return last[:ROWS].astype(BF16), last[ROWS:]


def shards(features, weight, values, coords, counts, cotangent):
    tile_values = values[0, 0]
    pairs = coords[0, 0].T.reshape(-1)
    place = lax.axis_index("dst")
    meta = jnp.stack([counts[0, 0], place // NY, lax.rem(place, NY)]).astype(jnp.int32)
    dest_rows = cotangent.shape[1] * N_SRC

    parts = gather_sources(features)
    terms = forward_sums(meta, pairs, tile_values, parts, dest_rows)
    terms = lax.all_to_all(terms.reshape(N_SRC, ROWS, WIDTH), "src", 0, 0, tiled=True)
    activations, message = middle(terms, weight, cotangent[0])
    message = lax.all_to_all(message, "src", 0, 0, tiled=True)
    sums = backward_sums(meta, pairs, tile_values, message)
    input_grad, weight_part = scatter_sources(*sums)
    share = weight_part.shape[0]
    weight_part = jnp.broadcast_to(weight_part, (N_SRC, share, WIDTH))
    weight_grad = lax.all_to_all(weight_part, "src", 0, 0, tiled=True).reshape(WIDTH, WIDTH)
    return (activations[None], input_grad, weight_grad)


def solution(mesh):
    in_specs = (
        P(("src", "dst"), None),
        P(),
        P("src", "dst", None, None, None),
        P("src", "dst", None, None),
        P("src", "dst"),
        P("dst", "src", None),
    )
    out_specs = (P("dst", "src", None), P(("src", "dst"), None), P())
    return jax.shard_map(shards, mesh=mesh, in_specs=in_specs, out_specs=out_specs, check_vma=False)
```

time: 1010 us -> 258 us (0.26)
  the two profiles are of different devices: /device:TPU:2 before, /device:TPU:1 now
where the time goes in v1:
time: 258 us; the launch traced here: 257 us
  blocking collectives  127 us (49%)
  starting transfers between devices  55.9 us (22%)
  waiting for transfers between devices  54.5 us (21%)
  Pallas kernels  11 us (4%)
  local copies, waits for them, and re-layouts  6.11 us (2%)
    all_to_all x1, blocking collectives, shards(): lax.all_to_all(terms.reshape(N_SRC, ROWS, WIDTH), 'src', 0, 0, tiled=True)  46.1 us
    ppermute x8, waiting for transfers between devices, shift(): return lax.ppermute(array, 'dst', from_z(step))  36.9 us
    all_gather x1, blocking collectives, gather_sources(): lax.all_gather(features, 'dst', axis=0, axis_index_groups=STRIDE_GROUPS)  28 us
    all_to_all x1, blocking collectives, shards(): message = lax.all_to_all(message, 'src', 0, 0, tiled=True)  28 us
    ppermute x8, starting transfers between devices, shift(): return lax.ppermute(array, 'dst', from_z(step))  26.7 us
    all_to_all x1, starting transfers between devices, shards(): lax.all_to_all(weight_part, 'src', 0, 0, tiled=True).reshape(WIDTH, WIDTH)  19.8 us
    all_to_all x1, blocking collectives, scatter_sources(): lax.all_to_all(message, 'dst', 0, 0, tiled=True, axis_index_groups=STRIDE...  18 us
    ppermute x1, waiting for transfers between devices, scatter_sources(): got = lax.ppermute(sent, 'dst', Y_SWAP)  9.54 us
  transfers between devices with their start and end apart: 10, of which 9 were waited for; matrix products, arithmetic and copies ran while one was open for 1% of the time, Pallas kernels for 0%

profile of v1, /device:TPU:1, one launch (start us, length us, event | category | flops | bytes accessed | tf_op | source)
XLA Modules:
  0.0 257.3 jit_solution(14558389664727242165)
XLA Ops:
  0.6 28.0 %all-gather = bf16[768,256]{1,0:T(8,128)(2,1)S(1)} all-gather(bf16[192,256]{1,0:T(8,128)(2,1)} %param.6), channel_id=2, replica_groups={{0,8,16,24},{1,9,17,25},{2,10,18,26},{3,11,19,27},{4,12,20,28},{5,13,21..., dimensions={0}, use_global_device_ids=true | all-gather | bytes 491520 | tf_op jit(solution)/shard_map/all_gather | solution.py:266
  28.7 7.3 %all_gather.11.g0 = bf16[4,384,256]{2,1,0:T(8,128)(2,1)S(1)} all-gather(bf16[4,192,256]{2,1,0:T(8,128)(2,1)S(1)} %bitcast.20), channel_id=1, replica_groups={{0,1},{2,3},{4,5},{6,7},{8,9},{10,11},{12,13},{14,15},{16,17},{18,19},{..., dimensions={1}, use_global_device_ids=true | all-gather | bytes 1179648 | tf_op jit(solution)/shard_map/all_gather | solution.py:267
  35.9 1.9 collective-permute-start.2
  37.9 4.5 %collective-permute-start = (bf16[4,384,256]{2,1,0:T(8,128)(2,1)S(1)}, bf16[4,384,256]{2,1,0:T(8,128)(2,1)S(1)}, u32[]{:S(2)}, u32[]{:S(2)}) collective-permute-start(bf16[4,384,256]{2,1,0:T(8,128)(2,1)S(1)} %all_gather.11.g0), channel_id=1, source_target_pairs={{2,0},{3,1},{4,2},{5,3},{6,4},{7,5},{8,6},{9,7},{10,8},{11,9},{12,... | collective-permute-start | bytes 2359304 | tf_op jit(solution)/shard_map/ppermute | solution.py:262
  42.4 10.3 %collective-permute-done.2.g3 = bf16[4,384,256]{2,1,0:T(8,128)(2,1)S(1)} collective-permute-done((bf16[4,384,256]{2,1,0:T(8,128)(2,1)S(1)}, bf16[4,384,256]{2,1,0:T(8,128)(2,1)S(1)}, u32[]{:S(2)}, u32[]{:S(2)}) %collective-permute-start.2) | collective-permute-done | bytes 786464 | tf_op jit(solution)/shard_map/ppermute | solution.py:262
  53.5 1.9 collective-permute-start.3
  56.2 4.6 %collective-permute-start.1 = (bf16[2,384,256]{2,1,0:T(8,128)(2,1)}, bf16[2,384,256]{2,1,0:T(8,128)(2,1)}, u32[]{:S(2)}, u32[]{:S(2)}) collective-permute-start(bf16[2,384,256]{2,1,0:T(8,128)(2,1)} %slice.81), channel_id=1, source_target_pairs={{2,0},{3,1},{4,2},{5,3},{6,4},{7,5},{8,6},{9,7},{10,8},{11,9},{12,... | collective-permute-start | bytes 1179656 | tf_op jit(solution)/shard_map/ppermute | solution.py:262
  63.4 2.4 collective-permute-done.1.g2a
  65.8 2.3 copy-done
  68.1 5.7 %forward_sums.1 = bf16[3072,256]{1,0:T(8,128)(2,1)S(1)} custom-call(s32[3]{0:T(128)S(1)} %pad_add_fusion.meta, s32[288]{0:T(512)S(1)} %reshape.18.coords, bf16[144,128,128]{2,1,0:T(8,128)(2,1)S(1)} %bitcast.14, bf16[4,384,256]{2,1,0:T(8,128)(2,1)S(1)} %all_gather.11.g0, bf16[4,384,256]{2,1,0:T(8,128)(2,1)S(1)} %collective-permute-done.g1, ...), custom_call_target="tpu_custom_call" | custom-call | tf_op jit(solution)/shard_map/forward_sums/pallas_call | solution.py:122
  73.9 46.1 %all_to_all.20.terms = bf16[16,192,256]{2,1,0:T(8,128)(2,1)S(1)} all-to-all(bf16[16,192,256]{2,1,0:T(8,128)(2,1)S(1)} %bitcast.18), channel_id=1, replica_groups=mesh['src'=16,'dst'=32] {'src'}, dimensions={0} | all-to-all | bytes 3145728 | tf_op jit(solution)/shard_map/all_to_all | solution.py:314
  121.1 28.0 %all_to_all.21.message = bf16[16,208,256]{2,1,0:T(8,128)(2,1)S(1)} all-to-all(bf16[16,208,256]{2,1,0:T(8,128)(2,1)S(1)} %get-tuple-element.14), channel_id=1, replica_groups=mesh['src'=16,'dst'=32] {'src'}, dimensions={0} | all-to-all | bytes 3407872 | tf_op jit(solution)/shard_map/all_to_all | solution.py:316
  149.1 4.2 %backward_sums.1 = (bf16[1536,256]{1,0:T(8,128)(2,1)S(1)}, bf16[768,256]{1,0:T(8,128)(2,1)S(1)}, bf16[768,256]{1,0:T(8,128)(2,1)S(1)}, bf16[768,256]{1,0:T(8,128...) custom-call(s32[3]{0:T(128)S(1)} %pad_add_fusion.meta, ...), custom_call_target="tpu_custom_call" | custom-call | tf_op jit(solution)/shard_map/backward_sums/pallas_call | solution.py:237
  153.3 1.9 collective-permute-start.4
  155.2 4.6 %collective-permute-start.5 = (bf16[784,256]{1,0:T(8,128)(2,1)S(1)}, bf16[784,256]{1,0:T(8,128)(2,1)S(1)}, u32[]{:S(2)}, u32[]{:S(2)}) collective-permute-start(bf16[784,256]{1,0:T(8,128)(2,1)S(1)} %get-tuple-element.20), channel_id=1, source_target_pairs={{2,0},{3,1},{4,2},{5,3},{6,4},{7,5},{8,6},{9,7},{10,8},{11,9},{12,... | collective-permute-start | bytes 1204232 | tf_op jit(solution)/shard_map/ppermute | solution.py:262
  159.8 6.5 %collective-permute-done.4 = bf16[768,256]{1,0:T(8,128)(2,1)S(1)} collective-permute-done((bf16[768,256]{1,0:T(8,128)(2,1)S(1)}, bf16[768,256]{1,0:T(8,128)(2,1)S(1)}, u32[]{:S(2)}, u32[]{:S(2)}) %collective-permute-start.4) | collective-permute-done | bytes 393248 | tf_op jit(solution)/shard_map/ppermute | solution.py:262
  167.6 1.9 collective-permute-start.6
  169.5 5.3 %collective-permute-start.7 = (bf16[1552,256]{1,0:T(8,128)(2,1)S(1)}, bf16[1552,256]{1,0:T(8,128)(2,1)S(1)}, u32[]{:S(2)}, u32[]{:S(2)}) collective-permute-start(bf16[1552,256]{1,0:T(8,128)(2,1)S(1)} %get-tuple-element.28), channel_id=1, source_target_pairs={{2,0},{3,1},{4,2},{5,3},{6,4},{7,5},{8,6},{9,7},{10,8},{11,9},{12,... | collective-permute-start | bytes 2383880 | tf_op jit(solution)/shard_map/ppermute | solution.py:262
  174.9 14.1 %collective-permute-done.6 = bf16[1552,256]{1,0:T(8,128)(2,1)S(1)} collective-permute-done((bf16[1552,256]{1,0:T(8,128)(2,1)S(1)}, bf16[1552,256]{1,0:T(8,128)(2,1)S(1)}, u32[]{:S(2)}, u32[]{:S(2)}) %collective-permute-start.6) | collective-permute-done | bytes 794656 | tf_op jit(solution)/shard_map/ppermute | solution.py:262
  190.2 9.4 %collective-permute-start.8 = (bf16[784,256]{1,0:T(8,128)(2,1)S(1)}, bf16[784,256]{1,0:T(8,128)(2,1)S(1)}, u32[]{:S(2)}, u32[]{:S(2)}) collective-permute-start(bf16[784,256]{1,0:T(8,128)(2,1)S(1)} %pad_maximum_fusion.3), channel_id=1, source_target_pairs={{0,1},{1,0},{2,3},{3,2},{4,5},{5,4},{6,7},{7,6},{8,9},{9,8},{10,11... | collective-permute-start | bytes 1204232 | tf_op jit(solution)/shard_map/ppermute | solution.py:296
  199.6 9.5 %collective-permute-done.8 = bf16[784,256]{1,0:T(8,128)(2,1)S(1)} collective-permute-done((bf16[784,256]{1,0:T(8,128)(2,1)S(1)}, bf16[784,256]{1,0:T(8,128)(2,1)S(1)}, u32[]{:S(2)}, u32[]{:S(2)}) %collective-permute-start.8) | collective-permute-done | bytes 401440 | tf_op jit(solution)/shard_map/ppermute | solution.py:296
  209.4 18.0 %all_to_all.22 = bf16[4,208,256]{2,1,0:T(8,128)(2,1)S(1)} all-to-all(bf16[4,208,256]{2,1,0:T(8,128)(2,1)S(1)} %pad_maximum_fusion.2), channel_id=1, replica_groups={{0,8,16,24},{1,9,17,25},{2,10,18,26},{3,11,19,27},{4,12,20,28},{5,13,21..., dimensions={0} | all-to-all | bytes 851968 | tf_op jit(solution)/shard_map/all_to_all | solution.py:300
  228.1 19.8 %all-to-all-start.3 = ((f32[16,16,256]{2,1,0:T(8,128)}), f32[16,16,256]{2,1,0:T(8,128)S(1)}, u32[]{:S(2)}, u32[]{:S(2)}) async-start(f32[16,16,256]{2,1,0:T(8,128)} %broadcast_in_dim.11), calls=%async_computation.3 | async-start | bytes 524288 | tf_op jit(solution)/shard_map/all_to_all | solution.py:321
  248.6 8.0 %all-to-all-done.3 = f32[16,16,256]{2,1,0:T(8,128)S(1)} async-done(((f32[16,16,256]{2,1,0:T(8,128)}), f32[16,16,256]{2,1,0:T(8,128)S(1)}, u32[]{:S(2)}, u32[]{:S(2)}) %all-to-all-start.3) | async-done | bytes 262176 | tf_op jit(solution)/shard_map/all_to_all | solution.py:321
  (38 shorter events, 9.5 us)
Async XLA Ops:
  0.6 60.8 %copy-start.3 = (s32[1,1,144,2]{2,3,1,0:T(2,128)S(1)}, s32[1,1,144,2]{2,3,1,0:T(2,128)}, u32[]{:S(2)}) copy-start(s32[1,1,144,2]{2,3,1,0:T(2,128)} %param.9) | copy-start | bytes 3460
  35.9 16.8 %collective-permute-start.2 = (bf16[4,384,256]{2,1,0:T(8,128)(2,1)S(1)}, bf16[4,384,256]{2,1,0:T(8,128)(2,1)S(1)}, u32[]{:S(2)}, u32[]{:S(2)}) collective-permute-start(bf16[4,384,256]{2,1,0:T(8,128)(2,1)S(1)} %all_gather.11.g0), channel_id=1, source_target_pairs={{30,0},{31,1},{0,2},{1,3},{2,4},{3,5},{4,6},{5,7},{6,8},{7,9},{8,1... | collective-permute-start | bytes 2359304 | tf_op jit(solution)/shard_map/ppermute | solution.py:262
  37.9 17.5 %collective-permute-start = (bf16[4,384,256]{2,1,0:T(8,128)(2,1)S(1)}, bf16[4,384,256]{2,1,0:T(8,128)(2,1)S(1)}, u32[]{:S(2)}, u32[]{:S(2)}) collective-permute-start(bf16[4,384,256]{2,1,0:T(8,128)(2,1)S(1)} %all_gather.11.g0), channel_id=1, source_target_pairs={{2,0},{3,1},{4,2},{5,3},{6,4},{7,5},{8,6},{9,7},{10,8},{11,9},{12,... | collective-permute-start | bytes 2359304 | tf_op jit(solution)/shard_map/ppermute | solution.py:262
  52.7 96.4 %slice-start = ((s8[4718592]{0:T(1024)(128)(4,1)}), s8[524288]{0:T(1024)(128)(4,1)S(1)}, s32[]{:S(2)}) async-start(s8[4718592]{0:T(1024)(128)(4,1)} %bitcast.15), calls=%async_computation.4 | async-start | bytes 1048576
  53.5 9.9 %collective-permute-start.3 = (bf16[2,384,256]{2,1,0:T(8,128)(2,1)}, bf16[2,384,256]{2,1,0:T(8,128)(2,1)S(1)}, u32[]{:S(2)}, u32[]{:S(2)}) collective-permute-start(bf16[2,384,256]{2,1,0:T(8,128)(2,1)} %slice.82), channel_id=1, source_target_pairs={{30,0},{31,1},{0,2},{1,3},{2,4},{3,5},{4,6},{5,7},{6,8},{7,9},{8,1... | collective-permute-start | bytes 1179656 | tf_op jit(solution)/shard_map/ppermute | solution.py:262
  56.2 9.6 %collective-permute-start.1 = (bf16[2,384,256]{2,1,0:T(8,128)(2,1)}, bf16[2,384,256]{2,1,0:T(8,128)(2,1)}, u32[]{:S(2)}, u32[]{:S(2)}) collective-permute-start(bf16[2,384,256]{2,1,0:T(8,128)(2,1)} %slice.81), channel_id=1, source_target_pairs={{2,0},{3,1},{4,2},{5,3},{6,4},{7,5},{8,6},{9,7},{10,8},{11,9},{12,... | collective-permute-start | bytes 1179656 | tf_op jit(solution)/shard_map/ppermute | solution.py:262
  65.8 2.3 copy-start
  68.1 80.9 %slice-start.1 = ((s8[4718592]{0:T(1024)(128)(4,1)}), s8[4194304]{0:T(1024)(128)(4,1)S(1)}, s32[]{:S(2)}) async-start(s8[4718592]{0:T(1024)(128)(4,1)} %bitcast.15), calls=%async_computation.5 | async-start | bytes 8388608
  73.9 46.1 %copy-start.1 = (bf16[256,256]{1,0:T(8,128)(2,1)S(1)}, bf16[256,256]{1,0:T(8,128)(2,1)}, u32[]{:S(2)}) copy-start(bf16[256,256]{1,0:T(8,128)(2,1)} %weight.1) | copy-start | bytes 393220
  73.9 46.1 %copy-start.2 = (bf16[1,192,256]{2,1,0:T(8,128)(2,1)S(1)}, bf16[1,192,256]{2,1,0:T(8,128)(2,1)}, u32[]{:S(2)}) copy-start(bf16[1,192,256]{2,1,0:T(8,128)(2,1)} %param.11) | copy-start | bytes 294916
  153.3 13.0 %collective-permute-start.4 = (bf16[768,256]{1,0:T(8,128)(2,1)S(1)}, bf16[768,256]{1,0:T(8,128)(2,1)S(1)}, u32[]{:S(2)}, u32[]{:S(2)}) collective-permute-start(bf16[768,256]{1,0:T(8,128)(2,1)S(1)} %get-tuple-element.17), channel_id=1, source_target_pairs={{30,0},{31,1},{0,2},{1,3},{2,4},{3,5},{4,6},{5,7},{6,8},{7,9},{8,1... | collective-permute-start | bytes 1179656 | tf_op jit(solution)/shard_map/ppermute | solution.py:262
  155.2 12.1 %collective-permute-start.5 = (bf16[784,256]{1,0:T(8,128)(2,1)S(1)}, bf16[784,256]{1,0:T(8,128)(2,1)S(1)}, u32[]{:S(2)}, u32[]{:S(2)}) collective-permute-start(bf16[784,256]{1,0:T(8,128)(2,1)S(1)} %get-tuple-element.20), channel_id=1, source_target_pairs={{2,0},{3,1},{4,2},{5,3},{6,4},{7,5},{8,6},{9,7},{10,8},{11,9},{12,... | collective-permute-start | bytes 1204232 | tf_op jit(solution)/shard_map/ppermute | solution.py:262
  167.6 21.4 %collective-permute-start.6 = (bf16[1552,256]{1,0:T(8,128)(2,1)S(1)}, bf16[1552,256]{1,0:T(8,128)(2,1)S(1)}, u32[]{:S(2)}, u32[]{:S(2)}) collective-permute-start(bf16[1552,256]{1,0:T(8,128)(2,1)S(1)} %get-tuple-element.27), channel_id=1, source_target_pairs={{30,0},{31,1},{0,2},{1,3},{2,4},{3,5},{4,6},{5,7},{6,8},{7,9},{8,1... | collective-permute-start | bytes 2383880 | tf_op jit(solution)/shard_map/ppermute | solution.py:262
  169.5 20.4 %collective-permute-start.7 = (bf16[1552,256]{1,0:T(8,128)(2,1)S(1)}, bf16[1552,256]{1,0:T(8,128)(2,1)S(1)}, u32[]{:S(2)}, u32[]{:S(2)}) collective-permute-start(bf16[1552,256]{1,0:T(8,128)(2,1)S(1)} %get-tuple-element.28), channel_id=1, source_target_pairs={{2,0},{3,1},{4,2},{5,3},{6,4},{7,5},{8,6},{9,7},{10,8},{11,9},{12,... | collective-permute-start | bytes 2383880 | tf_op jit(solution)/shard_map/ppermute | solution.py:262
  190.2 18.9 %collective-permute-start.8 = (bf16[784,256]{1,0:T(8,128)(2,1)S(1)}, bf16[784,256]{1,0:T(8,128)(2,1)S(1)}, u32[]{:S(2)}, u32[]{:S(2)}) collective-permute-start(bf16[784,256]{1,0:T(8,128)(2,1)S(1)} %pad_maximum_fusion.3), channel_id=1, source_target_pairs={{0,1},{1,0},{2,3},{3,2},{4,5},{5,4},{6,7},{7,6},{8,9},{9,8},{10,11... | collective-permute-start | bytes 1204232 | tf_op jit(solution)/shard_map/ppermute | solution.py:296
  228.1 28.5 %all-to-all-start.3 = ((f32[16,16,256]{2,1,0:T(8,128)}), f32[16,16,256]{2,1,0:T(8,128)S(1)}, u32[]{:S(2)}, u32[]{:S(2)}) async-start(f32[16,16,256]{2,1,0:T(8,128)} %broadcast_in_dim.11), calls=%async_computation.3 | async-start | bytes 524288 | tf_op jit(solution)/shard_map/all_to_all | solution.py:321

commit v2 on v1

v2 whole, which is shorter than its diff:
```python
import functools

import jax
import jax.numpy as jnp
from jax import lax
from jax.experimental import pallas as pl
from jax.experimental.pallas import tpu as pltpu
from jax.sharding import PartitionSpec as P

BF16 = jnp.bfloat16
F32 = jnp.float32
NZ, NY = 16, 2
N_SRC = 16
SIDE = 128
WIDTH = 256
ROWS = 192
PAIR = NY * ROWS
GROUP = 16
VMEM_LIMIT = 40 * 1024 * 1024

STRIDE_GROUPS = [[2 * z + y for z in range(q, NZ, 4)] for q in range(4) for y in range(NY)]
Y_GROUPS = [[2 * z, 2 * z + 1] for z in range(NZ)]
CHIPS = N_SRC // 2
CORE_GROUPS = [[2 * chip + core for chip in range(CHIPS)] for core in range(2)]
CORE_SWAP = [(s, s ^ 1) for s in range(N_SRC)]


def from_z(step):
    return [(((z + step) % NZ) * NY + y, z * NY + y) for z in range(NZ) for y in range(NY)]


def live_slots(slot_count, values_ref, held, sems, one_slot):
    slots = values_ref.shape[0]
    groups = slots // GROUP

    def copy(g):
        span = pl.ds(g * GROUP, GROUP)
        return pltpu.make_async_copy(values_ref.at[span], held.at[span], sems.at[g])

    def start():
        for g in range(groups):

            @pl.when(g * GROUP < slot_count)
            def _():
                copy(g).start()

    def run():
        for g in range(groups):

            @pl.when(g * GROUP < slot_count)
            def _():
                copy(g).wait()
                live = jnp.minimum(slot_count - g * GROUP, GROUP)

                def four(i, carry):
                    one_slot([g * GROUP + 4 * i + u for u in range(4)])
                    return carry

                def single(i, carry):
                    one_slot([g * GROUP + i])
                    return carry

                lax.fori_loop(0, live // 4, four, 0)
                lax.fori_loop((live // 4) * 4, live, single, 0)

    return start, run


def block_of(ref, index):
    return ref[pl.ds(pl.multiple_of(index * SIDE, SIDE), SIDE), :]


def add_block(ref, index, term):
    span = pl.ds(pl.multiple_of(index * SIDE, SIDE), SIDE)
    ref[span, :] = ref[span, :] + term


def forward_kernel(
    meta, coords, values_ref, g0, g1, g2a, g2b, g3, own, other, held, rows, total, value_sems, row_sems
):
    slot_count, z, core = meta[0], meta[1], meta[3]
    slots = values_ref.shape[0]

    def one_slot(ks):
        terms = [
            lax.dot_general(
                held[k], block_of(rows, coords[k]), (((0,), (0,)), ((), ())), preferred_element_type=F32
            )
            for k in ks
        ]
        for k, term in zip(ks, terms):
            add_block(total, coords[slots + k], term)

    start, run = live_slots(slot_count, values_ref, held, value_sems, one_slot)
    copies = []
    for offset, ref, first in ((0, g0, 0), (1, g1, 0), (3, g3, 0), (2, g2a, 0), (2, g2b, 2)):
        residue = lax.rem(z + offset, 4)
        for i in range(ref.shape[0]):
            place = (residue + 4 * (first + i)) * PAIR
            copies.append(
                pltpu.make_async_copy(
                    ref.at[i],
                    rows.at[pl.ds(pl.multiple_of(place, PAIR), PAIR)],
                    row_sems.at[len(copies)],
                )
            )
    for copy in copies:
        copy.start()
    start()
    total[...] = jnp.zeros_like(total)
    for copy in copies:
        copy.wait()
    run()
    for chip in range(CHIPS):
        for ref, target in ((own, core), (other, 1 - core)):
            place = pl.multiple_of((2 * chip + target) * ROWS, ROWS)
            ref[chip * ROWS : (chip + 1) * ROWS, :] = total[pl.ds(place, ROWS), :].astype(BF16)


def forward_sums(meta, coords, values, parts, dest_rows):
    slots = values.shape[0]
    source_rows = NZ * PAIR
    smem = pl.BlockSpec(memory_space=pltpu.SMEM)
    anywhere = pl.BlockSpec(memory_space=pl.ANY)
    vmem = pl.BlockSpec(memory_space=pltpu.VMEM)
    half = jax.ShapeDtypeStruct((dest_rows // 2, WIDTH), BF16)
    return pl.pallas_call(
        forward_kernel,
        out_shape=(half, half),
        in_specs=[smem, smem, pl.BlockSpec(memory_space=pltpu.HBM)] + [anywhere] * 5,
        out_specs=(vmem, vmem),
        scratch_shapes=[
            pltpu.VMEM(values.shape, BF16),
            pltpu.VMEM((source_rows, WIDTH), BF16),
            pltpu.VMEM((dest_rows, WIDTH), F32),
            pltpu.SemaphoreType.DMA((slots // GROUP,)),
            pltpu.SemaphoreType.DMA((NZ,)),
        ],
        compiler_params=pltpu.CompilerParams(vmem_limit_bytes=VMEM_LIMIT),
        name="forward_sums",
    )(meta, coords, values, *parts)


def middle_kernel(terms, weight, cotangent, act_ref, message):
    agg = jnp.sum(terms[...].astype(F32), axis=0).astype(BF16)
    w = weight[...]
    preact = jnp.dot(agg, w, preferred_element_type=F32)
    sigma = jax.nn.sigmoid(preact)
    act_ref[...] = (preact * sigma).astype(BF16)
    slope = sigma * (1.0 + preact * (1.0 - sigma))
    delta = (cotangent[...].astype(F32) * slope).astype(BF16)
    grad_agg = lax.dot_general(
        delta, w, (((1,), (1,)), ((), ())), preferred_element_type=F32
    ).astype(BF16)
    local = lax.dot_general(agg, delta, (((0,), (0,)), ((), ())), preferred_element_type=F32)
    share = WIDTH // N_SRC
    for chip in range(CHIPS):
        message[chip, :ROWS, :] = grad_agg
        message[chip, ROWS:, :] = local[2 * chip * share : 2 * (chip + 1) * share, :].astype(BF16)


def middle(terms, weight, cotangent):
    share = WIDTH // N_SRC
    vmem = pl.BlockSpec(memory_space=pltpu.VMEM)
    return pl.pallas_call(
        middle_kernel,
        out_shape=(
            jax.ShapeDtypeStruct((ROWS, WIDTH), BF16),
            jax.ShapeDtypeStruct((CHIPS, ROWS + 2 * share, WIDTH), BF16),
        ),
        in_specs=[vmem] * 3,
        out_specs=(vmem, vmem),
        compiler_params=pltpu.CompilerParams(vmem_limit_bytes=VMEM_LIMIT),
        name="middle",
    )(terms, weight, cotangent)


def backward_kernel(
    meta, coords, values_ref, mine, theirs, p0, p1, p3, p2a, p2b, wsum,
    held, rows, total, tail, value_sems, row_sems, tail_sems,
):
    slot_count, z, y, core = meta[0], meta[1], meta[2], meta[3]
    slots = values_ref.shape[0]

    def one_slot(ks):
        terms = [
            jnp.dot(held[k], block_of(rows, coords[slots + k]), preferred_element_type=F32)
            for k in ks
        ]
        for k, term in zip(ks, terms):
            add_block(total, coords[k], term)

    start, run = live_slots(slot_count, values_ref, held, value_sems, one_slot)
    share = (mine.shape[1] - ROWS) // 2
    copies = []
    for which, (ref, owner) in enumerate(((mine, core), (theirs, 1 - core))):
        for chip in range(CHIPS):
            place = pl.multiple_of((2 * chip + owner) * ROWS, ROWS)
            copies.append(
                pltpu.make_async_copy(
                    ref.at[chip, pl.ds(0, ROWS)], rows.at[pl.ds(place, ROWS)], row_sems.at[len(copies)]
                )
            )
        span = pl.ds(pl.multiple_of(ROWS + core * share, share), share)
        copies.append(pltpu.make_async_copy(ref.at[:, span], tail.at[which], tail_sems.at[which]))
    for copy in copies:
        copy.start()
    start()
    total[...] = jnp.zeros_like(total)
    for copy in copies:
        copy.wait()
    run()
    summed = jnp.sum(tail[...].astype(F32), axis=(0, 1))
    wsum[...] = summed
    for ref in (p1, p3, p2b):
        ref[ref.shape[0] - share :, :] = summed.astype(BF16)

    def put(ref, first_row, offset, member, other):
        place = (lax.rem(z + offset, 4) + 4 * member) * PAIR + (y if other == 0 else 1 - y) * ROWS
        chunk = total[pl.ds(pl.multiple_of(place, ROWS), ROWS), :]
        ref[first_row : first_row + ROWS, :] = chunk.astype(BF16)

    for other in range(2):
        for member in range(4):
            for ref, offset in ((p0, 0), (p1, 1), (p3, 3)):
                put(ref, (other * 4 + member) * ROWS, offset, member, other)
        for i in range(2):
            put(p2a, (other * 2 + i) * ROWS, 2, i, other)
            put(p2b, (other * 2 + i) * ROWS, 2, 2 + i, other)


def backward_sums(meta, coords, values, mine, theirs):
    slots = values.shape[0]
    share = (mine.shape[1] - ROWS) // 2
    dest_rows = N_SRC * ROWS
    source_rows = NZ * PAIR
    smem = pl.BlockSpec(memory_space=pltpu.SMEM)
    anywhere = pl.BlockSpec(memory_space=pl.ANY)
    vmem = pl.BlockSpec(memory_space=pltpu.VMEM)

    def rows_of(count):
        return jax.ShapeDtypeStruct((count, WIDTH), BF16)

    return pl.pallas_call(
        backward_kernel,
        out_shape=(
            rows_of(8 * ROWS),
            rows_of(8 * ROWS + share),
            rows_of(8 * ROWS + share),
            rows_of(4 * ROWS),
            rows_of(4 * ROWS + share),
            jax.ShapeDtypeStruct((share, WIDTH), F32),
        ),
        in_specs=[smem, smem, pl.BlockSpec(memory_space=pltpu.HBM), anywhere, anywhere],
        out_specs=(vmem,) * 6,
        scratch_shapes=[
            pltpu.VMEM(values.shape, BF16),
            pltpu.VMEM((dest_rows, WIDTH), BF16),
            pltpu.VMEM((source_rows, WIDTH), F32),
            pltpu.VMEM((2, CHIPS, share, WIDTH), BF16),
            pltpu.SemaphoreType.DMA((slots // GROUP,)),
            pltpu.SemaphoreType.DMA((N_SRC + 1,)),
            pltpu.SemaphoreType.DMA((2,)),
        ],
        compiler_params=pltpu.CompilerParams(vmem_limit_bytes=VMEM_LIMIT),
        name="backward_sums",
    )(meta, coords, values, mine, theirs)


def shift(array, step):
    return lax.ppermute(array, "dst", from_z(step))


def pair_swap(array, axis, groups, side):
    both = lax.all_gather(array, axis, axis=0, axis_index_groups=groups)
    return lax.dynamic_index_in_dim(both, 1 - side, 0, keepdims=False)


def gather_sources(features):
    own = lax.all_gather(features, "dst", axis=0, axis_index_groups=STRIDE_GROUPS)
    own = lax.all_gather(own, "dst", axis=1, tiled=True, axis_index_groups=Y_GROUPS)
    return own, shift(own, 1), shift(own[:2], 2), shift(own[2:], -2), shift(own, -1)


def scatter_sources(p0, p1, p3, p2a, p2b, wsum, y):
    half = 4 * ROWS
    quarter = half // 2
    below, above = shift(p1, -1), shift(p3, 1)
    low, high = shift(p2a, -2), shift(p2b, 2)
    w2 = wsum + below[2 * half :].astype(F32) + above[2 * half :].astype(F32) + high[half:].astype(F32)

    def side(first):
        far = jnp.concatenate([low[first // 2 : first // 2 + quarter], high[first // 2 : first // 2 + quarter]], 0)
        span = slice(first, first + half)
        near = below[span].astype(F32) + above[span].astype(F32)
        return p0[span].astype(F32) + near + far.astype(F32)

    sent = jnp.concatenate([side(half).astype(BF16), w2.astype(BF16)], 0)
    got = pair_swap(sent, "dst", Y_GROUPS, y).astype(F32)
    w3 = (w2 + got[half:]).astype(BF16)
    kept = (side(0) + got[:half]).astype(BF16).reshape(4, ROWS, WIDTH)
    message = jnp.concatenate([kept, jnp.broadcast_to(w3, (4,) + w3.shape)], 1)
    last = lax.all_to_all(message, "dst", 0, 0, tiled=True, axis_index_groups=STRIDE_GROUPS)
    last = jnp.sum(last.astype(F32), axis=0)
    return last[:ROWS].astype(BF16), last[ROWS:].astype(BF16)


def shards(features, weight, values, coords, counts, cotangent):
    tile_values = values[0, 0]
    pairs = coords[0, 0].T.reshape(-1)
    place = lax.axis_index("dst")
    z, y, core = place // NY, lax.rem(place, NY), lax.rem(lax.axis_index("src"), 2)
    meta = jnp.stack([counts[0, 0], z, y, core]).astype(jnp.int32)
    dest_rows = cotangent.shape[1] * N_SRC

    parts = gather_sources(features)
    own, other = forward_sums(meta, pairs, tile_values, parts, dest_rows)
    swapped = lax.ppermute(other, "src", CORE_SWAP)
    chip_sums = (own.astype(F32) + swapped.astype(F32)).astype(BF16)
    terms = lax.all_to_all(
        chip_sums.reshape(CHIPS, ROWS, WIDTH), "src", 0, 0, tiled=True, axis_index_groups=CORE_GROUPS
    )
    activations, message = middle(terms, weight, cotangent[0])
    mine = lax.all_to_all(message, "src", 0, 0, tiled=True, axis_index_groups=CORE_GROUPS)
    theirs = lax.ppermute(mine, "src", CORE_SWAP)
    sums = backward_sums(meta, pairs, tile_values, mine, theirs)
    input_grad, weight_part = scatter_sources(*sums, y)
    share = weight_part.shape[0]
    weight_part = jnp.broadcast_to(weight_part, (N_SRC, share, WIDTH))
    weight_grad = lax.all_to_all(weight_part, "src", 0, 0, tiled=True).reshape(WIDTH, WIDTH)
    return (activations[None], input_grad, weight_grad.astype(F32))


def solution(mesh):
    in_specs = (
        P(("src", "dst"), None),
        P(),
        P("src", "dst", None, None, None),
        P("src", "dst", None, None),
        P("src", "dst"),
        P("dst", "src", None),
    )
    out_specs = (P("dst", "src", None), P(("src", "dst"), None), P())
    return jax.shard_map(shards, mesh=mesh, in_specs=in_specs, out_specs=out_specs, check_vma=False)
```

time: 258 us -> 261 us (1.012)
  blocking collectives: 127 us -> 112 us
  starting transfers between devices: 55.9 us -> 65.2 us
  Pallas kernels: 11 us -> 17.6 us
  other arithmetic: 1 us -> 5.33 us
    all_to_all x2, blocking collectives: 74.1 us -> 37.9 us  [the longest x1 21.3 us: shards(): lax.all_to_all(chip_sums.reshape(CHIPS, ROWS, WIDTH), 'src', 0, 0, tiled=...]
    all_gather x0 -> x1, blocking collectives: none -> 11.3 us  [pair_swap(): both = lax.all_gather(array, axis, axis=0, axis_index_groups=groups)]
    all_to_all x1, blocking collectives: 18 us -> 27.3 us  [scatter_sources(): lax.all_to_all(message, 'dst', 0, 0, tiled=True, axis_index_groups=STRIDE...]
    ppermute x1 -> x2, starting transfers between devices: 9.36 us -> 18.2 us  [the longest x1 13.7 us: shards(): swapped = lax.ppermute(other, 'src', CORE_SWAP)]
    ppermute x8, starting transfers between devices: 26.7 us -> 34.3 us  [shift(): return lax.ppermute(array, 'dst', from_z(step))]
    all_to_all x1, starting transfers between devices: 19.8 us -> 12.7 us  [shards(): lax.all_to_all(weight_part, 'src', 0, 0, tiled=True).reshape(WIDTH, WIDTH)]
    pallas_call x2, Pallas kernels: 9.94 us -> 16.7 us  [the longest x1 8.76 us: forward_sums(): pl.pallas_call(forward_kernel, out_shape=(half, half), in_specs=[smem, sm...]
    ppermute x8, waiting for transfers between devices: 36.9 us -> 43.5 us  [shift(): return lax.ppermute(array, 'dst', from_z(step))]
  transfers between devices with their start and end apart: 10 -> 11, of which waited for: 9 -> 7; matrix products, arithmetic and copies ran while one was open for 1% -> 1% of each run, Pallas kernels for 0% -> 0%
where the time goes in v2:
time: 261 us
  blocking collectives  112 us (43%)
  starting transfers between devices  65.2 us (25%)
  waiting for transfers between devices  54.4 us (21%)
  Pallas kernels  17.6 us (7%)
  other arithmetic  5.33 us (2%)
  local copies, waits for them, and re-layouts  4.75 us (2%)
    ppermute x8, waiting for transfers between devices, shift(): return lax.ppermute(array, 'dst', from_z(step))  43.5 us
    ppermute x8, starting transfers between devices, shift(): return lax.ppermute(array, 'dst', from_z(step))  34.3 us
    all_gather x1, blocking collectives, gather_sources(): lax.all_gather(features, 'dst', axis=0, axis_index_groups=STRIDE_GROUPS)  28 us
    all_to_all x1, blocking collectives, scatter_sources(): lax.all_to_all(message, 'dst', 0, 0, tiled=True, axis_index_groups=STRIDE...  27.3 us
    all_to_all x1, blocking collectives, shards(): lax.all_to_all(chip_sums.reshape(CHIPS, ROWS, WIDTH), 'src', 0, 0, tiled=...  21.3 us
    all_to_all x1, blocking collectives, shards(): lax.all_to_all(message, 'src', 0, 0, tiled=True, axis_index_groups=CORE_G...  16.6 us
    ppermute x1, starting transfers between devices, shards(): swapped = lax.ppermute(other, 'src', CORE_SWAP)  13.7 us
    all_to_all x1, starting transfers between devices, shards(): lax.all_to_all(weight_part, 'src', 0, 0, tiled=True).reshape(WIDTH, WIDTH)  12.7 us
  transfers between devices with their start and end apart: 11, of which 7 were waited for; matrix products, arithmetic and copies ran while one was open for 1% of the time, Pallas kernels for 0%

profile of v2, /device:TPU:1, one launch (start us, length us, event | category | flops | bytes accessed | tf_op | source)
XLA Modules:
  0.0 260.6 jit_solution(9684793069625226711)
XLA Ops:
  0.6 28.0 %all-gather = bf16[768,256]{1,0:T(8,128)(2,1)S(1)} all-gather(bf16[192,256]{1,0:T(8,128)(2,1)} %param.6), channel_id=2, replica_groups={{0,8,16,24},{1,9,17,25},{2,10,18,26},{3,11,19,27},{4,12,20,28},{5,13,21..., dimensions={0}, use_global_device_ids=true | all-gather | bytes 491520 | tf_op jit(solution)/shard_map/all_gather | solution.py:280
  28.7 7.3 %all_gather.17.g0 = bf16[4,384,256]{2,1,0:T(8,128)(2,1)S(1)} all-gather(bf16[4,192,256]{2,1,0:T(8,128)(2,1)S(1)} %bitcast.37), channel_id=1, replica_groups={{0,1},{2,3},{4,5},{6,7},{8,9},{10,11},{12,13},{14,15},{16,17},{18,19},{..., dimensions={1}, use_global_device_ids=true | all-gather | bytes 1179648 | tf_op jit(solution)/shard_map/all_gather | solution.py:281
  35.9 1.9 collective-permute-start.3
  37.9 4.5 %collective-permute-start = (bf16[4,384,256]{2,1,0:T(8,128)(2,1)S(1)}, bf16[4,384,256]{2,1,0:T(8,128)(2,1)S(1)}, u32[]{:S(2)}, u32[]{:S(2)}) collective-permute-start(bf16[4,384,256]{2,1,0:T(8,128)(2,1)S(1)} %all_gather.17.g0), channel_id=1, source_target_pairs={{2,0},{3,1},{4,2},{5,3},{6,4},{7,5},{8,6},{9,7},{10,8},{11,9},{12,... | collective-permute-start | bytes 2359304 | tf_op jit(solution)/shard_map/ppermute | solution.py:271
  45.3 5.5 %collective-permute-start.1 = (bf16[2,384,256]{2,1,0:T(8,128)(2,1)}, bf16[2,384,256]{2,1,0:T(8,128)(2,1)}, u32[]{:S(2)}, u32[]{:S(2)}) collective-permute-start(bf16[2,384,256]{2,1,0:T(8,128)(2,1)} %get-tuple-element.24), channel_id=1, source_target_pairs={{4,0},{5,1},{6,2},{7,3},{8,4},{9,5},{10,6},{11,7},{12,8},{13,9},{1... | collective-permute-start | bytes 1179656 | tf_op jit(solution)/shard_map/ppermute | solution.py:271
  51.6 13.4 %collective-permute-done.2.g2b = bf16[2,384,256]{2,1,0:T(8,128)(2,1)S(1)} collective-permute-done((bf16[2,384,256]{2,1,0:T(8,128)(2,1)}, bf16[2,384,256]{2,1,0:T(8,128)(2,1)S(1)}, u32[]{:S(2)}, u32[]{:S(2)}) %collective-permute-start.2) | collective-permute-done | bytes 393248 | tf_op jit(solution)/shard_map/ppermute | solution.py:271
  66.4 2.3 copy-done
  68.7 8.8 %forward_sums.1 = (bf16[1536,256]{1,0:T(8,128)(2,1)S(1)}, bf16[1536,256]{1,0:T(8,128)(2,1)S(1)}) custom-call(s32[4]{0:T(128)S(1)} %pad_add_fusion.meta, s32[288]{0:T(512)S(1)} %reshape.21.coords, bf16[144,128,128]{2,1,0:T(8,128)(2,1)S(1)} %bitcast.30, bf16[4,384,256]{2,1,0:T(8,128)(2,1)S(1)} %all_gather.17.g0, ...), custom_call_target="tpu_custom_call" | custom-call | tf_op jit(solution)/shard_map/forward_sums/pallas_call | solution.py:127
  77.5 13.7 %collective-permute-start.4 = (bf16[1536,256]{1,0:T(8,128)(2,1)S(1)}, bf16[1536,256]{1,0:T(8,128)(2,1)S(1)}, u32[]{:S(2)}, u32[]{:S(2)}) collective-permute-start(bf16[1536,256]{1,0:T(8,128)(2,1)S(1)} %get-tuple-element.14), channel_id=1, source_target_pairs={{0,32},{32,0},{64,96},{96,64},{128,160},{160,128},{192,224},{224,1... | collective-permute-start | bytes 2359304 | tf_op jit(solution)/shard_map/ppermute | solution.py:318
  93.3 21.3 %all_to_all.20.terms = bf16[8,192,256]{2,1,0:T(8,128)(2,1)S(1)} all-to-all(bf16[8,192,256]{2,1,0:T(8,128)(2,1)S(1)} %bitcast.35), channel_id=1, replica_groups={{0,64,128,192,256,320,384,448},{32,96,160,224,288,352,416,480},{1,65,12..., dimensions={0} | all-to-all | bytes 1572864 | tf_op jit(solution)/shard_map/all_to_all | solution.py:320
  115.5 16.6 %all_to_all.21.mine = bf16[8,224,256]{2,1,0:T(8,128)(2,1)S(1)} all-to-all(bf16[8,224,256]{2,1,0:T(8,128)(2,1)S(1)} %get-tuple-element.16), channel_id=1, replica_groups={{0,64,128,192,256,320,384,448},{32,96,160,224,288,352,416,480},{1,65,12..., dimensions={0} | all-to-all | bytes 1835008 | tf_op jit(solution)/shard_map/all_to_all | solution.py:324
  132.1 4.4 %collective-permute-start.5 = (bf16[8,224,256]{2,1,0:T(8,128)(2,1)S(1)}, bf16[8,224,256]{2,1,0:T(8,128)(2,1)S(1)}, u32[]{:S(2)}, u32[]{:S(2)}) collective-permute-start(bf16[8,224,256]{2,1,0:T(8,128)(2,1)S(1)} %all_to_all.21.mine), channel_id=1, source_target_pairs={{0,32},{32,0},{64,96},{96,64},{128,160},{160,128},{192,224},{224,1... | collective-permute-start | bytes 2752520 | tf_op jit(solution)/shard_map/ppermute | solution.py:325
  136.6 2.1 collective-permute-done.5.theirs
  138.6 8.0 %backward_sums.1 = (bf16[1536,256]{1,0:T(8,128)(2,1)S(1)}, bf16[1552,256]{1,0:T(8,128)(2,1)S(1)}, bf16[1552,256]{1,0:T(8,128)(2,1)S(1)}, bf16[768,256]{1,0:T(8,1...) custom-call(s32[4]{0:T(128)S(1)} %pad_add_fusion.meta, s32[288]{0:T(512)S(1)} %reshape.21.coords, ...), custom_call_target="tpu_custom_call" | custom-call | tf_op jit(solution)/shard_map/backward_sums/pallas_call | solution.py:244
  146.6 8.7 %collective-permute-start.8 = (bf16[768,256]{1,0:T(8,128)(2,1)}, bf16[768,256]{1,0:T(8,128)(2,1)S(1)}, u32[]{:S(2)}, u32[]{:S(2)}) collective-permute-start(bf16[768,256]{1,0:T(8,128)(2,1)} %get-tuple-element.20), channel_id=1, source_target_pairs={{28,0},{29,1},{30,2},{31,3},{0,4},{1,5},{2,6},{3,7},{4,8},{5,9},{6... | collective-permute-start | bytes 1179656 | tf_op jit(solution)/shard_map/ppermute | solution.py:271
  155.3 1.9 collective-permute-start.6
  157.2 4.6 %collective-permute-start.7 = (bf16[1552,256]{1,0:T(8,128)(2,1)S(1)}, bf16[1552,256]{1,0:T(8,128)(2,1)}, u32[]{:S(2)}, u32[]{:S(2)}) collective-permute-start(bf16[1552,256]{1,0:T(8,128)(2,1)S(1)} %get-tuple-element.19), channel_id=1, source_target_pairs={{2,0},{3,1},{4,2},{5,3},{6,4},{7,5},{8,6},{9,7},{10,8},{11,9},{12,... | collective-permute-start | bytes 2383880 | tf_op jit(solution)/shard_map/ppermute | solution.py:271
  161.8 5.2 %collective-permute-start.9 = (bf16[784,256]{1,0:T(8,128)(2,1)}, bf16[784,256]{1,0:T(8,128)(2,1)S(1)}, u32[]{:S(2)}, u32[]{:S(2)}) collective-permute-start(bf16[784,256]{1,0:T(8,128)(2,1)} %get-tuple-element.21), channel_id=1, source_target_pairs={{4,0},{5,1},{6,2},{7,3},{8,4},{9,5},{10,6},{11,7},{12,8},{13,9},{1... | collective-permute-start | bytes 1204232 | tf_op jit(solution)/shard_map/ppermute | solution.py:271
  167.0 7.6 %collective-permute-done.8 = bf16[768,256]{1,0:T(8,128)(2,1)S(1)} collective-permute-done((bf16[768,256]{1,0:T(8,128)(2,1)}, bf16[768,256]{1,0:T(8,128)(2,1)S(1)}, u32[]{:S(2)}, u32[]{:S(2)}) %collective-permute-start.8) | collective-permute-done | bytes 393248 | tf_op jit(solution)/shard_map/ppermute | solution.py:271
  174.7 21.1 %collective-permute-done.9 = bf16[784,256]{1,0:T(8,128)(2,1)S(1)} collective-permute-done((bf16[784,256]{1,0:T(8,128)(2,1)}, bf16[784,256]{1,0:T(8,128)(2,1)S(1)}, u32[]{:S(2)}, u32[]{:S(2)}) %collective-permute-start.9) | collective-permute-done | bytes 401440 | tf_op jit(solution)/shard_map/ppermute | solution.py:271
  197.9 11.3 %all-gather.1 = bf16[1568,256]{1,0:T(8,128)(2,1)S(1)} all-gather(bf16[784,256]{1,0:T(8,128)(2,1)S(1)} %pad_maximum_fusion.1), channel_id=3, replica_groups={{0,1},{2,3},{4,5},{6,7},{8,9},{10,11},{12,13},{14,15},{16,17},{18,19},{..., dimensions={0}, use_global_device_ids=true | all-gather | bytes 1204224 | tf_op jit(solution)/shard_map/all_gather | solution.py:275
  211.5 27.3 %all_to_all.22 = bf16[4,208,256]{2,1,0:T(8,128)(2,1)S(1)} all-to-all(bf16[4,208,256]{2,1,0:T(8,128)(2,1)S(1)} %pad_maximum_fusion), channel_id=1, replica_groups={{0,8,16,24},{1,9,17,25},{2,10,18,26},{3,11,19,27},{4,12,20,28},{5,13,21..., dimensions={0} | all-to-all | bytes 851968 | tf_op jit(solution)/shard_map/all_to_all | solution.py:303
  239.6 12.7 %all-to-all-start.3 = ((bf16[16,16,256]{2,1,0:T(8,128)(2,1)}), bf16[16,16,256]{2,1,0:T(8,128)(2,1)S(1)}, u32[]{:S(2)}, u32[]{:S(2)}) async-start(bf16[16,16,256]{2,1,0:T(8,128)(2,1)} %broadcast_in_dim.11), calls=%async_computation.3 | async-start | bytes 262144 | tf_op jit(solution)/shard_map/all_to_all | solution.py:330
  252.9 6.9 %all-to-all-done.3 = bf16[16,16,256]{2,1,0:T(8,128)(2,1)S(1)} async-done(((bf16[16,16,256]{2,1,0:T(8,128)(2,1)}), bf16[16,16,256]{2,1,0:T(8,128)(2,1)S(1)}, u32[]{:S(2)}, u32[]{:S(2)}) %all-to-all-start.3) | async-done | bytes 131104 | tf_op jit(solution)/shard_map/all_to_all | solution.py:330
  (39 shorter events, 13.8 us)
Async XLA Ops:
  0.6 50.8 %copy-start.3 = (s32[1,1,144,2]{2,3,1,0:T(2,128)S(1)}, s32[1,1,144,2]{2,3,1,0:T(2,128)}, u32[]{:S(2)}) copy-start(s32[1,1,144,2]{2,3,1,0:T(2,128)} %param.9) | copy-start | bytes 3460
  35.9 30.4 %collective-permute-start.3 = (bf16[4,384,256]{2,1,0:T(8,128)(2,1)S(1)}, bf16[4,384,256]{2,1,0:T(8,128)(2,1)S(1)}, u32[]{:S(2)}, u32[]{:S(2)}) collective-permute-start(bf16[4,384,256]{2,1,0:T(8,128)(2,1)S(1)} %all_gather.17.g0), channel_id=1, source_target_pairs={{30,0},{31,1},{0,2},{1,3},{2,4},{3,5},{4,6},{5,7},{6,8},{7,9},{8,1... | collective-permute-start | bytes 2359304 | tf_op jit(solution)/shard_map/ppermute | solution.py:271
  37.9 28.5 %collective-permute-start = (bf16[4,384,256]{2,1,0:T(8,128)(2,1)S(1)}, bf16[4,384,256]{2,1,0:T(8,128)(2,1)S(1)}, u32[]{:S(2)}, u32[]{:S(2)}) collective-permute-start(bf16[4,384,256]{2,1,0:T(8,128)(2,1)S(1)} %all_gather.17.g0), channel_id=1, source_target_pairs={{2,0},{3,1},{4,2},{5,3},{6,4},{7,5},{8,6},{9,7},{10,8},{11,9},{12,... | collective-permute-start | bytes 2359304 | tf_op jit(solution)/shard_map/ppermute | solution.py:271
  42.4 96.2 %slice-start = ((s8[4718592]{0:T(1024)(128)(4,1)}), s8[524288]{0:T(1024)(128)(4,1)S(1)}, s32[]{:S(2)}) async-start(s8[4718592]{0:T(1024)(128)(4,1)} %bitcast.31), calls=%async_computation.4 | async-start | bytes 1048576
  43.4 21.6 %collective-permute-start.2 = (bf16[2,384,256]{2,1,0:T(8,128)(2,1)}, bf16[2,384,256]{2,1,0:T(8,128)(2,1)S(1)}, u32[]{:S(2)}, u32[]{:S(2)}) collective-permute-start(bf16[2,384,256]{2,1,0:T(8,128)(2,1)} %get-tuple-element.23), channel_id=1, source_target_pairs={{28,0},{29,1},{30,2},{31,3},{0,4},{1,5},{2,6},{3,7},{4,8},{5,9},{6... | collective-permute-start | bytes 1179656 | tf_op jit(solution)/shard_map/ppermute | solution.py:271
  45.3 21.0 %collective-permute-start.1 = (bf16[2,384,256]{2,1,0:T(8,128)(2,1)}, bf16[2,384,256]{2,1,0:T(8,128)(2,1)}, u32[]{:S(2)}, u32[]{:S(2)}) collective-permute-start(bf16[2,384,256]{2,1,0:T(8,128)(2,1)} %get-tuple-element.24), channel_id=1, source_target_pairs={{4,0},{5,1},{6,2},{7,3},{8,4},{9,5},{10,6},{11,7},{12,8},{13,9},{1... | collective-permute-start | bytes 1179656 | tf_op jit(solution)/shard_map/ppermute | solution.py:271
  66.4 2.3 copy-start
  68.7 69.9 %slice-start.1 = ((s8[4718592]{0:T(1024)(128)(4,1)}), s8[4194304]{0:T(1024)(128)(4,1)S(1)}, s32[]{:S(2)}) async-start(s8[4718592]{0:T(1024)(128)(4,1)} %bitcast.31), calls=%async_computation.5 | async-start | bytes 8388608
  77.5 15.6 %collective-permute-start.4 = (bf16[1536,256]{1,0:T(8,128)(2,1)S(1)}, bf16[1536,256]{1,0:T(8,128)(2,1)S(1)}, u32[]{:S(2)}, u32[]{:S(2)}) collective-permute-start(bf16[1536,256]{1,0:T(8,128)(2,1)S(1)} %get-tuple-element.14), channel_id=1, source_target_pairs={{0,32},{32,0},{64,96},{96,64},{128,160},{160,128},{192,224},{224,1... | collective-permute-start | bytes 2359304 | tf_op jit(solution)/shard_map/ppermute | solution.py:318
  93.1 21.5 %copy-start.1 = (bf16[256,256]{1,0:T(8,128)(2,1)S(1)}, bf16[256,256]{1,0:T(8,128)(2,1)}, u32[]{:S(2)}) copy-start(bf16[256,256]{1,0:T(8,128)(2,1)} %weight.1) | copy-start | bytes 393220
  93.1 21.5 %copy-start.2 = (bf16[1,192,256]{2,1,0:T(8,128)(2,1)S(1)}, bf16[1,192,256]{2,1,0:T(8,128)(2,1)}, u32[]{:S(2)}) copy-start(bf16[1,192,256]{2,1,0:T(8,128)(2,1)} %param.11) | copy-start | bytes 294916
  132.1 6.5 %collective-permute-start.5 = (bf16[8,224,256]{2,1,0:T(8,128)(2,1)S(1)}, bf16[8,224,256]{2,1,0:T(8,128)(2,1)S(1)}, u32[]{:S(2)}, u32[]{:S(2)}) collective-permute-start(bf16[8,224,256]{2,1,0:T(8,128)(2,1)S(1)} %all_to_all.21.mine), channel_id=1, source_target_pairs={{0,32},{32,0},{64,96},{96,64},{128,160},{160,128},{192,224},{224,1... | collective-permute-start | bytes 2752520 | tf_op jit(solution)/shard_map/ppermute | solution.py:325
  146.6 28.0 %collective-permute-start.8 = (bf16[768,256]{1,0:T(8,128)(2,1)}, bf16[768,256]{1,0:T(8,128)(2,1)S(1)}, u32[]{:S(2)}, u32[]{:S(2)}) collective-permute-start(bf16[768,256]{1,0:T(8,128)(2,1)} %get-tuple-element.20), channel_id=1, source_target_pairs={{28,0},{29,1},{30,2},{31,3},{0,4},{1,5},{2,6},{3,7},{4,8},{5,9},{6... | collective-permute-start | bytes 1179656 | tf_op jit(solution)/shard_map/ppermute | solution.py:271
  155.3 40.6 %collective-permute-start.6 = (bf16[1552,256]{1,0:T(8,128)(2,1)S(1)}, bf16[1552,256]{1,0:T(8,128)(2,1)}, u32[]{:S(2)}, u32[]{:S(2)}) collective-permute-start(bf16[1552,256]{1,0:T(8,128)(2,1)S(1)} %get-tuple-element.18), channel_id=1, source_target_pairs={{30,0},{31,1},{0,2},{1,3},{2,4},{3,5},{4,6},{5,7},{6,8},{7,9},{8,1... | collective-permute-start | bytes 2383880 | tf_op jit(solution)/shard_map/ppermute | solution.py:271
  157.2 38.6 %collective-permute-start.7 = (bf16[1552,256]{1,0:T(8,128)(2,1)S(1)}, bf16[1552,256]{1,0:T(8,128)(2,1)}, u32[]{:S(2)}, u32[]{:S(2)}) collective-permute-start(bf16[1552,256]{1,0:T(8,128)(2,1)S(1)} %get-tuple-element.19), channel_id=1, source_target_pairs={{2,0},{3,1},{4,2},{5,3},{6,4},{7,5},{8,6},{9,7},{10,8},{11,9},{12,... | collective-permute-start | bytes 2383880 | tf_op jit(solution)/shard_map/ppermute | solution.py:271
  161.8 34.0 %collective-permute-start.9 = (bf16[784,256]{1,0:T(8,128)(2,1)}, bf16[784,256]{1,0:T(8,128)(2,1)S(1)}, u32[]{:S(2)}, u32[]{:S(2)}) collective-permute-start(bf16[784,256]{1,0:T(8,128)(2,1)} %get-tuple-element.21), channel_id=1, source_target_pairs={{4,0},{5,1},{6,2},{7,3},{8,4},{9,5},{10,6},{11,7},{12,8},{13,9},{1... | collective-permute-start | bytes 1204232 | tf_op jit(solution)/shard_map/ppermute | solution.py:271
  239.6 20.3 %all-to-all-start.3 = ((bf16[16,16,256]{2,1,0:T(8,128)(2,1)}), bf16[16,16,256]{2,1,0:T(8,128)(2,1)S(1)}, u32[]{:S(2)}, u32[]{:S(2)}) async-start(bf16[16,16,256]{2,1,0:T(8,128)(2,1)} %broadcast_in_dim.11), calls=%async_computation.3 | async-start | bytes 262144 | tf_op jit(solution)/shard_map/all_to_all | solution.py:330

commit v3 on v2

v3 whole, which is shorter than its diff:
```python
import functools

import jax
import jax.numpy as jnp
from jax import lax
from jax.experimental import pallas as pl
from jax.experimental.pallas import tpu as pltpu
from jax.sharding import PartitionSpec as P

BF16 = jnp.bfloat16
F32 = jnp.float32
NZ, NY = 16, 2
N_SRC = 16
SIDE = 128
WIDTH = 256
ROWS = 192
PAIR = NY * ROWS
VMEM_LIMIT = 32 * 1024 * 1024

STRIDE_GROUPS = [[2 * z + y for z in range(q, NZ, 4)] for q in range(4) for y in range(NY)]
Y_GROUPS = [[2 * z, 2 * z + 1] for z in range(NZ)]
Y_SWAP = [(d, d ^ 1) for d in range(NZ * NY)]
CHIPS = N_SRC // 2
CORE_GROUPS = [[2 * chip + core for chip in range(CHIPS)] for core in range(2)]
CORE_SWAP = [(s, s ^ 1) for s in range(N_SRC)]


def from_z(step):
    return [(((z + step) % NZ) * NY + y, z * NY + y) for z in range(NZ) for y in range(NY)]


def each_slot(slot_count, one_slot):
    def four(i, carry):
        one_slot([4 * i + u for u in range(4)])
        return carry

    def single(i, carry):
        one_slot([i])
        return carry

    lax.fori_loop(0, slot_count // 4, four, 0)
    lax.fori_loop((slot_count // 4) * 4, slot_count, single, 0)


def block_of(ref, index):
    return ref[pl.ds(pl.multiple_of(index * SIDE, SIDE), SIDE), :]


def add_block(ref, index, term):
    span = pl.ds(pl.multiple_of(index * SIDE, SIDE), SIDE)
    ref[span, :] = ref[span, :] + term


def forward_kernel(meta, coords, blocks, g0, g1, g2a, g2b, g3, own, other, rows, total):
    slot_count, z, core = meta[0], meta[1], meta[3]
    slots = blocks.shape[0]

    def one_slot(ks):
        terms = [
            lax.dot_general(
                blocks[k], block_of(rows, coords[k]), (((0,), (0,)), ((), ())), preferred_element_type=F32
            )
            for k in ks
        ]
        for k, term in zip(ks, terms):
            add_block(total, coords[slots + k], term)

    for offset, ref, first in ((0, g0, 0), (1, g1, 0), (3, g3, 0), (2, g2a, 0), (2, g2b, 2)):
        residue = lax.rem(z + offset, 4)
        for i in range(ref.shape[0]):
            place = pl.multiple_of((residue + 4 * (first + i)) * PAIR, PAIR)
            rows[pl.ds(place, PAIR), :] = ref[i]
    total[...] = jnp.zeros_like(total)
    each_slot(slot_count, one_slot)
    for chip in range(CHIPS):
        for ref, target in ((own, core), (other, 1 - core)):
            place = pl.multiple_of((2 * chip + target) * ROWS, ROWS)
            ref[chip * ROWS : (chip + 1) * ROWS, :] = total[pl.ds(place, ROWS), :].astype(BF16)


def forward_sums(meta, coords, values, parts, dest_rows):
    source_rows = NZ * PAIR
    smem = pl.BlockSpec(memory_space=pltpu.SMEM)
    vmem = pl.BlockSpec(memory_space=pltpu.VMEM)
    half = jax.ShapeDtypeStruct((dest_rows // 2, WIDTH), BF16)
    return pl.pallas_call(
        forward_kernel,
        out_shape=(half, half),
        in_specs=[smem, smem] + [vmem] * 6,
        out_specs=(vmem, vmem),
        scratch_shapes=[pltpu.VMEM((source_rows, WIDTH), BF16), pltpu.VMEM((dest_rows, WIDTH), F32)],
        compiler_params=pltpu.CompilerParams(vmem_limit_bytes=VMEM_LIMIT),
        name="forward_sums",
    )(meta, coords, values, *parts)


def middle_kernel(terms, weight, cotangent, act_ref, message):
    agg = jnp.sum(terms[...].astype(F32), axis=0).astype(BF16)
    w = weight[...]
    preact = jnp.dot(agg, w, preferred_element_type=F32)
    sigma = jax.nn.sigmoid(preact)
    act_ref[...] = (preact * sigma).astype(BF16)
    slope = sigma * (1.0 + preact * (1.0 - sigma))
    delta = (cotangent[...].astype(F32) * slope).astype(BF16)
    grad_agg = lax.dot_general(
        delta, w, (((1,), (1,)), ((), ())), preferred_element_type=F32
    ).astype(BF16)
    local = lax.dot_general(agg, delta, (((0,), (0,)), ((), ())), preferred_element_type=F32)
    share = WIDTH // N_SRC
    for chip in range(CHIPS):
        message[chip, :ROWS, :] = grad_agg
        message[chip, ROWS:, :] = local[2 * chip * share : 2 * (chip + 1) * share, :].astype(BF16)


def middle(terms, weight, cotangent):
    share = WIDTH // N_SRC
    vmem = pl.BlockSpec(memory_space=pltpu.VMEM)
    return pl.pallas_call(
        middle_kernel,
        out_shape=(
            jax.ShapeDtypeStruct((ROWS, WIDTH), BF16),
            jax.ShapeDtypeStruct((CHIPS, ROWS + 2 * share, WIDTH), BF16),
        ),
        in_specs=[vmem] * 3,
        out_specs=(vmem, vmem),
        compiler_params=pltpu.CompilerParams(vmem_limit_bytes=VMEM_LIMIT),
        name="middle",
    )(terms, weight, cotangent)


def backward_kernel(meta, coords, blocks, mine, theirs, *refs):
    kept, sent, (wsum, rows, total) = refs[:4], refs[4:8], refs[8:]
    slot_count, z, y, core = meta[0], meta[1], meta[2], meta[3]
    slots = blocks.shape[0]

    def one_slot(ks):
        terms = [
            jnp.dot(blocks[k], block_of(rows, coords[slots + k]), preferred_element_type=F32)
            for k in ks
        ]
        for k, term in zip(ks, terms):
            add_block(total, coords[k], term)

    share = wsum.shape[0]
    summed = jnp.zeros(wsum.shape, F32)
    for ref, owner in ((mine, core), (theirs, 1 - core)):
        for chip in range(CHIPS):
            place = pl.multiple_of((2 * chip + owner) * ROWS, ROWS)
            rows[pl.ds(place, ROWS), :] = ref[chip, :ROWS, :]
            tail = pl.ds(pl.multiple_of(ROWS + core * share, share), share)
            summed = summed + ref[chip, tail, :].astype(F32)
    wsum[...] = summed.astype(BF16)
    total[...] = jnp.zeros_like(total)
    each_slot(slot_count, one_slot)
    for refs, side in ((sent, 1 - y), (kept, y)):
        for offset, ref in zip((0, 1, 6, 15), refs):
            for member in range(4):
                place = lax.rem(z + offset + 4 * member, NZ) * PAIR + side * ROWS
                chunk = total[pl.ds(pl.multiple_of(place, ROWS), ROWS), :]
                ref[member * ROWS : (member + 1) * ROWS, :] = chunk.astype(BF16)


def backward_sums(meta, coords, values, mine, theirs):
    share = (mine.shape[1] - ROWS) // 2
    dest_rows = N_SRC * ROWS
    source_rows = NZ * PAIR
    smem = pl.BlockSpec(memory_space=pltpu.SMEM)
    vmem = pl.BlockSpec(memory_space=pltpu.VMEM)
    half = jax.ShapeDtypeStruct((4 * ROWS, WIDTH), BF16)
    out = pl.pallas_call(
        backward_kernel,
        out_shape=(half,) * 8 + (jax.ShapeDtypeStruct((share, WIDTH), BF16),),
        in_specs=[smem, smem, vmem, vmem, vmem],
        out_specs=(vmem,) * 9,
        scratch_shapes=[pltpu.VMEM((dest_rows, WIDTH), BF16), pltpu.VMEM((source_rows, WIDTH), F32)],
        compiler_params=pltpu.CompilerParams(vmem_limit_bytes=VMEM_LIMIT),
        name="backward_sums",
    )(meta, coords, values, mine, theirs)
    return out[:4], out[4:8], out[8]


def shift(array, step):
    return lax.ppermute(array, "dst", from_z(step))


def gather_sources(features):
    own = lax.all_gather(features, "dst", axis=0, axis_index_groups=STRIDE_GROUPS)
    own = lax.all_gather(own, "dst", axis=1, tiled=True, axis_index_groups=Y_GROUPS)
    right = shift(own, 1)
    left = shift(own, -1)
    return own, right, shift(right[:2], 1), shift(left[2:], -1), left


def total_of(*terms):
    return sum(term.astype(F32) for term in terms).astype(BF16)


def scatter_sources(kept, sent, weight_part):
    half = 2 * ROWS
    swapped = [None] * 4
    for which in (2, 1, 3, 0):
        swapped[which] = lax.ppermute(sent[which], "dst", Y_SWAP)
    low = shift(total_of(kept[2][:half], swapped[2][:half]), -1)
    high = shift(total_of(kept[2][half:], swapped[2][half:]), 1)
    none = jnp.zeros_like(low[:ROWS])
    up = total_of(kept[1], swapped[1], jnp.concatenate([none, low, none], 0))
    down = total_of(kept[3], swapped[3], jnp.concatenate([high, none, none], 0))
    near = total_of(kept[0], swapped[0], shift(up, -1), shift(down, 1)).reshape(4, ROWS, WIDTH)
    near, weight_part = lax.optimization_barrier((near, weight_part))
    return total_of(near[0], shift(near[2], -8), shift(near[1], -4), shift(near[3], 4)), weight_part


def everywhere(part, axis, count):
    copies = jnp.broadcast_to(part, (count,) + part.shape)
    return lax.all_to_all(copies, axis, 0, 0, tiled=True)


def shards(features, weight, values, coords, counts, cotangent):
    tile_values = values[0, 0]
    pairs = coords[0, 0].T.reshape(-1)
    place = lax.axis_index("dst")
    z, y, core = place // NY, lax.rem(place, NY), lax.rem(lax.axis_index("src"), 2)
    meta = jnp.stack([counts[0, 0], z, y, core]).astype(jnp.int32)
    dest_rows = cotangent.shape[1] * N_SRC

    parts = gather_sources(features)
    own, other = forward_sums(meta, pairs, tile_values, parts, dest_rows)
    swapped = lax.ppermute(other, "src", CORE_SWAP)
    chip_sums = (own.astype(F32) + swapped.astype(F32)).astype(BF16)
    terms = lax.all_to_all(
        chip_sums.reshape(CHIPS, ROWS, WIDTH), "src", 0, 0, tiled=True, axis_index_groups=CORE_GROUPS
    )
    activations, message = middle(terms, weight, cotangent[0])
    mine = lax.all_to_all(message, "src", 0, 0, tiled=True, axis_index_groups=CORE_GROUPS)
    theirs = lax.ppermute(mine, "src", CORE_SWAP)
    kept, sent, weight_part = backward_sums(meta, pairs, tile_values, mine, theirs)
    input_grad, weight_part = scatter_sources(kept, sent, weight_part)
    weight_part = everywhere(weight_part, "dst", NZ * NY)
    weight_part = jnp.sum(weight_part.astype(F32), axis=0).astype(BF16)
    weight_grad = everywhere(weight_part, "src", N_SRC).reshape(WIDTH, WIDTH)
    return (activations[None], input_grad, weight_grad.astype(F32))


def solution(mesh):
    in_specs = (
        P(("src", "dst"), None),
        P(),
        P("src", "dst", None, None, None),
        P("src", "dst", None, None),
        P("src", "dst"),
        P("dst", "src", None),
    )
    out_specs = (P("dst", "src", None), P(("src", "dst"), None), P())
    return jax.shard_map(shards, mesh=mesh, in_specs=in_specs, out_specs=out_specs, check_vma=False)
```

time: 261 us -> 233 us (0.89)
  blocking collectives: 112 us -> 74 us
  starting transfers between devices: 65.2 us -> 98.1 us
  Pallas kernels: 17.6 us -> 4.71 us
  waiting for transfers between devices: 54.4 us -> 45.5 us
  other arithmetic: 5.33 us -> 2.41 us
    all_to_all x1 -> x0, blocking collectives: 27.3 us -> none  [scatter_sources(): lax.all_to_all(message, 'dst', 0, 0, tiled=True, axis_index_groups=STRIDE...]
    ppermute x0 -> x4, starting transfers between devices: none -> 13.9 us  [scatter_sources(): swapped[which] = lax.ppermute(sent[which], 'dst', Y_SWAP)]
    ppermute x8 -> x11, starting transfers between devices: 34.3 us -> 47.5 us  [shift(): return lax.ppermute(array, 'dst', from_z(step))]
    all_gather x1 -> x0, blocking collectives: 11.3 us -> none  [pair_swap(): both = lax.all_gather(array, axis, axis=0, axis_index_groups=groups)]
    ppermute x8 -> x11, waiting for transfers between devices: 43.5 us -> 34.1 us  [shift(): return lax.ppermute(array, 'dst', from_z(step))]
    ppermute x0 -> x4, waiting for transfers between devices: none -> 7.47 us  [scatter_sources(): swapped[which] = lax.ppermute(sent[which], 'dst', Y_SWAP)]
    all_to_all x1 -> x2, waiting for transfers between devices: 6.94 us -> 0.01 us  [everywhere(): return lax.all_to_all(copies, axis, 0, 0, tiled=True)]
    pallas_call x1, Pallas kernels: 8.76 us -> 2.12 us  [forward_sums(): pl.pallas_call(forward_kernel, out_shape=(half, half), in_specs=[smem, sm...]
  transfers between devices with their start and end apart: 11 -> 19, of which waited for: 7 -> 11; matrix products, arithmetic and copies ran while one was open for 1% -> 2% of each run, Pallas kernels for 0% -> 0%
where the time goes in v3:
time: 233 us; the launch traced here: 232 us
  starting transfers between devices  98.1 us (42%)
  blocking collectives  74 us (32%)
  waiting for transfers between devices  45.5 us (20%)
  local copies, waits for them, and re-layouts  5.43 us (2%)
  Pallas kernels  4.71 us (2%)
  other arithmetic  2.41 us (1%)
    ppermute x11, starting transfers between devices, shift(): return lax.ppermute(array, 'dst', from_z(step))  47.5 us
    ppermute x11, waiting for transfers between devices, shift(): return lax.ppermute(array, 'dst', from_z(step))  34.1 us
    all_gather x1, blocking collectives, gather_sources(): lax.all_gather(features, 'dst', axis=0, axis_index_groups=STRIDE_GROUPS)  28 us
    all_to_all x1, blocking collectives, shards(): lax.all_to_all(chip_sums.reshape(CHIPS, ROWS, WIDTH), 'src', 0, 0, tiled=...  22.1 us
    all_to_all x2, starting transfers between devices, everywhere(): return lax.all_to_all(copies, axis, 0, 0, tiled=True)  18.5 us
    all_to_all x1, blocking collectives, shards(): lax.all_to_all(message, 'src', 0, 0, tiled=True, axis_index_groups=CORE_G...  16.6 us
    ppermute x4, starting transfers between devices, scatter_sources(): swapped[which] = lax.ppermute(sent[which], 'dst', Y_SWAP)  13.9 us
    ppermute x1, starting transfers between devices, shards(): swapped = lax.ppermute(other, 'src', CORE_SWAP)  13.8 us
  transfers between devices with their start and end apart: 19, of which 11 were waited for; matrix products, arithmetic and copies ran while one was open for 2% of the time, Pallas kernels for 0%

profile of v3, /device:TPU:1, one launch (start us, length us, event | category | flops | bytes accessed | tf_op | source)
XLA Modules:
  0.0 231.7 jit_solution(10161893083481990377)
XLA Ops:
  0.6 28.0 %all-gather = bf16[768,256]{1,0:T(8,128)(2,1)S(1)} all-gather(bf16[192,256]{1,0:T(8,128)(2,1)} %param.6), channel_id=2, replica_groups={{0,8,16,24},{1,9,17,25},{2,10,18,26},{3,11,19,27},{4,12,20,28},{5,13,21..., dimensions={0}, use_global_device_ids=true | all-gather | bytes 491520 | tf_op jit(solution)/shard_map/all_gather | solution.py:187
  28.7 7.3 %all_gather.11.g0 = bf16[4,384,256]{2,1,0:T(8,128)(2,1)S(1)} all-gather(bf16[4,192,256]{2,1,0:T(8,128)(2,1)S(1)} %bitcast.32), channel_id=1, replica_groups={{0,1},{2,3},{4,5},{6,7},{8,9},{10,11},{12,13},{14,15},{16,17},{18,19},{..., dimensions={1}, use_global_device_ids=true | all-gather | bytes 1179648 | tf_op jit(solution)/shard_map/all_gather | solution.py:188
  35.9 2.9 %collective-permute-start = (bf16[4,384,256]{2,1,0:T(8,128)(2,1)S(1)}, bf16[4,384,256]{2,1,0:T(8,128)(2,1)S(1)}, u32[]{:S(2)}, u32[]{:S(2)}) collective-permute-start(bf16[4,384,256]{2,1,0:T(8,128)(2,1)S(1)} %all_gather.11.g0), channel_id=1, source_target_pairs={{2,0},{3,1},{4,2},{5,3},{6,4},{7,5},{8,6},{9,7},{10,8},{11,9},{12,... | collective-permute-start | bytes 2359304 | tf_op jit(solution)/shard_map/ppermute | solution.py:183
  38.9 2.3 %collective-permute-start.2 = (bf16[4,384,256]{2,1,0:T(8,128)(2,1)S(1)}, bf16[4,384,256]{2,1,0:T(8,128)(2,1)S(1)}, u32[]{:S(2)}, u32[]{:S(2)}) collective-permute-start(bf16[4,384,256]{2,1,0:T(8,128)(2,1)S(1)} %all_gather.11.g0), channel_id=1, source_target_pairs={{30,0},{31,1},{0,2},{1,3},{2,4},{3,5},{4,6},{5,7},{6,8},{7,9},{8,1... | collective-permute-start | bytes 2359304 | tf_op jit(solution)/shard_map/ppermute | solution.py:183
  41.2 10.3 %collective-permute-done.g1 = bf16[4,384,256]{2,1,0:T(8,128)(2,1)S(1)} collective-permute-done((bf16[4,384,256]{2,1,0:T(8,128)(2,1)S(1)}, bf16[4,384,256]{2,1,0:T(8,128)(2,1)S(1)}, u32[]{:S(2)}, u32[]{:S(2)}) %collective-permute-start) | collective-permute-done | bytes 786464 | tf_op jit(solution)/shard_map/ppermute | solution.py:183
  52.3 4.6 %collective-permute-start.1 = (bf16[2,384,256]{2,1,0:T(8,128)(2,1)}, bf16[2,384,256]{2,1,0:T(8,128)(2,1)S(1)}, u32[]{:S(2)}, u32[]{:S(2)}) collective-permute-start(bf16[2,384,256]{2,1,0:T(8,128)(2,1)} %slice.40), channel_id=1, source_target_pairs={{2,0},{3,1},{4,2},{5,3},{6,4},{7,5},{8,6},{9,7},{10,8},{11,9},{12,... | collective-permute-start | bytes 1179656 | tf_op jit(solution)/shard_map/ppermute | solution.py:183
  61.9 5.8 %collective-permute-done.3.g2b = bf16[2,384,256]{2,1,0:T(8,128)(2,1)} collective-permute-done((bf16[2,384,256]{2,1,0:T(8,128)(2,1)}, bf16[2,384,256]{2,1,0:T(8,128)(2,1)}, u32[]{:S(2)}, u32[]{:S(2)}) %collective-permute-start.3) | collective-permute-done | bytes 393248 | tf_op jit(solution)/shard_map/ppermute | solution.py:183
  67.7 2.3 %copy-done = bf16[1,1,144,128,128]{4,3,2,1,0:T(8,128)(2,1)S(1)} copy-done((bf16[1,1,144,128,128]{4,3,2,1,0:T(8,128)(2,1)S(1)}, bf16[1,1,144,128,128]{4,3,2,1,0:T(8,128)(2,1)}, u32[]{:S(2)}) %copy-start) | copy-done | bytes 4718616
  72.2 13.8 %collective-permute-start.4 = (bf16[1536,256]{1,0:T(8,128)(2,1)S(1)}, bf16[1536,256]{1,0:T(8,128)(2,1)S(1)}, u32[]{:S(2)}, u32[]{:S(2)}) collective-permute-start(bf16[1536,256]{1,0:T(8,128)(2,1)S(1)} %get-tuple-element.19), channel_id=1, source_target_pairs={{0,32},{32,0},{64,96},{96,64},{128,160},{160,128},{192,224},{224,1... | collective-permute-start | bytes 2359304 | tf_op jit(solution)/shard_map/ppermute | solution.py:228
  88.1 22.1 %all_to_all.20.terms = bf16[8,192,256]{2,1,0:T(8,128)(2,1)S(1)} all-to-all(bf16[8,192,256]{2,1,0:T(8,128)(2,1)S(1)} %bitcast.31), channel_id=1, replica_groups={{0,64,128,192,256,320,384,448},{32,96,160,224,288,352,416,480},{1,65,12..., dimensions={0} | all-to-all | bytes 1572864 | tf_op jit(solution)/shard_map/all_to_all | solution.py:230
  111.0 16.6 %all_to_all.21.mine = bf16[8,224,256]{2,1,0:T(8,128)(2,1)S(1)} all-to-all(bf16[8,224,256]{2,1,0:T(8,128)(2,1)S(1)} %get-tuple-element.21), channel_id=1, replica_groups={{0,64,128,192,256,320,384,448},{32,96,160,224,288,352,416,480},{1,65,12..., dimensions={0} | all-to-all | bytes 1835008 | tf_op jit(solution)/shard_map/all_to_all | solution.py:234
  127.6 4.4 %collective-permute-start.5 = (bf16[8,224,256]{2,1,0:T(8,128)(2,1)S(1)}, bf16[8,224,256]{2,1,0:T(8,128)(2,1)S(1)}, u32[]{:S(2)}, u32[]{:S(2)}) collective-permute-start(bf16[8,224,256]{2,1,0:T(8,128)(2,1)S(1)} %all_to_all.21.mine), channel_id=1, source_target_pairs={{0,32},{32,0},{64,96},{96,64},{128,160},{160,128},{192,224},{224,1... | collective-permute-start | bytes 2752520 | tf_op jit(solution)/shard_map/ppermute | solution.py:235
  135.9 6.0 %collective-permute-start.8 = (bf16[768,256]{1,0:T(8,128)(2,1)S(1)}, bf16[768,256]{1,0:T(8,128)(2,1)S(1)}, u32[]{:S(2)}, u32[]{:S(2)}) collective-permute-start(bf16[768,256]{1,0:T(8,128)(2,1)S(1)} %get-tuple-element.27), channel_id=1, source_target_pairs={{0,1},{1,0},{2,3},{3,2},{4,5},{5,4},{6,7},{7,6},{8,9},{9,8},{10,11... | collective-permute-start | bytes 1179656 | tf_op jit(solution)/shard_map/ppermute | solution.py:202
  143.8 6.7 %collective-permute-done.8 = bf16[768,256]{1,0:T(8,128)(2,1)S(1)} collective-permute-done((bf16[768,256]{1,0:T(8,128)(2,1)S(1)}, bf16[768,256]{1,0:T(8,128)(2,1)S(1)}, u32[]{:S(2)}, u32[]{:S(2)}) %collective-permute-start.8) | collective-permute-done | bytes 393248 | tf_op jit(solution)/shard_map/ppermute | solution.py:202
  150.5 5.7 %collective-permute-start.12 = (bf16[384,256]{1,0:T(8,128)(2,1)S(1)}, bf16[384,256]{1,0:T(8,128)(2,1)S(1)}, u32[]{:S(2)}, u32[]{:S(2)}) collective-permute-start(bf16[384,256]{1,0:T(8,128)(2,1)S(1)} %get-tuple-element.34), channel_id=1, source_target_pairs={{2,0},{3,1},{4,2},{5,3},{6,4},{7,5},{8,6},{9,7},{10,8},{11,9},{12,... | collective-permute-start | bytes 589832 | tf_op jit(solution)/shard_map/ppermute | solution.py:183
  156.2 4.1 %collective-permute-start.7 = (bf16[768,256]{1,0:T(8,128)(2,1)S(1)}, bf16[768,256]{1,0:T(8,128)(2,1)S(1)}, u32[]{:S(2)}, u32[]{:S(2)}) collective-permute-start(bf16[768,256]{1,0:T(8,128)(2,1)S(1)} %get-tuple-element.25), channel_id=1, source_target_pairs={{0,1},{1,0},{2,3},{3,2},{4,5},{5,4},{6,7},{7,6},{8,9},{9,8},{10,11... | collective-permute-start | bytes 1179656 | tf_op jit(solution)/shard_map/ppermute | solution.py:202
  164.3 4.6 %collective-permute-start.13 = (bf16[768,256]{1,0:T(8,128)(2,1)S(1)}, bf16[768,256]{1,0:T(8,128)(2,1)S(1)}, u32[]{:S(2)}, u32[]{:S(2)}) collective-permute-start(bf16[768,256]{1,0:T(8,128)(2,1)S(1)} %add_convert_fusion.2), channel_id=1, source_target_pairs={{2,0},{3,1},{4,2},{5,3},{6,4},{7,5},{8,6},{9,7},{10,8},{11,9},{12,... | collective-permute-start | bytes 1179656 | tf_op jit(solution)/shard_map/ppermute | solution.py:183
  170.1 2.6 %collective-permute-start.10 = (bf16[768,256]{1,0:T(8,128)(2,1)S(1)}, bf16[768,256]{1,0:T(8,128)(2,1)S(1)}, u32[]{:S(2)}, u32[]{:S(2)}) collective-permute-start(bf16[768,256]{1,0:T(8,128)(2,1)S(1)} %add_convert_fusion.3), channel_id=1, source_target_pairs={{30,0},{31,1},{0,2},{1,3},{2,4},{3,5},{4,6},{5,7},{6,8},{7,9},{8,1... | collective-permute-start | bytes 1179656 | tf_op jit(solution)/shard_map/ppermute | solution.py:183
  174.0 6.5 %collective-permute-done.10 = bf16[768,256]{1,0:T(8,128)(2,1)S(1)} collective-permute-done((bf16[768,256]{1,0:T(8,128)(2,1)S(1)}, bf16[768,256]{1,0:T(8,128)(2,1)S(1)}, u32[]{:S(2)}, u32[]{:S(2)}) %collective-permute-start.10) | collective-permute-done | bytes 393248 | tf_op jit(solution)/shard_map/ppermute | solution.py:183
  181.5 10.3 %all-to-all-start.2 = ((bf16[32,16,256]{2,1,0:T(8,128)(2,1)}), bf16[32,16,256]{2,1,0:T(8,128)(2,1)S(1)}, u32[]{:S(2)}, u32[]{:S(2)}) async-start(bf16[32,16,256]{2,1,0:T(8,128)(2,1)} %broadcast_in_dim.14), calls=%async_computation.2 | async-start | bytes 524288 | tf_op jit(solution)/shard_map/all_to_all | solution.py:215
  191.8 7.1 %collective-permute-start.16 = (bf16[192,256]{1,0:T(8,128)(2,1)S(1)}, bf16[192,256]{1,0:T(8,128)(2,1)S(1)}, u32[]{:S(2)}, u32[]{:S(2)}) collective-permute-start(bf16[192,256]{1,0:T(8,128)(2,1)S(1)} %get-tuple-element.36), channel_id=1, source_target_pairs={{8,0},{9,1},{10,2},{11,3},{12,4},{13,5},{14,6},{15,7},{16,8},{17,9... | collective-permute-start | bytes 294920 | tf_op jit(solution)/shard_map/ppermute | solution.py:183
  201.0 11.9 %collective-permute-start.14 = (bf16[192,256]{1,0:T(8,128)(2,1)S(1)}, bf16[192,256]{1,0:T(8,128)(2,1)S(1)}, u32[]{:S(2)}, u32[]{:S(2)}) collective-permute-start(bf16[192,256]{1,0:T(8,128)(2,1)S(1)} %get-tuple-element.35), channel_id=1, source_target_pairs={{16,0},{17,1},{18,2},{19,3},{20,4},{21,5},{22,6},{23,7},{24,8},{25... | collective-permute-start | bytes 294920 | tf_op jit(solution)/shard_map/ppermute | solution.py:183
  213.6 8.2 %all-to-all-start.3 = ((bf16[16,16,256]{2,1,0:T(8,128)(2,1)}), bf16[16,16,256]{2,1,0:T(8,128)(2,1)S(1)}, u32[]{:S(2)}, u32[]{:S(2)}) async-start(bf16[16,16,256]{2,1,0:T(8,128)(2,1)} %broadcast_in_dim.15), calls=%async_computation.3 | async-start | bytes 262144 | tf_op jit(solution)/shard_map/all_to_all | solution.py:215
  221.8 8.5 %collective-permute-done.14 = bf16[192,256]{1,0:T(8,128)(2,1)S(1)} collective-permute-done((bf16[192,256]{1,0:T(8,128)(2,1)S(1)}, bf16[192,256]{1,0:T(8,128)(2,1)S(1)}, u32[]{:S(2)}, u32[]{:S(2)}) %collective-permute-start.14) | collective-permute-done | bytes 98336 | tf_op jit(solution)/shard_map/ppermute | solution.py:183
  (50 shorter events, 27.7 us)
Async XLA Ops:
  0.6 59.6 %copy-start.3 = (s32[1,1,144,2]{2,3,1,0:T(2,128)S(1)}, s32[1,1,144,2]{2,3,1,0:T(2,128)}, u32[]{:S(2)}) copy-start(s32[1,1,144,2]{2,3,1,0:T(2,128)} %param.9) | copy-start | bytes 3460
  35.9 15.6 %collective-permute-start = (bf16[4,384,256]{2,1,0:T(8,128)(2,1)S(1)}, bf16[4,384,256]{2,1,0:T(8,128)(2,1)S(1)}, u32[]{:S(2)}, u32[]{:S(2)}) collective-permute-start(bf16[4,384,256]{2,1,0:T(8,128)(2,1)S(1)} %all_gather.11.g0), channel_id=1, source_target_pairs={{2,0},{3,1},{4,2},{5,3},{6,4},{7,5},{8,6},{9,7},{10,8},{11,9},{12,... | collective-permute-start | bytes 2359304 | tf_op jit(solution)/shard_map/ppermute | solution.py:183
  38.9 18.0 %collective-permute-start.2 = (bf16[4,384,256]{2,1,0:T(8,128)(2,1)S(1)}, bf16[4,384,256]{2,1,0:T(8,128)(2,1)S(1)}, u32[]{:S(2)}, u32[]{:S(2)}) collective-permute-start(bf16[4,384,256]{2,1,0:T(8,128)(2,1)S(1)} %all_gather.11.g0), channel_id=1, source_target_pairs={{30,0},{31,1},{0,2},{1,3},{2,4},{3,5},{4,6},{5,7},{6,8},{7,9},{8,1... | collective-permute-start | bytes 2359304 | tf_op jit(solution)/shard_map/ppermute | solution.py:183
  51.5 82.7 %slice-start = ((s8[4718592]{0:T(1024)(128)(4,1)}), s8[524288]{0:T(1024)(128)(4,1)S(1)}, s32[]{:S(2)}) async-start(s8[4718592]{0:T(1024)(128)(4,1)} %bitcast.27), calls=%async_computation.4 | async-start | bytes 1048576
  52.3 9.6 %collective-permute-start.1 = (bf16[2,384,256]{2,1,0:T(8,128)(2,1)}, bf16[2,384,256]{2,1,0:T(8,128)(2,1)S(1)}, u32[]{:S(2)}, u32[]{:S(2)}) collective-permute-start(bf16[2,384,256]{2,1,0:T(8,128)(2,1)} %slice.40), channel_id=1, source_target_pairs={{2,0},{3,1},{4,2},{5,3},{6,4},{7,5},{8,6},{9,7},{10,8},{11,9},{12,... | collective-permute-start | bytes 1179656 | tf_op jit(solution)/shard_map/ppermute | solution.py:183
  57.7 10.0 %collective-permute-start.3 = (bf16[2,384,256]{2,1,0:T(8,128)(2,1)}, bf16[2,384,256]{2,1,0:T(8,128)(2,1)}, u32[]{:S(2)}, u32[]{:S(2)}) collective-permute-start(bf16[2,384,256]{2,1,0:T(8,128)(2,1)} %slice.41), channel_id=1, source_target_pairs={{30,0},{31,1},{0,2},{1,3},{2,4},{3,5},{4,6},{5,7},{6,8},{7,9},{8,1... | collective-permute-start | bytes 1179656 | tf_op jit(solution)/shard_map/ppermute | solution.py:183
  70.0 64.1 %slice-start.1 = ((s8[4718592]{0:T(1024)(128)(4,1)}), s8[4194304]{0:T(1024)(128)(4,1)S(1)}, s32[]{:S(2)}) async-start(s8[4718592]{0:T(1024)(128)(4,1)} %bitcast.27), calls=%async_computation.5 | async-start | bytes 8388608
  72.2 15.7 %collective-permute-start.4 = (bf16[1536,256]{1,0:T(8,128)(2,1)S(1)}, bf16[1536,256]{1,0:T(8,128)(2,1)S(1)}, u32[]{:S(2)}, u32[]{:S(2)}) collective-permute-start(bf16[1536,256]{1,0:T(8,128)(2,1)S(1)} %get-tuple-element.19), channel_id=1, source_target_pairs={{0,32},{32,0},{64,96},{96,64},{128,160},{160,128},{192,224},{224,1... | collective-permute-start | bytes 2359304 | tf_op jit(solution)/shard_map/ppermute | solution.py:228
  87.8 22.3 %copy-start.1 = (bf16[256,256]{1,0:T(8,128)(2,1)S(1)}, bf16[256,256]{1,0:T(8,128)(2,1)}, u32[]{:S(2)}) copy-start(bf16[256,256]{1,0:T(8,128)(2,1)} %weight.1) | copy-start | bytes 393220
  87.8 22.3 %copy-start.2 = (bf16[1,192,256]{2,1,0:T(8,128)(2,1)S(1)}, bf16[1,192,256]{2,1,0:T(8,128)(2,1)}, u32[]{:S(2)}) copy-start(bf16[1,192,256]{2,1,0:T(8,128)(2,1)} %param.11) | copy-start | bytes 294916
  127.6 6.5 %collective-permute-start.5 = (bf16[8,224,256]{2,1,0:T(8,128)(2,1)S(1)}, bf16[8,224,256]{2,1,0:T(8,128)(2,1)S(1)}, u32[]{:S(2)}, u32[]{:S(2)}) collective-permute-start(bf16[8,224,256]{2,1,0:T(8,128)(2,1)S(1)} %all_to_all.21.mine), channel_id=1, source_target_pairs={{0,32},{32,0},{64,96},{96,64},{128,160},{160,128},{192,224},{224,1... | collective-permute-start | bytes 2752520 | tf_op jit(solution)/shard_map/ppermute | solution.py:235
  135.9 14.6 %collective-permute-start.8 = (bf16[768,256]{1,0:T(8,128)(2,1)S(1)}, bf16[768,256]{1,0:T(8,128)(2,1)S(1)}, u32[]{:S(2)}, u32[]{:S(2)}) collective-permute-start(bf16[768,256]{1,0:T(8,128)(2,1)S(1)} %get-tuple-element.27), channel_id=1, source_target_pairs={{0,1},{1,0},{2,3},{3,2},{4,5},{5,4},{6,7},{7,6},{8,9},{9,8},{10,11... | collective-permute-start | bytes 1179656 | tf_op jit(solution)/shard_map/ppermute | solution.py:202
  141.8 22.3 %collective-permute-start.11 = (bf16[768,256]{1,0:T(8,128)(2,1)S(1)}, bf16[768,256]{1,0:T(8,128)(2,1)S(1)}, u32[]{:S(2)}, u32[]{:S(2)}) collective-permute-start(bf16[768,256]{1,0:T(8,128)(2,1)S(1)} %get-tuple-element.29), channel_id=1, source_target_pairs={{0,1},{1,0},{2,3},{3,2},{4,5},{5,4},{6,7},{7,6},{8,9},{9,8},{10,11... | collective-permute-start | bytes 1179656 | tf_op jit(solution)/shard_map/ppermute | solution.py:202
  150.5 13.7 %collective-permute-start.12 = (bf16[384,256]{1,0:T(8,128)(2,1)S(1)}, bf16[384,256]{1,0:T(8,128)(2,1)S(1)}, u32[]{:S(2)}, u32[]{:S(2)}) collective-permute-start(bf16[384,256]{1,0:T(8,128)(2,1)S(1)} %get-tuple-element.34), channel_id=1, source_target_pairs={{2,0},{3,1},{4,2},{5,3},{6,4},{7,5},{8,6},{9,7},{10,8},{11,9},{12,... | collective-permute-start | bytes 589832 | tf_op jit(solution)/shard_map/ppermute | solution.py:183
  156.2 12.7 %collective-permute-start.7 = (bf16[768,256]{1,0:T(8,128)(2,1)S(1)}, bf16[768,256]{1,0:T(8,128)(2,1)S(1)}, u32[]{:S(2)}, u32[]{:S(2)}) collective-permute-start(bf16[768,256]{1,0:T(8,128)(2,1)S(1)} %get-tuple-element.25), channel_id=1, source_target_pairs={{0,1},{1,0},{2,3},{3,2},{4,5},{5,4},{6,7},{7,6},{8,9},{9,8},{10,11... | collective-permute-start | bytes 1179656 | tf_op jit(solution)/shard_map/ppermute | solution.py:202
  160.3 13.1 %collective-permute-start.6 = (bf16[768,256]{1,0:T(8,128)(2,1)S(1)}, bf16[768,256]{1,0:T(8,128)(2,1)S(1)}, u32[]{:S(2)}, u32[]{:S(2)}) collective-permute-start(bf16[768,256]{1,0:T(8,128)(2,1)S(1)} %get-tuple-element.23), channel_id=1, source_target_pairs={{0,1},{1,0},{2,3},{3,2},{4,5},{5,4},{6,7},{7,6},{8,9},{9,8},{10,11... | collective-permute-start | bytes 1179656 | tf_op jit(solution)/shard_map/ppermute | solution.py:202
  162.3 7.6 %collective-permute-start.9 = (bf16[384,256]{1,0:T(8,128)(2,1)S(1)}, bf16[384,256]{1,0:T(8,128)(2,1)S(1)}, u32[]{:S(2)}, u32[]{:S(2)}) collective-permute-start(bf16[384,256]{1,0:T(8,128)(2,1)S(1)} %get-tuple-element.33), channel_id=1, source_target_pairs={{30,0},{31,1},{0,2},{1,3},{2,4},{3,5},{4,6},{5,7},{6,8},{7,9},{8,1... | collective-permute-start | bytes 589832 | tf_op jit(solution)/shard_map/ppermute | solution.py:183
  164.3 9.6 %collective-permute-start.13 = (bf16[768,256]{1,0:T(8,128)(2,1)S(1)}, bf16[768,256]{1,0:T(8,128)(2,1)S(1)}, u32[]{:S(2)}, u32[]{:S(2)}) collective-permute-start(bf16[768,256]{1,0:T(8,128)(2,1)S(1)} %add_convert_fusion.2), channel_id=1, source_target_pairs={{2,0},{3,1},{4,2},{5,3},{6,4},{7,5},{8,6},{9,7},{10,8},{11,9},{12,... | collective-permute-start | bytes 1179656 | tf_op jit(solution)/shard_map/ppermute | solution.py:183
  170.1 10.4 %collective-permute-start.10 = (bf16[768,256]{1,0:T(8,128)(2,1)S(1)}, bf16[768,256]{1,0:T(8,128)(2,1)S(1)}, u32[]{:S(2)}, u32[]{:S(2)}) collective-permute-start(bf16[768,256]{1,0:T(8,128)(2,1)S(1)} %add_convert_fusion.3), channel_id=1, source_target_pairs={{30,0},{31,1},{0,2},{1,3},{2,4},{3,5},{4,6},{5,7},{6,8},{7,9},{8,1... | collective-permute-start | bytes 1179656 | tf_op jit(solution)/shard_map/ppermute | solution.py:183
  181.5 31.4 %all-to-all-start.2 = ((bf16[32,16,256]{2,1,0:T(8,128)(2,1)}), bf16[32,16,256]{2,1,0:T(8,128)(2,1)S(1)}, u32[]{:S(2)}, u32[]{:S(2)}) async-start(bf16[32,16,256]{2,1,0:T(8,128)(2,1)} %broadcast_in_dim.14), calls=%async_computation.2 | async-start | bytes 524288 | tf_op jit(solution)/shard_map/all_to_all | solution.py:215
  191.8 30.0 %collective-permute-start.16 = (bf16[192,256]{1,0:T(8,128)(2,1)S(1)}, bf16[192,256]{1,0:T(8,128)(2,1)S(1)}, u32[]{:S(2)}, u32[]{:S(2)}) collective-permute-start(bf16[192,256]{1,0:T(8,128)(2,1)S(1)} %get-tuple-element.36), channel_id=1, source_target_pairs={{8,0},{9,1},{10,2},{11,3},{12,4},{13,5},{14,6},{15,7},{16,8},{17,9... | collective-permute-start | bytes 294920 | tf_op jit(solution)/shard_map/ppermute | solution.py:183
  198.9 22.9 %collective-permute-start.15 = (bf16[192,256]{1,0:T(8,128)(2,1)S(1)}, bf16[192,256]{1,0:T(8,128)(2,1)S(1)}, u32[]{:S(2)}, u32[]{:S(2)}) collective-permute-start(bf16[192,256]{1,0:T(8,128)(2,1)S(1)} %get-tuple-element.37), channel_id=1, source_target_pairs={{24,0},{25,1},{26,2},{27,3},{28,4},{29,5},{30,6},{31,7},{0,8},{1,9... | collective-permute-start | bytes 294920 | tf_op jit(solution)/shard_map/ppermute | solution.py:183
  201.0 29.3 %collective-permute-start.14 = (bf16[192,256]{1,0:T(8,128)(2,1)S(1)}, bf16[192,256]{1,0:T(8,128)(2,1)S(1)}, u32[]{:S(2)}, u32[]{:S(2)}) collective-permute-start(bf16[192,256]{1,0:T(8,128)(2,1)S(1)} %get-tuple-element.35), channel_id=1, source_target_pairs={{16,0},{17,1},{18,2},{19,3},{20,4},{21,5},{22,6},{23,7},{24,8},{25... | collective-permute-start | bytes 294920 | tf_op jit(solution)/shard_map/ppermute | solution.py:183
  213.6 17.4 %all-to-all-start.3 = ((bf16[16,16,256]{2,1,0:T(8,128)(2,1)}), bf16[16,16,256]{2,1,0:T(8,128)(2,1)S(1)}, u32[]{:S(2)}, u32[]{:S(2)}) async-start(bf16[16,16,256]{2,1,0:T(8,128)(2,1)} %broadcast_in_dim.15), calls=%async_computation.3 | async-start | bytes 262144 | tf_op jit(solution)/shard_map/all_to_all | solution.py:215
  (1 other events, 2.3 us)

commit v4 on v3

--- a/solution.py
+++ b/solution.py
@@ -15,13 +15,20 @@
 WIDTH = 256
 ROWS = 192
 PAIR = NY * ROWS
-VMEM_LIMIT = 32 * 1024 * 1024
+VMEM_LIMIT = 24 * 1024 * 1024
 
 STRIDE_GROUPS = [[2 * z + y for z in range(q, NZ, 4)] for q in range(4) for y in range(NY)]
 Y_GROUPS = [[2 * z, 2 * z + 1] for z in range(NZ)]
 Y_SWAP = [(d, d ^ 1) for d in range(NZ * NY)]
 CHIPS = N_SRC // 2
 CORE_GROUPS = [[2 * chip + core for chip in range(CHIPS)] for core in range(2)]
+CHIP_PAIRS = [[2 * chip, 2 * chip + 1] for chip in range(CHIPS)]
+PEER_GROUPS = [
+    [(2 * chip + core) * NZ * NY + (q + 4 * m) * NY + y for m in range(4) for chip in range(CHIPS)]
+    for core in range(2)
+    for q in range(4)
+    for y in range(NY)
+]
 CORE_SWAP = [(s, s ^ 1) for s in range(N_SRC)]
 
 
@@ -30,16 +37,16 @@
 
 
 def each_slot(slot_count, one_slot):
-    def four(i, carry):
-        one_slot([4 * i + u for u in range(4)])
-        return carry
-
-    def single(i, carry):
-        one_slot([i])
-        return carry
-
-    lax.fori_loop(0, slot_count // 4, four, 0)
-    lax.fori_loop((slot_count // 4) * 4, slot_count, single, 0)
+    done = 0
+    for step in (16, 4, 1):
+
+        def several(i, carry, step=step, done=done):
+            one_slot([done + i * step + u for u in range(step)])
+            return carry
+
+        turns = (slot_count - done) // step
+        lax.fori_loop(0, turns, several, 0)
+        done = done + turns * step
 
 
 def block_of(ref, index):
@@ -51,7 +58,7 @@
     ref[span, :] = ref[span, :] + term
 
 
-def forward_kernel(meta, coords, blocks, g0, g1, g2a, g2b, g3, own, other, rows, total):
+def forward_kernel(meta, coords, blocks, g0, g1a, g1b, g2a, g2b, g3a, g3b, own, other, rows, total):
     slot_count, z, core = meta[0], meta[1], meta[3]
     slots = blocks.shape[0]
 
@@ -65,7 +72,8 @@
         for k, term in zip(ks, terms):
             add_block(total, coords[slots + k], term)
 
-    for offset, ref, first in ((0, g0, 0), (1, g1, 0), (3, g3, 0), (2, g2a, 0), (2, g2b, 2)):
+    pieces = ((0, g0, 0), (1, g1a, 0), (1, g1b, 2), (2, g2a, 0), (2, g2b, 2), (3, g3a, 0), (3, g3b, 2))
+    for offset, ref, first in pieces:
         residue = lax.rem(z + offset, 4)
         for i in range(ref.shape[0]):
             place = pl.multiple_of((residue + 4 * (first + i)) * PAIR, PAIR)
@@ -86,7 +94,7 @@
     return pl.pallas_call(
         forward_kernel,
         out_shape=(half, half),
-        in_specs=[smem, smem] + [vmem] * 6,
+        in_specs=[smem, smem] + [vmem] * 8,
         out_specs=(vmem, vmem),
         scratch_shapes=[pltpu.VMEM((source_rows, WIDTH), BF16), pltpu.VMEM((dest_rows, WIDTH), F32)],
         compiler_params=pltpu.CompilerParams(vmem_limit_bytes=VMEM_LIMIT),
@@ -149,7 +157,8 @@
             rows[pl.ds(place, ROWS), :] = ref[chip, :ROWS, :]
             tail = pl.ds(pl.multiple_of(ROWS + core * share, share), share)
             summed = summed + ref[chip, tail, :].astype(F32)
-    wsum[...] = summed.astype(BF16)
+    wsum[...] = summed
+    sent[2][4 * ROWS :, :] = summed.astype(BF16)
     total[...] = jnp.zeros_like(total)
     each_slot(slot_count, one_slot)
     for refs, side in ((sent, 1 - y), (kept, y)):
@@ -169,7 +178,12 @@
     half = jax.ShapeDtypeStruct((4 * ROWS, WIDTH), BF16)
     out = pl.pallas_call(
         backward_kernel,
-        out_shape=(half,) * 8 + (jax.ShapeDtypeStruct((share, WIDTH), BF16),),
+        out_shape=(half,) * 6
+        + (
+            jax.ShapeDtypeStruct((4 * ROWS + share, WIDTH), BF16),
+            half,
+            jax.ShapeDtypeStruct((share, WIDTH), F32),
+        ),
         in_specs=[smem, smem, vmem, vmem, vmem],
         out_specs=(vmem,) * 9,
         scratch_shapes=[pltpu.VMEM((dest_rows, WIDTH), BF16), pltpu.VMEM((source_rows, WIDTH), F32)],
@@ -186,33 +200,49 @@
 def gather_sources(features):
     own = lax.all_gather(features, "dst", axis=0, axis_index_groups=STRIDE_GROUPS)
     own = lax.all_gather(own, "dst", axis=1, tiled=True, axis_index_groups=Y_GROUPS)
-    right = shift(own, 1)
-    left = shift(own, -1)
-    return own, right, shift(right[:2], 1), shift(left[2:], -1), left
+    low, high = own[:2], own[2:]
+    right_low, left_high = shift(low, 1), shift(high, -1)
+    right_high, left_low = shift(high, 1), shift(low, -1)
+    far_low, far_high = shift(right_low, 1), shift(left_high, -1)
+    return own, right_low, right_high, far_low, far_high, left_low, left_high
 
 
 def total_of(*terms):
     return sum(term.astype(F32) for term in terms).astype(BF16)
 
 
+def total_f32(*terms):
+    return sum(term.astype(F32) for term in terms)
+
+
 def scatter_sources(kept, sent, weight_part):
-    half = 2 * ROWS
+    half, full = 2 * ROWS, 4 * ROWS
     swapped = [None] * 4
     for which in (2, 1, 3, 0):
         swapped[which] = lax.ppermute(sent[which], "dst", Y_SWAP)
+    w = total_f32(weight_part, swapped[2][full:])
     low = shift(total_of(kept[2][:half], swapped[2][:half]), -1)
-    high = shift(total_of(kept[2][half:], swapped[2][half:]), 1)
+    high = jnp.concatenate([total_of(kept[2][half:], swapped[2][half:full]), w.astype(BF16)], 0)
+    high = shift(high, 1)
+    w = total_of(w, high[half:])
     none = jnp.zeros_like(low[:ROWS])
     up = total_of(kept[1], swapped[1], jnp.concatenate([none, low, none], 0))
-    down = total_of(kept[3], swapped[3], jnp.concatenate([high, none, none], 0))
-    near = total_of(kept[0], swapped[0], shift(up, -1), shift(down, 1)).reshape(4, ROWS, WIDTH)
-    near, weight_part = lax.optimization_barrier((near, weight_part))
-    return total_of(near[0], shift(near[2], -8), shift(near[1], -4), shift(near[3], 4)), weight_part
-
-
-def everywhere(part, axis, count):
-    copies = jnp.broadcast_to(part, (count,) + part.shape)
-    return lax.all_to_all(copies, axis, 0, 0, tiled=True)
+    down = total_of(kept[3], swapped[3], jnp.concatenate([high[:half], none, none], 0))
+    up = shift(jnp.concatenate([up, w], 0), -1)
+    down = shift(jnp.concatenate([down, w], 0), 1)
+    w = total_of(up[full:], down[full:])
+    near = total_of(kept[0], swapped[0], up[:full], down[:full]).reshape(4, ROWS, WIDTH)
+    far, left, right = shift(near[2], -8), shift(near[1], -4), shift(near[3], 4)
+    weight_grad, mine = lax.optimization_barrier((gather_weight(w), near[0]))
+    return total_of(mine, far, left, right), weight_grad
+
+
+def gather_weight(part):
+    share = part.shape[0]
+    pair = lax.all_gather(part, "src", axis=0, tiled=True, axis_index_groups=CHIP_PAIRS)
+    copies = jnp.broadcast_to(pair, (4 * CHIPS,) + pair.shape)
+    pieces = lax.all_to_all(copies, ("src", "dst"), 0, 0, tiled=True, axis_index_groups=PEER_GROUPS)
+    return jnp.sum(pieces.astype(F32).reshape(4, CHIPS * 2 * share, WIDTH), axis=0)
 
 
 def shards(features, weight, values, coords, counts, cotangent):
@@ -224,7 +254,10 @@
     dest_rows = cotangent.shape[1] * N_SRC
 
     parts = gather_sources(features)
-    own, other = forward_sums(meta, pairs, tile_values, parts, dest_rows)
+    tile_values, _ = lax.optimization_barrier((tile_values, parts[0]))
+    live = jnp.arange(tile_values.shape[0], dtype=jnp.int32) < meta[0]
+    blocks = jnp.where(live[:, None, None], tile_values, jnp.zeros((), BF16))
+    own, other = forward_sums(meta, pairs, blocks, parts, dest_rows)
     swapped = lax.ppermute(other, "src", CORE_SWAP)
     chip_sums = (own.astype(F32) + swapped.astype(F32)).astype(BF16)
     terms = lax.all_to_all(
@@ -233,12 +266,9 @@
     activations, message = middle(terms, weight, cotangent[0])
     mine = lax.all_to_all(message, "src", 0, 0, tiled=True, axis_index_groups=CORE_GROUPS)
     theirs = lax.ppermute(mine, "src", CORE_SWAP)
-    kept, sent, weight_part = backward_sums(meta, pairs, tile_values, mine, theirs)
-    input_grad, weight_part = scatter_sources(kept, sent, weight_part)
-    weight_part = everywhere(weight_part, "dst", NZ * NY)
-    weight_part = jnp.sum(weight_part.astype(F32), axis=0).astype(BF16)
-    weight_grad = everywhere(weight_part, "src", N_SRC).reshape(WIDTH, WIDTH)
-    return (activations[None], input_grad, weight_grad.astype(F32))
+    kept, sent, weight_part = backward_sums(meta, pairs, blocks, mine, theirs)
+    input_grad, weight_grad = scatter_sources(kept, sent, weight_part)
+    return (activations[None], input_grad, weight_grad)
 
 
 def solution(mesh):

time: 233 us -> 235 us (level)
  starting transfers between devices: 98.1 us -> 78.8 us
  waiting for transfers between devices: 45.5 us -> 61.8 us
  local copies, waits for them, and re-layouts: 5.43 us -> 1.75 us
  Pallas kernels: 4.71 us -> 8.07 us
  other arithmetic: 2.41 us -> 5.17 us
    ppermute x4, waiting for transfers between devices: 7.47 us -> 26.6 us  [scatter_sources(): swapped[which] = lax.ppermute(sent[which], 'dst', Y_SWAP)]
    all_to_all x2 -> x1, starting transfers between devices: 18.5 us -> 8.95 us  [gather_weight(): lax.all_to_all(copies, ('src', 'dst'), 0, 0, tiled=True, axis_index_group...]
    ppermute x1, starting transfers between devices: 13.8 us -> 5.3 us  [shards(): swapped = lax.ppermute(other, 'src', CORE_SWAP)]
    ppermute x4, starting transfers between devices: 13.9 us -> 9.12 us  [scatter_sources(): swapped[which] = lax.ppermute(sent[which], 'dst', Y_SWAP)]
    ppermute x11 -> x13, starting transfers between devices: 47.5 us -> 51 us  [shift(): return lax.ppermute(array, 'dst', from_z(step))]
    all_gather x0 -> x1, blocking collectives: none -> 3.12 us  [gather_weight(): lax.all_gather(part, 'src', axis=0, tiled=True, axis_index_groups=CHIP_PA...]
    ppermute x11 -> x13, waiting for transfers between devices: 34.1 us -> 31.2 us  [shift(): return lax.ppermute(array, 'dst', from_z(step))]
    select_n x0 -> x1, other arithmetic: none -> 2.73 us  [shards(): blocks = jnp.where(live[:, None, None], tile_values, jnp.zeros((), BF16))]
  transfers between devices with their start and end apart: 19 -> 20, of which waited for: 11 -> 13; matrix products, arithmetic and copies ran while one was open for 2% -> 2% of each run, Pallas kernels for 0% -> 0%
where the time goes in v4:
time: 235 us; the launch traced here: 233 us
  starting transfers between devices  78.8 us (34%)
  blocking collectives  75.7 us (32%)
  waiting for transfers between devices  61.8 us (26%)
  Pallas kernels  8.07 us (3%)
  other arithmetic  5.17 us (2%)
    ppermute x13, starting transfers between devices, shift(): return lax.ppermute(array, 'dst', from_z(step))  51 us
    ppermute x13, waiting for transfers between devices, shift(): return lax.ppermute(array, 'dst', from_z(step))  31.2 us
    all_gather x1, blocking collectives, gather_sources(): lax.all_gather(features, 'dst', axis=0, axis_index_groups=STRIDE_GROUPS)  28 us
    ppermute x4, waiting for transfers between devices, scatter_sources(): swapped[which] = lax.ppermute(sent[which], 'dst', Y_SWAP)  26.6 us
    all_to_all x1, blocking collectives, shards(): lax.all_to_all(chip_sums.reshape(CHIPS, ROWS, WIDTH), 'src', 0, 0, tiled=...  20.6 us
    all_to_all x1, blocking collectives, shards(): lax.all_to_all(message, 'src', 0, 0, tiled=True, axis_index_groups=CORE_G...  16.6 us
    ppermute x4, starting transfers between devices, scatter_sources(): swapped[which] = lax.ppermute(sent[which], 'dst', Y_SWAP)  9.12 us
    all_to_all x1, starting transfers between devices, gather_weight(): lax.all_to_all(copies, ('src', 'dst'), 0, 0, tiled=True, axis_index_group...  8.95 us
  transfers between devices with their start and end apart: 20, of which 13 were waited for; matrix products, arithmetic and copies ran while one was open for 2% of the time, Pallas kernels for 0%

profile of v4, /device:TPU:1, one launch (start us, length us, event | category | flops | bytes accessed | tf_op | source)
XLA Modules:
  0.0 232.8 jit_solution(1202119329696268403)
XLA Ops:
  0.6 28.0 %all-gather = bf16[768,256]{1,0:T(8,128)(2,1)S(1)} all-gather(bf16[192,256]{1,0:T(8,128)(2,1)} %param.6), channel_id=2, replica_groups={{0,8,16,24},{1,9,17,25},{2,10,18,26},{3,11,19,27},{4,12,20,28},{5,13,21..., dimensions={0}, use_global_device_ids=true | all-gather | bytes 491520 | tf_op jit(solution)/shard_map/all_gather | solution.py:201
  28.6 7.3 %all_gather.14.g0 = bf16[4,384,256]{2,1,0:T(8,128)(2,1)S(1)} all-gather(bf16[4,192,256]{2,1,0:T(8,128)(2,1)S(1)} %bitcast.23), channel_id=1, replica_groups={{0,1},{2,3},{4,5},{6,7},{8,9},{10,11},{12,13},{14,15},{16,17},{18,19},{..., dimensions={1}, use_global_device_ids=true | all-gather | bytes 1179648 | tf_op jit(solution)/shard_map/all_gather | solution.py:202
  41.3 4.2 %collective-permute-start.1 = (bf16[2,384,256]{2,1,0:T(8,128)(2,1)S(1)}, bf16[2,384,256]{2,1,0:T(8,128)(2,1)S(1)}, u32[]{:S(2)}, u32[]{:S(2)}) collective-permute-start(bf16[2,384,256]{2,1,0:T(8,128)(2,1)S(1)} %get-tuple-element.37), channel_id=1, source_target_pairs={{2,0},{3,1},{4,2},{5,3},{6,4},{7,5},{8,6},{9,7},{10,8},{11,9},{12,... | collective-permute-start | bytes 1179656 | tf_op jit(solution)/shard_map/ppermute | solution.py:197
  48.9 4.6 %collective-permute-start.2 = (bf16[2,384,256]{2,1,0:T(8,128)(2,1)S(1)}, bf16[2,384,256]{2,1,0:T(8,128)(2,1)S(1)}, u32[]{:S(2)}, u32[]{:S(2)}) collective-permute-start(bf16[2,384,256]{2,1,0:T(8,128)(2,1)S(1)} %collective-permute-done.g1a), channel_id=1, source_target_pairs={{2,0},{3,1},{4,2},{5,3},{6,4},{7,5},{8,6},{9,7},{10,8},{11,9},{12,... | collective-permute-start | bytes 1179656 | tf_op jit(solution)/shard_map/ppermute | solution.py:197
  59.7 3.1 %collective-permute-done.2.g2a = bf16[2,384,256]{2,1,0:T(8,128)(2,1)S(1)} collective-permute-done((bf16[2,384,256]{2,1,0:T(8,128)(2,1)S(1)}, bf16[2,384,256]{2,1,0:T(8,128)(2,1)S(1)}, u32[]{:S(2)}, u32[]{:S(2)}) %collective-permute-start.2) | collective-permute-done | bytes 393248 | tf_op jit(solution)/shard_map/ppermute | solution.py:197
  62.8 5.3 %collective-permute-done.4.g2b = bf16[2,384,256]{2,1,0:T(8,128)(2,1)S(1)} collective-permute-done((bf16[2,384,256]{2,1,0:T(8,128)(2,1)S(1)}, bf16[2,384,256]{2,1,0:T(8,128)(2,1)S(1)}, u32[]{:S(2)}, u32[]{:S(2)}) %collective-permute-start.4) | collective-permute-done | bytes 393248 | tf_op jit(solution)/shard_map/ppermute | solution.py:197
  68.1 3.6 %forward_sums.1 = (bf16[1536,256]{1,0:T(8,128)(2,1)S(1)}, bf16[1536,256]{1,0:T(8,128)(2,1)S(1)}) custom-call(s32[4]{0:T(128)S(1)} %pad_add_fusion.meta, s32[288]{0:T(512)S(1)} %reshape.31.coords, bf16[144,128,128]{2,1,0:T(8,128)(2,1)S(1)} %broadcast_select_fusion.blocks, bf16[4,384,256]{2,1,0:T(8,128)(2,1)S(1)} %all_gather.14.g0, ...), custom_call_target="tpu_custom_call" | custom-call | tf_op jit(solution)/shard_map/forward_sums/pallas_call | solution.py:94
  71.7 5.3 %collective-permute-start.6 = (bf16[1536,256]{1,0:T(8,128)(2,1)S(1)}, bf16[1536,256]{1,0:T(8,128)(2,1)S(1)}, u32[]{:S(2)}, u32[]{:S(2)}) collective-permute-start(bf16[1536,256]{1,0:T(8,128)(2,1)S(1)} %get-tuple-element.21), channel_id=1, source_target_pairs={{0,32},{32,0},{64,96},{96,64},{128,160},{160,128},{192,224},{224,1... | collective-permute-start | bytes 2359304 | tf_op jit(solution)/shard_map/ppermute | solution.py:261
  79.1 20.6 %all_to_all.15.terms = bf16[8,192,256]{2,1,0:T(8,128)(2,1)S(1)} all-to-all(bf16[8,192,256]{2,1,0:T(8,128)(2,1)S(1)} %bitcast.21), channel_id=1, replica_groups={{0,64,128,192,256,320,384,448},{32,96,160,224,288,352,416,480},{1,65,12..., dimensions={0} | all-to-all | bytes 1572864 | tf_op jit(solution)/shard_map/all_to_all | solution.py:263
  100.6 16.6 %all_to_all.16.mine = bf16[8,224,256]{2,1,0:T(8,128)(2,1)S(1)} all-to-all(bf16[8,224,256]{2,1,0:T(8,128)(2,1)S(1)} %get-tuple-element.23), channel_id=1, replica_groups={{0,64,128,192,256,320,384,448},{32,96,160,224,288,352,416,480},{1,65,12..., dimensions={0} | all-to-all | bytes 1835008 | tf_op jit(solution)/shard_map/all_to_all | solution.py:267
  117.2 4.4 %collective-permute-start.7 = (bf16[8,224,256]{2,1,0:T(8,128)(2,1)S(1)}, bf16[8,224,256]{2,1,0:T(8,128)(2,1)S(1)}, u32[]{:S(2)}, u32[]{:S(2)}) collective-permute-start(bf16[8,224,256]{2,1,0:T(8,128)(2,1)S(1)} %all_to_all.16.mine), channel_id=1, source_target_pairs={{0,32},{32,0},{64,96},{96,64},{128,160},{160,128},{192,224},{224,1... | collective-permute-start | bytes 2752520 | tf_op jit(solution)/shard_map/ppermute | solution.py:268
  123.7 3.6 %backward_sums.1 = (bf16[768,256]{1,0:T(8,128)(2,1)S(1)}, bf16[768,256]{1,0:T(8,128)(2,1)S(1)}, bf16[768,256]{1,0:T(8,128)(2,1)S(1)}, bf16[768,256]{1,0:T(8,128)...) custom-call(s32[4]{0:T(128)S(1)} %pad_add_fusion.meta, ...), custom_call_target="tpu_custom_call" | custom-call | tf_op jit(solution)/shard_map/backward_sums/pallas_call | solution.py:179
  129.3 3.4 %collective-permute-start.8 = (bf16[768,256]{1,0:T(8,128)(2,1)S(1)}, bf16[768,256]{1,0:T(8,128)(2,1)S(1)}, u32[]{:S(2)}, u32[]{:S(2)}) collective-permute-start(bf16[768,256]{1,0:T(8,128)(2,1)S(1)} %get-tuple-element.25), channel_id=1, source_target_pairs={{0,1},{1,0},{2,3},{3,2},{4,5},{5,4},{6,7},{7,6},{8,9},{9,8},{10,11... | collective-permute-start | bytes 1179656 | tf_op jit(solution)/shard_map/ppermute | solution.py:222
  134.6 5.6 %collective-permute-done.9 = bf16[784,256]{1,0:T(8,128)(2,1)S(1)} collective-permute-done((bf16[784,256]{1,0:T(8,128)(2,1)S(1)}, bf16[784,256]{1,0:T(8,128)(2,1)S(1)}, u32[]{:S(2)}, u32[]{:S(2)}) %collective-permute-start.9) | collective-permute-done | bytes 401440 | tf_op jit(solution)/shard_map/ppermute | solution.py:222
  142.2 4.6 %collective-permute-start.11 = (bf16[400,256]{1,0:T(8,128)(2,1)S(1)}, bf16[400,256]{1,0:T(8,128)(2,1)S(1)}, u32[]{:S(2)}, u32[]{:S(2)}) collective-permute-start(bf16[400,256]{1,0:T(8,128)(2,1)S(1)} %pad_maximum_fusion.2), channel_id=1, source_target_pairs={{2,0},{3,1},{4,2},{5,3},{6,4},{7,5},{8,6},{9,7},{10,8},{11,9},{12,... | collective-permute-start | bytes 614408 | tf_op jit(solution)/shard_map/ppermute | solution.py:197
  149.8 7.2 %collective-permute-done.13 = bf16[768,256]{1,0:T(8,128)(2,1)S(1)} collective-permute-done((bf16[768,256]{1,0:T(8,128)(2,1)S(1)}, bf16[768,256]{1,0:T(8,128)(2,1)S(1)}, u32[]{:S(2)}, u32[]{:S(2)}) %collective-permute-start.13) | collective-permute-done | bytes 393248 | tf_op jit(solution)/shard_map/ppermute | solution.py:222
  159.2 3.4 %collective-permute-start.12 = (bf16[784,256]{1,0:T(8,128)(2,1)S(1)}, bf16[784,256]{1,0:T(8,128)(2,1)S(1)}, u32[]{:S(2)}, u32[]{:S(2)}) collective-permute-start(bf16[784,256]{1,0:T(8,128)(2,1)S(1)} %get-tuple-element.43), channel_id=1, source_target_pairs={{30,0},{31,1},{0,2},{1,3},{2,4},{3,5},{4,6},{5,7},{6,8},{7,9},{8,1... | collective-permute-start | bytes 1204232 | tf_op jit(solution)/shard_map/ppermute | solution.py:197
  162.5 6.7 %collective-permute-done.14 = bf16[784,256]{1,0:T(8,128)(2,1)S(1)} collective-permute-done((bf16[784,256]{1,0:T(8,128)(2,1)S(1)}, bf16[784,256]{1,0:T(8,128)(2,1)S(1)}, u32[]{:S(2)}, u32[]{:S(2)}) %collective-permute-start.14) | collective-permute-done | bytes 401440 | tf_op jit(solution)/shard_map/ppermute | solution.py:197
  169.2 3.1 %collective-permute-done.12 = bf16[784,256]{1,0:T(8,128)(2,1)S(1)} collective-permute-done((bf16[784,256]{1,0:T(8,128)(2,1)S(1)}, bf16[784,256]{1,0:T(8,128)(2,1)S(1)}, u32[]{:S(2)}, u32[]{:S(2)}) %collective-permute-start.12) | collective-permute-done | bytes 401440 | tf_op jit(solution)/shard_map/ppermute | solution.py:197
  176.3 8.9 %all-to-all-start.2 = ((bf16[32,32,256]{2,1,0:T(8,128)(2,1)}), bf16[32,32,256]{2,1,0:T(8,128)(2,1)S(1)}, u32[]{:S(2)}, u32[]{:S(2)}) async-start(bf16[32,32,256]{2,1,0:T(8,128)(2,1)} %broadcast_in_dim.26), calls=%async_computation.2 | async-start | bytes 1048576 | tf_op jit(solution)/shard_map/all_to_all | solution.py:244
  187.2 12.0 %collective-permute-done.15 = bf16[768,256]{1,0:T(8,128)(2,1)S(1)} collective-permute-done((bf16[768,256]{1,0:T(8,128)(2,1)S(1)}, bf16[768,256]{1,0:T(8,128)(2,1)S(1)}, u32[]{:S(2)}, u32[]{:S(2)}) %collective-permute-start.15) | collective-permute-done | bytes 393248 | tf_op jit(solution)/shard_map/ppermute | solution.py:222
  199.5 6.9 %collective-permute-start.18 = (bf16[192,256]{1,0:T(8,128)(2,1)S(1)}, bf16[192,256]{1,0:T(8,128)(2,1)S(1)}, u32[]{:S(2)}, u32[]{:S(2)}) collective-permute-start(bf16[192,256]{1,0:T(8,128)(2,1)S(1)} %get-tuple-element.40), channel_id=1, source_target_pairs={{8,0},{9,1},{10,2},{11,3},{12,4},{13,5},{14,6},{15,7},{16,8},{17,9... | collective-permute-start | bytes 294920 | tf_op jit(solution)/shard_map/ppermute | solution.py:197
  208.7 12.2 %collective-permute-start.16 = (bf16[192,256]{1,0:T(8,128)(2,1)S(1)}, bf16[192,256]{1,0:T(8,128)(2,1)S(1)}, u32[]{:S(2)}, u32[]{:S(2)}) collective-permute-start(bf16[192,256]{1,0:T(8,128)(2,1)S(1)} %get-tuple-element.42), channel_id=1, source_target_pairs={{16,0},{17,1},{18,2},{19,3},{20,4},{21,5},{22,6},{23,7},{24,8},{25... | collective-permute-start | bytes 294920 | tf_op jit(solution)/shard_map/ppermute | solution.py:197
  221.6 10.5 %collective-permute-done.16 = bf16[192,256]{1,0:T(8,128)(2,1)S(1)} collective-permute-done((bf16[192,256]{1,0:T(8,128)(2,1)S(1)}, bf16[192,256]{1,0:T(8,128)(2,1)S(1)}, u32[]{:S(2)}, u32[]{:S(2)}) %collective-permute-start.16) | collective-permute-done | bytes 98336 | tf_op jit(solution)/shard_map/ppermute | solution.py:197
  (49 shorter events, 40.2 us)
Async XLA Ops:
  36.0 12.9 %collective-permute-start = (bf16[2,384,256]{2,1,0:T(8,128)(2,1)S(1)}, bf16[2,384,256]{2,1,0:T(8,128)(2,1)S(1)}, u32[]{:S(2)}, u32[]{:S(2)}) collective-permute-start(bf16[2,384,256]{2,1,0:T(8,128)(2,1)S(1)} %get-tuple-element.38), channel_id=1, source_target_pairs={{2,0},{3,1},{4,2},{5,3},{6,4},{7,5},{8,6},{9,7},{10,8},{11,9},{12,... | collective-permute-start | bytes 1179656 | tf_op jit(solution)/shard_map/ppermute | solution.py:197
  38.9 14.5 %collective-permute-start.3 = (bf16[2,384,256]{2,1,0:T(8,128)(2,1)S(1)}, bf16[2,384,256]{2,1,0:T(8,128)(2,1)S(1)}, u32[]{:S(2)}, u32[]{:S(2)}) collective-permute-start(bf16[2,384,256]{2,1,0:T(8,128)(2,1)S(1)} %get-tuple-element.37), channel_id=1, source_target_pairs={{30,0},{31,1},{0,2},{1,3},{2,4},{3,5},{4,6},{5,7},{6,8},{7,9},{8,1... | collective-permute-start | bytes 1179656 | tf_op jit(solution)/shard_map/ppermute | solution.py:197
  41.3 16.9 %collective-permute-start.1 = (bf16[2,384,256]{2,1,0:T(8,128)(2,1)S(1)}, bf16[2,384,256]{2,1,0:T(8,128)(2,1)S(1)}, u32[]{:S(2)}, u32[]{:S(2)}) collective-permute-start(bf16[2,384,256]{2,1,0:T(8,128)(2,1)S(1)} %get-tuple-element.37), channel_id=1, source_target_pairs={{2,0},{3,1},{4,2},{5,3},{6,4},{7,5},{8,6},{9,7},{10,8},{11,9},{12,... | collective-permute-start | bytes 1179656 | tf_op jit(solution)/shard_map/ppermute | solution.py:197
  45.5 14.2 %collective-permute-start.5 = (bf16[2,384,256]{2,1,0:T(8,128)(2,1)S(1)}, bf16[2,384,256]{2,1,0:T(8,128)(2,1)S(1)}, u32[]{:S(2)}, u32[]{:S(2)}) collective-permute-start(bf16[2,384,256]{2,1,0:T(8,128)(2,1)S(1)} %get-tuple-element.38), channel_id=1, source_target_pairs={{30,0},{31,1},{0,2},{1,3},{2,4},{3,5},{4,6},{5,7},{6,8},{7,9},{8,1... | collective-permute-start | bytes 1179656 | tf_op jit(solution)/shard_map/ppermute | solution.py:197
  48.9 13.9 %collective-permute-start.2 = (bf16[2,384,256]{2,1,0:T(8,128)(2,1)S(1)}, bf16[2,384,256]{2,1,0:T(8,128)(2,1)S(1)}, u32[]{:S(2)}, u32[]{:S(2)}) collective-permute-start(bf16[2,384,256]{2,1,0:T(8,128)(2,1)S(1)} %collective-permute-done.g1a), channel_id=1, source_target_pairs={{2,0},{3,1},{4,2},{5,3},{6,4},{7,5},{8,6},{9,7},{10,8},{11,9},{12,... | collective-permute-start | bytes 1179656 | tf_op jit(solution)/shard_map/ppermute | solution.py:197
  53.5 14.6 %collective-permute-start.4 = (bf16[2,384,256]{2,1,0:T(8,128)(2,1)S(1)}, bf16[2,384,256]{2,1,0:T(8,128)(2,1)S(1)}, u32[]{:S(2)}, u32[]{:S(2)}) collective-permute-start(bf16[2,384,256]{2,1,0:T(8,128)(2,1)S(1)} %collective-permute-done.3.g3b), channel_id=1, source_target_pairs={{30,0},{31,1},{0,2},{1,3},{2,4},{3,5},{4,6},{5,7},{6,8},{7,9},{8,1... | collective-permute-start | bytes 1179656 | tf_op jit(solution)/shard_map/ppermute | solution.py:197
  58.1 41.6 %copy-start = (bf16[256,256]{1,0:T(8,128)(2,1)S(1)}, bf16[256,256]{1,0:T(8,128)(2,1)}, u32[]{:S(2)}) copy-start(bf16[256,256]{1,0:T(8,128)(2,1)} %weight.1) | copy-start | bytes 393220
  58.2 41.6 %copy-start.1 = (bf16[1,192,256]{2,1,0:T(8,128)(2,1)S(1)}, bf16[1,192,256]{2,1,0:T(8,128)(2,1)}, u32[]{:S(2)}) copy-start(bf16[1,192,256]{2,1,0:T(8,128)(2,1)} %param.11) | copy-start | bytes 294916
  71.7 7.2 %collective-permute-start.6 = (bf16[1536,256]{1,0:T(8,128)(2,1)S(1)}, bf16[1536,256]{1,0:T(8,128)(2,1)S(1)}, u32[]{:S(2)}, u32[]{:S(2)}) collective-permute-start(bf16[1536,256]{1,0:T(8,128)(2,1)S(1)} %get-tuple-element.21), channel_id=1, source_target_pairs={{0,32},{32,0},{64,96},{96,64},{128,160},{160,128},{192,224},{224,1... | collective-permute-start | bytes 2359304 | tf_op jit(solution)/shard_map/ppermute | solution.py:261
  117.2 6.5 %collective-permute-start.7 = (bf16[8,224,256]{2,1,0:T(8,128)(2,1)S(1)}, bf16[8,224,256]{2,1,0:T(8,128)(2,1)S(1)}, u32[]{:S(2)}, u32[]{:S(2)}) collective-permute-start(bf16[8,224,256]{2,1,0:T(8,128)(2,1)S(1)} %all_to_all.16.mine), channel_id=1, source_target_pairs={{0,32},{32,0},{64,96},{96,64},{128,160},{160,128},{192,224},{224,1... | collective-permute-start | bytes 2752520 | tf_op jit(solution)/shard_map/ppermute | solution.py:268
  127.3 12.8 %collective-permute-start.9 = (bf16[784,256]{1,0:T(8,128)(2,1)S(1)}, bf16[784,256]{1,0:T(8,128)(2,1)S(1)}, u32[]{:S(2)}, u32[]{:S(2)}) collective-permute-start(bf16[784,256]{1,0:T(8,128)(2,1)S(1)} %get-tuple-element.27), channel_id=1, source_target_pairs={{0,1},{1,0},{2,3},{3,2},{4,5},{5,4},{6,7},{7,6},{8,9},{9,8},{10,11... | collective-permute-start | bytes 1204232 | tf_op jit(solution)/shard_map/ppermute | solution.py:222
  129.3 19.3 %collective-permute-start.8 = (bf16[768,256]{1,0:T(8,128)(2,1)S(1)}, bf16[768,256]{1,0:T(8,128)(2,1)S(1)}, u32[]{:S(2)}, u32[]{:S(2)}) collective-permute-start(bf16[768,256]{1,0:T(8,128)(2,1)S(1)} %get-tuple-element.25), channel_id=1, source_target_pairs={{0,1},{1,0},{2,3},{3,2},{4,5},{5,4},{6,7},{7,6},{8,9},{9,8},{10,11... | collective-permute-start | bytes 1179656 | tf_op jit(solution)/shard_map/ppermute | solution.py:222
  132.6 24.4 %collective-permute-start.13 = (bf16[768,256]{1,0:T(8,128)(2,1)S(1)}, bf16[768,256]{1,0:T(8,128)(2,1)S(1)}, u32[]{:S(2)}, u32[]{:S(2)}) collective-permute-start(bf16[768,256]{1,0:T(8,128)(2,1)S(1)} %get-tuple-element.30), channel_id=1, source_target_pairs={{0,1},{1,0},{2,3},{3,2},{4,5},{5,4},{6,7},{7,6},{8,9},{9,8},{10,11... | collective-permute-start | bytes 1179656 | tf_op jit(solution)/shard_map/ppermute | solution.py:222
  140.3 8.4 %collective-permute-start.10 = (bf16[384,256]{1,0:T(8,128)(2,1)S(1)}, bf16[384,256]{1,0:T(8,128)(2,1)S(1)}, u32[]{:S(2)}, u32[]{:S(2)}) collective-permute-start(bf16[384,256]{1,0:T(8,128)(2,1)S(1)} %get-tuple-element.35), channel_id=1, source_target_pairs={{30,0},{31,1},{0,2},{1,3},{2,4},{3,5},{4,6},{5,7},{6,8},{7,9},{8,1... | collective-permute-start | bytes 589832 | tf_op jit(solution)/shard_map/ppermute | solution.py:197
  142.2 7.5 %collective-permute-start.11 = (bf16[400,256]{1,0:T(8,128)(2,1)S(1)}, bf16[400,256]{1,0:T(8,128)(2,1)S(1)}, u32[]{:S(2)}, u32[]{:S(2)}) collective-permute-start(bf16[400,256]{1,0:T(8,128)(2,1)S(1)} %pad_maximum_fusion.2), channel_id=1, source_target_pairs={{2,0},{3,1},{4,2},{5,3},{6,4},{7,5},{8,6},{9,7},{10,8},{11,9},{12,... | collective-permute-start | bytes 614408 | tf_op jit(solution)/shard_map/ppermute | solution.py:197
  157.2 12.0 %collective-permute-start.14 = (bf16[784,256]{1,0:T(8,128)(2,1)S(1)}, bf16[784,256]{1,0:T(8,128)(2,1)S(1)}, u32[]{:S(2)}, u32[]{:S(2)}) collective-permute-start(bf16[784,256]{1,0:T(8,128)(2,1)S(1)} %get-tuple-element.44), channel_id=1, source_target_pairs={{2,0},{3,1},{4,2},{5,3},{6,4},{7,5},{8,6},{9,7},{10,8},{11,9},{12,... | collective-permute-start | bytes 1204232 | tf_op jit(solution)/shard_map/ppermute | solution.py:197
  159.2 13.2 %collective-permute-start.12 = (bf16[784,256]{1,0:T(8,128)(2,1)S(1)}, bf16[784,256]{1,0:T(8,128)(2,1)S(1)}, u32[]{:S(2)}, u32[]{:S(2)}) collective-permute-start(bf16[784,256]{1,0:T(8,128)(2,1)S(1)} %get-tuple-element.43), channel_id=1, source_target_pairs={{30,0},{31,1},{0,2},{1,3},{2,4},{3,5},{4,6},{5,7},{6,8},{7,9},{8,1... | collective-permute-start | bytes 1204232 | tf_op jit(solution)/shard_map/ppermute | solution.py:197
  176.3 44.5 %all-to-all-start.2 = ((bf16[32,32,256]{2,1,0:T(8,128)(2,1)}), bf16[32,32,256]{2,1,0:T(8,128)(2,1)S(1)}, u32[]{:S(2)}, u32[]{:S(2)}) async-start(bf16[32,32,256]{2,1,0:T(8,128)(2,1)} %broadcast_in_dim.26), calls=%async_computation.2 | async-start | bytes 1048576 | tf_op jit(solution)/shard_map/all_to_all | solution.py:244
  185.3 13.9 %collective-permute-start.15 = (bf16[768,256]{1,0:T(8,128)(2,1)S(1)}, bf16[768,256]{1,0:T(8,128)(2,1)S(1)}, u32[]{:S(2)}, u32[]{:S(2)}) collective-permute-start(bf16[768,256]{1,0:T(8,128)(2,1)S(1)} %get-tuple-element.32), channel_id=1, source_target_pairs={{0,1},{1,0},{2,3},{3,2},{4,5},{5,4},{6,7},{7,6},{8,9},{9,8},{10,11... | collective-permute-start | bytes 1179656 | tf_op jit(solution)/shard_map/ppermute | solution.py:222
  199.5 22.2 %collective-permute-start.18 = (bf16[192,256]{1,0:T(8,128)(2,1)S(1)}, bf16[192,256]{1,0:T(8,128)(2,1)S(1)}, u32[]{:S(2)}, u32[]{:S(2)}) collective-permute-start(bf16[192,256]{1,0:T(8,128)(2,1)S(1)} %get-tuple-element.40), channel_id=1, source_target_pairs={{8,0},{9,1},{10,2},{11,3},{12,4},{13,5},{14,6},{15,7},{16,8},{17,9... | collective-permute-start | bytes 294920 | tf_op jit(solution)/shard_map/ppermute | solution.py:197
  206.4 15.2 %collective-permute-start.17 = (bf16[192,256]{1,0:T(8,128)(2,1)S(1)}, bf16[192,256]{1,0:T(8,128)(2,1)S(1)}, u32[]{:S(2)}, u32[]{:S(2)}) collective-permute-start(bf16[192,256]{1,0:T(8,128)(2,1)S(1)} %get-tuple-element.41), channel_id=1, source_target_pairs={{24,0},{25,1},{26,2},{27,3},{28,4},{29,5},{30,6},{31,7},{0,8},{1,9... | collective-permute-start | bytes 294920 | tf_op jit(solution)/shard_map/ppermute | solution.py:197
  208.7 23.4 %collective-permute-start.16 = (bf16[192,256]{1,0:T(8,128)(2,1)S(1)}, bf16[192,256]{1,0:T(8,128)(2,1)S(1)}, u32[]{:S(2)}, u32[]{:S(2)}) collective-permute-start(bf16[192,256]{1,0:T(8,128)(2,1)S(1)} %get-tuple-element.42), channel_id=1, source_target_pairs={{16,0},{17,1},{18,2},{19,3},{20,4},{21,5},{22,6},{23,7},{24,8},{25... | collective-permute-start | bytes 294920 | tf_op jit(solution)/shard_map/ppermute | solution.py:197

commit v5 on v4

--- a/solution.py
+++ b/solution.py
@@ -22,13 +22,6 @@
 Y_SWAP = [(d, d ^ 1) for d in range(NZ * NY)]
 CHIPS = N_SRC // 2
 CORE_GROUPS = [[2 * chip + core for chip in range(CHIPS)] for core in range(2)]
-CHIP_PAIRS = [[2 * chip, 2 * chip + 1] for chip in range(CHIPS)]
-PEER_GROUPS = [
-    [(2 * chip + core) * NZ * NY + (q + 4 * m) * NY + y for m in range(4) for chip in range(CHIPS)]
-    for core in range(2)
-    for q in range(4)
-    for y in range(NY)
-]
 CORE_SWAP = [(s, s ^ 1) for s in range(N_SRC)]
 
 
@@ -136,8 +129,9 @@
     )(terms, weight, cotangent)
 
 
-def backward_kernel(meta, coords, blocks, mine, theirs, *refs):
-    kept, sent, (wsum, rows, total) = refs[:4], refs[4:8], refs[8:]
+def backward_kernel(
+    meta, coords, blocks, mine, theirs, kept0, kept1, kept2, kept3, sent0, sent13, sent2, wsum, rows, total
+):
     slot_count, z, y, core = meta[0], meta[1], meta[2], meta[3]
     slots = blocks.shape[0]
 
@@ -158,15 +152,19 @@
             tail = pl.ds(pl.multiple_of(ROWS + core * share, share), share)
             summed = summed + ref[chip, tail, :].astype(F32)
     wsum[...] = summed
-    sent[2][4 * ROWS :, :] = summed.astype(BF16)
+    sent2[4 * ROWS :, :] = summed.astype(BF16)
     total[...] = jnp.zeros_like(total)
     each_slot(slot_count, one_slot)
-    for refs, side in ((sent, 1 - y), (kept, y)):
-        for offset, ref in zip((0, 1, 6, 15), refs):
-            for member in range(4):
-                place = lax.rem(z + offset + 4 * member, NZ) * PAIR + side * ROWS
-                chunk = total[pl.ds(pl.multiple_of(place, ROWS), ROWS), :]
-                ref[member * ROWS : (member + 1) * ROWS, :] = chunk.astype(BF16)
+    mirror = 1 - y
+    lists = (
+        (sent2, 0, 6, mirror), (sent13, 0, 1, mirror), (sent13, 4, 15, mirror), (sent0, 0, 0, mirror),
+        (kept0, 0, 0, y), (kept1, 0, 1, y), (kept2, 0, 6, y), (kept3, 0, 15, y),
+    )
+    for ref, first, offset, side in lists:
+        for member in range(4):
+            place = lax.rem(z + offset + 4 * member, NZ) * PAIR + side * ROWS
+            chunk = total[pl.ds(pl.multiple_of(place, ROWS), ROWS), :]
+            ref[(first + member) * ROWS : (first + member + 1) * ROWS, :] = chunk.astype(BF16)
 
 
 def backward_sums(meta, coords, values, mine, theirs):
@@ -175,22 +173,22 @@
     source_rows = NZ * PAIR
     smem = pl.BlockSpec(memory_space=pltpu.SMEM)
     vmem = pl.BlockSpec(memory_space=pltpu.VMEM)
-    half = jax.ShapeDtypeStruct((4 * ROWS, WIDTH), BF16)
+
+    def rows_of(count):
+        return jax.ShapeDtypeStruct((count, WIDTH), BF16)
+
+    list_rows = 4 * ROWS
     out = pl.pallas_call(
         backward_kernel,
-        out_shape=(half,) * 6
-        + (
-            jax.ShapeDtypeStruct((4 * ROWS + share, WIDTH), BF16),
-            half,
-            jax.ShapeDtypeStruct((share, WIDTH), F32),
-        ),
+        out_shape=(rows_of(list_rows),) * 5
+        + (rows_of(2 * list_rows), rows_of(list_rows + share), jax.ShapeDtypeStruct((share, WIDTH), F32)),
         in_specs=[smem, smem, vmem, vmem, vmem],
-        out_specs=(vmem,) * 9,
+        out_specs=(vmem,) * 8,
         scratch_shapes=[pltpu.VMEM((dest_rows, WIDTH), BF16), pltpu.VMEM((source_rows, WIDTH), F32)],
         compiler_params=pltpu.CompilerParams(vmem_limit_bytes=VMEM_LIMIT),
         name="backward_sums",
     )(meta, coords, values, mine, theirs)
-    return out[:4], out[4:8], out[8]
+    return (out[:4],) + tuple(out[4:])
 
 
 def shift(array, step):
@@ -215,34 +213,49 @@
     return sum(term.astype(F32) for term in terms)
 
 
-def scatter_sources(kept, sent, weight_part):
+def total_f32(*terms):
+    return sum(term.astype(F32) for term in terms)
+
+
+def pair_swap(array, axis, groups, side):
+    both = lax.all_gather(array, axis, axis=0, axis_index_groups=groups)
+    return lax.dynamic_index_in_dim(both, 1 - side, 0, keepdims=False)
+
+
+def scatter_sources(kept, sent0, sent13, sent2, w, y):
     half, full = 2 * ROWS, 4 * ROWS
-    swapped = [None] * 4
-    for which in (2, 1, 3, 0):
-        swapped[which] = lax.ppermute(sent[which], "dst", Y_SWAP)
-    w = total_f32(weight_part, swapped[2][full:])
-    low = shift(total_of(kept[2][:half], swapped[2][:half]), -1)
-    high = jnp.concatenate([total_of(kept[2][half:], swapped[2][half:full]), w.astype(BF16)], 0)
+    swap2 = pair_swap(sent2, "dst", Y_GROUPS, y)
+    swap13 = lax.ppermute(sent13, "dst", Y_SWAP)
+    w = total_f32(w, swap2[full:])
+    low = shift(total_of(kept[2][:half], swap2[:half]), -1)
+    high = jnp.concatenate([total_of(kept[2][half:], swap2[half:full]), w.astype(BF16)], 0)
     high = shift(high, 1)
+    sent0, low = lax.optimization_barrier((sent0, low))
+    swap0 = lax.ppermute(sent0, "dst", Y_SWAP)
     w = total_of(w, high[half:])
     none = jnp.zeros_like(low[:ROWS])
-    up = total_of(kept[1], swapped[1], jnp.concatenate([none, low, none], 0))
-    down = total_of(kept[3], swapped[3], jnp.concatenate([high[:half], none, none], 0))
+    up = total_of(kept[1], swap13[:full], jnp.concatenate([none, low, none], 0))
+    down = total_of(kept[3], swap13[full:], jnp.concatenate([high[:half], none, none], 0))
     up = shift(jnp.concatenate([up, w], 0), -1)
     down = shift(jnp.concatenate([down, w], 0), 1)
     w = total_of(up[full:], down[full:])
-    near = total_of(kept[0], swapped[0], up[:full], down[:full]).reshape(4, ROWS, WIDTH)
-    far, left, right = shift(near[2], -8), shift(near[1], -4), shift(near[3], 4)
-    weight_grad, mine = lax.optimization_barrier((gather_weight(w), near[0]))
-    return total_of(mine, far, left, right), weight_grad
+    near = total_of(kept[0], swap0, up[:full], down[:full]).reshape(4, ROWS, WIDTH)
+
+    part = ROWS // 2
+    from_left = shift(jnp.concatenate([near[2, :part], w], 0), -4)
+    from_right = shift(jnp.concatenate([near[2, part:], w], 0), 4)
+    w_left, w_right = from_left[part:], from_right[part:]
+    none = jnp.zeros((part, WIDTH), BF16)
+    left = shift(total_of(near[1], jnp.concatenate([from_left[:part], none], 0)), -4)
+    right = total_of(near[3], jnp.concatenate([none, from_right[:part]], 0))
+    right = shift(jnp.concatenate([right, w_right], 0), 4)
+    w = total_of(w, w_left, w_right, right[ROWS:])
+    return total_of(near[0], left, right[:ROWS]), w
 
 
 def gather_weight(part):
-    share = part.shape[0]
-    pair = lax.all_gather(part, "src", axis=0, tiled=True, axis_index_groups=CHIP_PAIRS)
-    copies = jnp.broadcast_to(pair, (4 * CHIPS,) + pair.shape)
-    pieces = lax.all_to_all(copies, ("src", "dst"), 0, 0, tiled=True, axis_index_groups=PEER_GROUPS)
-    return jnp.sum(pieces.astype(F32).reshape(4, CHIPS * 2 * share, WIDTH), axis=0)
+    copies = jnp.broadcast_to(part, (N_SRC,) + part.shape)
+    return lax.all_to_all(copies, "src", 0, 0, tiled=True).reshape(WIDTH, WIDTH).astype(F32)
 
 
 def shards(features, weight, values, coords, counts, cotangent):
@@ -266,8 +279,9 @@
     activations, message = middle(terms, weight, cotangent[0])
     mine = lax.all_to_all(message, "src", 0, 0, tiled=True, axis_index_groups=CORE_GROUPS)
     theirs = lax.ppermute(mine, "src", CORE_SWAP)
-    kept, sent, weight_part = backward_sums(meta, pairs, blocks, mine, theirs)
-    input_grad, weight_grad = scatter_sources(kept, sent, weight_part)
+    sums = backward_sums(meta, pairs, blocks, mine, theirs)
+    input_grad, weight_part = scatter_sources(*sums, y)
+    weight_grad = gather_weight(weight_part)
     return (activations[None], input_grad, weight_grad)
 
 

time: 235 us -> 226 us (0.962)
  waiting for transfers between devices: 61.8 us -> 47.7 us
  blocking collectives: 75.7 us -> 86 us
  starting transfers between devices: 78.8 us -> 72.5 us
    ppermute x4 -> x2, waiting for transfers between devices: 26.6 us -> 15.1 us  [the longest x1 7.83 us: scatter_sources(): swap0 = lax.ppermute(sent0, 'dst', Y_SWAP)]
    ppermute x13 -> x14, waiting for transfers between devices: 31.2 us -> 21.6 us  [shift(): return lax.ppermute(array, 'dst', from_z(step))]
    all_gather x1, blocking collectives: 3.12 us -> 11.5 us  [pair_swap(): both = lax.all_gather(array, axis, axis=0, axis_index_groups=groups)]
    all_to_all x1, waiting for transfers between devices: 0.01 us -> 6.97 us  [gather_weight(): lax.all_to_all(copies, 'src', 0, 0, tiled=True).reshape(WIDTH, WIDTH)]
    ppermute x4 -> x2, starting transfers between devices: 9.12 us -> 4.43 us  [the longest x1 2.34 us: scatter_sources(): swap0 = lax.ppermute(sent0, 'dst', Y_SWAP)]
    ppermute x13 -> x14, starting transfers between devices: 51 us -> 46.8 us  [shift(): return lax.ppermute(array, 'dst', from_z(step))]
    all_to_all x1, starting transfers between devices: 8.95 us -> 11.4 us  [gather_weight(): lax.all_to_all(copies, 'src', 0, 0, tiled=True).reshape(WIDTH, WIDTH)]
  transfers between devices with their start and end apart: 20 -> 19, of which waited for: 13 -> 12; matrix products, arithmetic and copies ran while one was open for 2% -> 2% of each run, Pallas kernels for 0% -> 0%
where the time goes in v5:
time: 226 us; the launch traced here: 225 us
  blocking collectives  86 us (38%)
  starting transfers between devices  72.5 us (32%)
  waiting for transfers between devices  47.7 us (21%)
  Pallas kernels  7.84 us (3%)
  other arithmetic  5.19 us (2%)
  local copies, waits for them, and re-layouts  3.88 us (2%)
    ppermute x14, starting transfers between devices, shift(): return lax.ppermute(array, 'dst', from_z(step))  46.8 us
    all_gather x1, blocking collectives, gather_sources(): lax.all_gather(features, 'dst', axis=0, axis_index_groups=STRIDE_GROUPS)  28 us
    all_to_all x1, blocking collectives, shards(): lax.all_to_all(chip_sums.reshape(CHIPS, ROWS, WIDTH), 'src', 0, 0, tiled=...  22.5 us
    ppermute x14, waiting for transfers between devices, shift(): return lax.ppermute(array, 'dst', from_z(step))  21.6 us
    all_to_all x1, blocking collectives, shards(): lax.all_to_all(message, 'src', 0, 0, tiled=True, axis_index_groups=CORE_G...  16.6 us
    all_gather x1, blocking collectives, pair_swap(): both = lax.all_gather(array, axis, axis=0, axis_index_groups=groups)  11.5 us
    all_to_all x1, starting transfers between devices, gather_weight(): lax.all_to_all(copies, 'src', 0, 0, tiled=True).reshape(WIDTH, WIDTH)  11.4 us
    ppermute x1, waiting for transfers between devices, scatter_sources(): swap0 = lax.ppermute(sent0, 'dst', Y_SWAP)  7.83 us
  transfers between devices with their start and end apart: 19, of which 12 were waited for; matrix products, arithmetic and copies ran while one was open for 2% of the time, Pallas kernels for 0%

profile of v5, /device:TPU:1, one launch (start us, length us, event | category | flops | bytes accessed | tf_op | source)
XLA Modules:
  0.0 224.6 jit_solution(4223271985552440842)
XLA Ops:
  0.6 28.0 %all-gather = bf16[768,256]{1,0:T(8,128)(2,1)S(1)} all-gather(bf16[192,256]{1,0:T(8,128)(2,1)} %param.6), channel_id=2, replica_groups={{0,8,16,24},{1,9,17,25},{2,10,18,26},{3,11,19,27},{4,12,20,28},{5,13,21..., dimensions={0}, use_global_device_ids=true | all-gather | bytes 491520 | tf_op jit(solution)/shard_map/all_gather | solution.py:199
  28.6 7.3 %all_gather.17.g0 = bf16[4,384,256]{2,1,0:T(8,128)(2,1)S(1)} all-gather(bf16[4,192,256]{2,1,0:T(8,128)(2,1)S(1)} %bitcast.47), channel_id=1, replica_groups={{0,1},{2,3},{4,5},{6,7},{8,9},{10,11},{12,13},{14,15},{16,17},{18,19},{..., dimensions={1}, use_global_device_ids=true | all-gather | bytes 1179648 | tf_op jit(solution)/shard_map/all_gather | solution.py:200
  41.3 4.2 %collective-permute-start.1 = (bf16[2,384,256]{2,1,0:T(8,128)(2,1)S(1)}, bf16[2,384,256]{2,1,0:T(8,128)(2,1)S(1)}, u32[]{:S(2)}, u32[]{:S(2)}) collective-permute-start(bf16[2,384,256]{2,1,0:T(8,128)(2,1)S(1)} %get-tuple-element.37), channel_id=1, source_target_pairs={{2,0},{3,1},{4,2},{5,3},{6,4},{7,5},{8,6},{9,7},{10,8},{11,9},{12,... | collective-permute-start | bytes 1179656 | tf_op jit(solution)/shard_map/ppermute | solution.py:195
  48.9 4.6 %collective-permute-start.2 = (bf16[2,384,256]{2,1,0:T(8,128)(2,1)S(1)}, bf16[2,384,256]{2,1,0:T(8,128)(2,1)S(1)}, u32[]{:S(2)}, u32[]{:S(2)}) collective-permute-start(bf16[2,384,256]{2,1,0:T(8,128)(2,1)S(1)} %collective-permute-done.g1a), channel_id=1, source_target_pairs={{2,0},{3,1},{4,2},{5,3},{6,4},{7,5},{8,6},{9,7},{10,8},{11,9},{12,... | collective-permute-start | bytes 1179656 | tf_op jit(solution)/shard_map/ppermute | solution.py:195
  59.7 3.1 %collective-permute-done.2.g2a = bf16[2,384,256]{2,1,0:T(8,128)(2,1)S(1)} collective-permute-done((bf16[2,384,256]{2,1,0:T(8,128)(2,1)S(1)}, bf16[2,384,256]{2,1,0:T(8,128)(2,1)S(1)}, u32[]{:S(2)}, u32[]{:S(2)}) %collective-permute-start.2) | collective-permute-done | bytes 393248 | tf_op jit(solution)/shard_map/ppermute | solution.py:195
  62.8 5.3 %collective-permute-done.4.g2b = bf16[2,384,256]{2,1,0:T(8,128)(2,1)S(1)} collective-permute-done((bf16[2,384,256]{2,1,0:T(8,128)(2,1)S(1)}, bf16[2,384,256]{2,1,0:T(8,128)(2,1)S(1)}, u32[]{:S(2)}, u32[]{:S(2)}) %collective-permute-start.4) | collective-permute-done | bytes 393248 | tf_op jit(solution)/shard_map/ppermute | solution.py:195
  68.1 3.4 %forward_sums.1 = (bf16[1536,256]{1,0:T(8,128)(2,1)S(1)}, bf16[1536,256]{1,0:T(8,128)(2,1)S(1)}) custom-call(s32[4]{0:T(128)S(1)} %pad_add_fusion.meta, s32[288]{0:T(512)S(1)} %reshape.37.coords, bf16[144,128,128]{2,1,0:T(8,128)(2,1)S(1)} %broadcast_select_fusion.blocks, bf16[4,384,256]{2,1,0:T(8,128)(2,1)S(1)} %all_gather.17.g0, ...), custom_call_target="tpu_custom_call" | custom-call | tf_op jit(solution)/shard_map/forward_sums/pallas_call | solution.py:87
  71.5 5.4 %collective-permute-start.6 = (bf16[1536,256]{1,0:T(8,128)(2,1)S(1)}, bf16[1536,256]{1,0:T(8,128)(2,1)S(1)}, u32[]{:S(2)}, u32[]{:S(2)}) collective-permute-start(bf16[1536,256]{1,0:T(8,128)(2,1)S(1)} %get-tuple-element.20), channel_id=1, source_target_pairs={{0,32},{32,0},{64,96},{96,64},{128,160},{160,128},{192,224},{224,1... | collective-permute-start | bytes 2359304 | tf_op jit(solution)/shard_map/ppermute | solution.py:274
  79.0 22.5 %all_to_all.15.terms = bf16[8,192,256]{2,1,0:T(8,128)(2,1)S(1)} all-to-all(bf16[8,192,256]{2,1,0:T(8,128)(2,1)S(1)} %bitcast.43), channel_id=1, replica_groups={{0,64,128,192,256,320,384,448},{32,96,160,224,288,352,416,480},{1,65,12..., dimensions={0} | all-to-all | bytes 1572864 | tf_op jit(solution)/shard_map/all_to_all | solution.py:276
  102.4 16.6 %all_to_all.16.mine = bf16[8,224,256]{2,1,0:T(8,128)(2,1)S(1)} all-to-all(bf16[8,224,256]{2,1,0:T(8,128)(2,1)S(1)} %get-tuple-element.22), channel_id=1, replica_groups={{0,64,128,192,256,320,384,448},{32,96,160,224,288,352,416,480},{1,65,12..., dimensions={0} | all-to-all | bytes 1835008 | tf_op jit(solution)/shard_map/all_to_all | solution.py:280
  119.0 4.4 %collective-permute-start.7 = (bf16[8,224,256]{2,1,0:T(8,128)(2,1)S(1)}, bf16[8,224,256]{2,1,0:T(8,128)(2,1)S(1)}, u32[]{:S(2)}, u32[]{:S(2)}) collective-permute-start(bf16[8,224,256]{2,1,0:T(8,128)(2,1)S(1)} %all_to_all.16.mine), channel_id=1, source_target_pairs={{0,32},{32,0},{64,96},{96,64},{128,160},{160,128},{192,224},{224,1... | collective-permute-start | bytes 2752520 | tf_op jit(solution)/shard_map/ppermute | solution.py:281
  127.9 3.5 %backward_sums.1 = (bf16[768,256]{1,0:T(8,128)(2,1)S(1)}, bf16[768,256]{1,0:T(8,128)(2,1)S(1)}, bf16[768,256]{1,0:T(8,128)(2,1)S(1)}, bf16[768,256]{1,0:T(8,128)...) custom-call(s32[4]{0:T(128)S(1)} %pad_add_fusion.meta, ...), custom_call_target="tpu_custom_call" | custom-call | tf_op jit(solution)/shard_map/backward_sums/pallas_call | solution.py:181
  131.4 11.5 %all-gather.1 = bf16[1568,256]{1,0:T(8,128)(2,1)S(1)} all-gather(bf16[784,256]{1,0:T(8,128)(2,1)S(1)} %get-tuple-element.26), channel_id=3, replica_groups={{0,1},{2,3},{4,5},{6,7},{8,9},{10,11},{12,13},{14,15},{16,17},{18,19},{..., dimensions={0}, use_global_device_ids=true | all-gather | bytes 1204224 | tf_op jit(solution)/shard_map/all_gather | solution.py:221
  147.1 3.4 %collective-permute-start.8 = (bf16[384,256]{1,0:T(8,128)(2,1)S(1)}, bf16[384,256]{1,0:T(8,128)(2,1)S(1)}, u32[]{:S(2)}, u32[]{:S(2)}) collective-permute-start(bf16[384,256]{1,0:T(8,128)(2,1)S(1)} %get-tuple-element.34), channel_id=1, source_target_pairs={{30,0},{31,1},{0,2},{1,3},{2,4},{3,5},{4,6},{5,7},{6,8},{7,9},{8,1... | collective-permute-start | bytes 589832 | tf_op jit(solution)/shard_map/ppermute | solution.py:195
  150.5 5.2 %collective-permute-done.8 = bf16[384,256]{1,0:T(8,128)(2,1)S(1)} collective-permute-done((bf16[384,256]{1,0:T(8,128)(2,1)S(1)}, bf16[384,256]{1,0:T(8,128)(2,1)S(1)}, u32[]{:S(2)}, u32[]{:S(2)}) %collective-permute-start.8) | collective-permute-done | bytes 196640 | tf_op jit(solution)/shard_map/ppermute | solution.py:195
  155.8 7.3 %collective-permute-done.10 = bf16[1536,256]{1,0:T(8,128)(2,1)S(1)} collective-permute-done((bf16[1536,256]{1,0:T(8,128)(2,1)S(1)}, bf16[1536,256]{1,0:T(8,128)(2,1)S(1)}, u32[]{:S(2)}, u32[]{:S(2)}) %collective-permute-start.10) | collective-permute-done | bytes 786464 | tf_op jit(solution)/shard_map/ppermute | solution.py:228
  165.3 3.4 %collective-permute-start.12 = (bf16[784,256]{1,0:T(8,128)(2,1)S(1)}, bf16[784,256]{1,0:T(8,128)(2,1)S(1)}, u32[]{:S(2)}, u32[]{:S(2)}) collective-permute-start(bf16[784,256]{1,0:T(8,128)(2,1)S(1)} %get-tuple-element.45), channel_id=1, source_target_pairs={{30,0},{31,1},{0,2},{1,3},{2,4},{3,5},{4,6},{5,7},{6,8},{7,9},{8,1... | collective-permute-start | bytes 1204232 | tf_op jit(solution)/shard_map/ppermute | solution.py:195
  171.0 7.8 %collective-permute-done.9 = bf16[768,256]{1,0:T(8,128)(2,1)S(1)} collective-permute-done((bf16[768,256]{1,0:T(8,128)(2,1)S(1)}, bf16[768,256]{1,0:T(8,128)(2,1)S(1)}, u32[]{:S(2)}, u32[]{:S(2)}) %collective-permute-start.9) | collective-permute-done | bytes 393248 | tf_op jit(solution)/shard_map/ppermute | solution.py:234
  179.1 5.2 %collective-permute-start.16 = (bf16[112,256]{1,0:T(8,128)(2,1)S(1)}, bf16[112,256]{1,0:T(8,128)(2,1)S(1)}, u32[]{:S(2)}, u32[]{:S(2)}) collective-permute-start(bf16[112,256]{1,0:T(8,128)(2,1)S(1)} %get-tuple-element.43), channel_id=1, source_target_pairs={{8,0},{9,1},{10,2},{11,3},{12,4},{13,5},{14,6},{15,7},{16,8},{17,9... | collective-permute-start | bytes 172040 | tf_op jit(solution)/shard_map/ppermute | solution.py:195
  184.4 4.0 %collective-permute-start.14 = (bf16[112,256]{1,0:T(8,128)(2,1)S(1)}, bf16[112,256]{1,0:T(8,128)(2,1)S(1)}, u32[]{:S(2)}, u32[]{:S(2)}) collective-permute-start(bf16[112,256]{1,0:T(8,128)(2,1)S(1)} %get-tuple-element.44), channel_id=1, source_target_pairs={{24,0},{25,1},{26,2},{27,3},{28,4},{29,5},{30,6},{31,7},{0,8},{1,9... | collective-permute-start | bytes 172040 | tf_op jit(solution)/shard_map/ppermute | solution.py:195
  188.8 4.4 %collective-permute-done.14 = bf16[112,256]{1,0:T(8,128)(2,1)S(1)} collective-permute-done((bf16[112,256]{1,0:T(8,128)(2,1)S(1)}, bf16[112,256]{1,0:T(8,128)(2,1)S(1)}, u32[]{:S(2)}, u32[]{:S(2)}) %collective-permute-start.14) | collective-permute-done | bytes 57376 | tf_op jit(solution)/shard_map/ppermute | solution.py:195
  193.2 6.6 %collective-permute-start.17 = (bf16[208,256]{1,0:T(8,128)(2,1)S(1)}, bf16[208,256]{1,0:T(8,128)(2,1)S(1)}, u32[]{:S(2)}, u32[]{:S(2)}) collective-permute-start(bf16[208,256]{1,0:T(8,128)(2,1)S(1)} %pad_maximum_fusion.3), channel_id=1, source_target_pairs={{8,0},{9,1},{10,2},{11,3},{12,4},{13,5},{14,6},{15,7},{16,8},{17,9... | collective-permute-start | bytes 319496 | tf_op jit(solution)/shard_map/ppermute | solution.py:195
  204.8 11.4 %all-to-all-start.2 = ((bf16[16,16,256]{2,1,0:T(8,128)(2,1)}), bf16[16,16,256]{2,1,0:T(8,128)(2,1)S(1)}, u32[]{:S(2)}, u32[]{:S(2)}) async-start(bf16[16,16,256]{2,1,0:T(8,128)(2,1)} %broadcast_in_dim.27), calls=%async_computation.2 | async-start | bytes 262144 | tf_op jit(solution)/shard_map/all_to_all | solution.py:258
  216.9 7.0 %all-to-all-done.2 = bf16[16,16,256]{2,1,0:T(8,128)(2,1)S(1)} async-done(((bf16[16,16,256]{2,1,0:T(8,128)(2,1)}), bf16[16,16,256]{2,1,0:T(8,128)(2,1)S(1)}, u32[]{:S(2)}, u32[]{:S(2)}) %all-to-all-start.2) | async-done | bytes 131104 | tf_op jit(solution)/shard_map/all_to_all | solution.py:258
  (57 shorter events, 37.5 us)
Async XLA Ops:
  36.0 12.9 %collective-permute-start = (bf16[2,384,256]{2,1,0:T(8,128)(2,1)S(1)}, bf16[2,384,256]{2,1,0:T(8,128)(2,1)S(1)}, u32[]{:S(2)}, u32[]{:S(2)}) collective-permute-start(bf16[2,384,256]{2,1,0:T(8,128)(2,1)S(1)} %get-tuple-element.38), channel_id=1, source_target_pairs={{2,0},{3,1},{4,2},{5,3},{6,4},{7,5},{8,6},{9,7},{10,8},{11,9},{12,... | collective-permute-start | bytes 1179656 | tf_op jit(solution)/shard_map/ppermute | solution.py:195
  38.9 14.5 %collective-permute-start.3 = (bf16[2,384,256]{2,1,0:T(8,128)(2,1)S(1)}, bf16[2,384,256]{2,1,0:T(8,128)(2,1)S(1)}, u32[]{:S(2)}, u32[]{:S(2)}) collective-permute-start(bf16[2,384,256]{2,1,0:T(8,128)(2,1)S(1)} %get-tuple-element.37), channel_id=1, source_target_pairs={{30,0},{31,1},{0,2},{1,3},{2,4},{3,5},{4,6},{5,7},{6,8},{7,9},{8,1... | collective-permute-start | bytes 1179656 | tf_op jit(solution)/shard_map/ppermute | solution.py:195
  41.3 16.9 %collective-permute-start.1 = (bf16[2,384,256]{2,1,0:T(8,128)(2,1)S(1)}, bf16[2,384,256]{2,1,0:T(8,128)(2,1)S(1)}, u32[]{:S(2)}, u32[]{:S(2)}) collective-permute-start(bf16[2,384,256]{2,1,0:T(8,128)(2,1)S(1)} %get-tuple-element.37), channel_id=1, source_target_pairs={{2,0},{3,1},{4,2},{5,3},{6,4},{7,5},{8,6},{9,7},{10,8},{11,9},{12,... | collective-permute-start | bytes 1179656 | tf_op jit(solution)/shard_map/ppermute | solution.py:195
  45.5 14.2 %collective-permute-start.5 = (bf16[2,384,256]{2,1,0:T(8,128)(2,1)S(1)}, bf16[2,384,256]{2,1,0:T(8,128)(2,1)S(1)}, u32[]{:S(2)}, u32[]{:S(2)}) collective-permute-start(bf16[2,384,256]{2,1,0:T(8,128)(2,1)S(1)} %get-tuple-element.38), channel_id=1, source_target_pairs={{30,0},{31,1},{0,2},{1,3},{2,4},{3,5},{4,6},{5,7},{6,8},{7,9},{8,1... | collective-permute-start | bytes 1179656 | tf_op jit(solution)/shard_map/ppermute | solution.py:195
  48.9 13.9 %collective-permute-start.2 = (bf16[2,384,256]{2,1,0:T(8,128)(2,1)S(1)}, bf16[2,384,256]{2,1,0:T(8,128)(2,1)S(1)}, u32[]{:S(2)}, u32[]{:S(2)}) collective-permute-start(bf16[2,384,256]{2,1,0:T(8,128)(2,1)S(1)} %collective-permute-done.g1a), channel_id=1, source_target_pairs={{2,0},{3,1},{4,2},{5,3},{6,4},{7,5},{8,6},{9,7},{10,8},{11,9},{12,... | collective-permute-start | bytes 1179656 | tf_op jit(solution)/shard_map/ppermute | solution.py:195
  53.5 14.6 %collective-permute-start.4 = (bf16[2,384,256]{2,1,0:T(8,128)(2,1)S(1)}, bf16[2,384,256]{2,1,0:T(8,128)(2,1)S(1)}, u32[]{:S(2)}, u32[]{:S(2)}) collective-permute-start(bf16[2,384,256]{2,1,0:T(8,128)(2,1)S(1)} %collective-permute-done.3.g3b), channel_id=1, source_target_pairs={{30,0},{31,1},{0,2},{1,3},{2,4},{3,5},{4,6},{5,7},{6,8},{7,9},{8,1... | collective-permute-start | bytes 1179656 | tf_op jit(solution)/shard_map/ppermute | solution.py:195
  58.1 20.8 %copy-start = (bf16[144,128,128]{2,1,0:T(8,128)(2,1)}, bf16[144,128,128]{2,1,0:T(8,128)(2,1)S(1)}, u32[]{:S(2)}) copy-start(bf16[144,128,128]{2,1,0:T(8,128)(2,1)S(1)} %broadcast_select_fusion.blocks) | copy-start | bytes 14155780
  58.2 43.4 %copy-start.2 = (bf16[256,256]{1,0:T(8,128)(2,1)S(1)}, bf16[256,256]{1,0:T(8,128)(2,1)}, u32[]{:S(2)}) copy-start(bf16[256,256]{1,0:T(8,128)(2,1)} %weight.1) | copy-start | bytes 393220
  58.2 43.4 %copy-start.3 = (bf16[1,192,256]{2,1,0:T(8,128)(2,1)S(1)}, bf16[1,192,256]{2,1,0:T(8,128)(2,1)}, u32[]{:S(2)}) copy-start(bf16[1,192,256]{2,1,0:T(8,128)(2,1)} %param.11) | copy-start | bytes 294916
  71.5 7.3 %collective-permute-start.6 = (bf16[1536,256]{1,0:T(8,128)(2,1)S(1)}, bf16[1536,256]{1,0:T(8,128)(2,1)S(1)}, u32[]{:S(2)}, u32[]{:S(2)}) collective-permute-start(bf16[1536,256]{1,0:T(8,128)(2,1)S(1)} %get-tuple-element.20), channel_id=1, source_target_pairs={{0,32},{32,0},{64,96},{96,64},{128,160},{160,128},{192,224},{224,1... | collective-permute-start | bytes 2359304 | tf_op jit(solution)/shard_map/ppermute | solution.py:274
  119.0 6.5 %collective-permute-start.7 = (bf16[8,224,256]{2,1,0:T(8,128)(2,1)S(1)}, bf16[8,224,256]{2,1,0:T(8,128)(2,1)S(1)}, u32[]{:S(2)}, u32[]{:S(2)}) collective-permute-start(bf16[8,224,256]{2,1,0:T(8,128)(2,1)S(1)} %all_to_all.16.mine), channel_id=1, source_target_pairs={{0,32},{32,0},{64,96},{96,64},{128,160},{160,128},{192,224},{224,1... | collective-permute-start | bytes 2752520 | tf_op jit(solution)/shard_map/ppermute | solution.py:281
  125.5 2.3 %copy-start.1 = (bf16[144,128,128]{2,1,0:T(8,128)(2,1)S(1)}, bf16[144,128,128]{2,1,0:T(8,128)(2,1)}, u32[]{:S(2)}) copy-start(bf16[144,128,128]{2,1,0:T(8,128)(2,1)} %copy-done) | copy-start | bytes 14155780
  143.0 20.1 %collective-permute-start.10 = (bf16[1536,256]{1,0:T(8,128)(2,1)S(1)}, bf16[1536,256]{1,0:T(8,128)(2,1)S(1)}, u32[]{:S(2)}, u32[]{:S(2)}) collective-permute-start(bf16[1536,256]{1,0:T(8,128)(2,1)S(1)} %get-tuple-element.29), channel_id=1, source_target_pairs={{0,1},{1,0},{2,3},{3,2},{4,5},{5,4},{6,7},{7,6},{8,9},{9,8},{10,11... | collective-permute-start | bytes 2359304 | tf_op jit(solution)/shard_map/ppermute | solution.py:228
  145.2 10.5 %collective-permute-start.11 = (bf16[400,256]{1,0:T(8,128)(2,1)S(1)}, bf16[400,256]{1,0:T(8,128)(2,1)S(1)}, u32[]{:S(2)}, u32[]{:S(2)}) collective-permute-start(bf16[400,256]{1,0:T(8,128)(2,1)S(1)} %pad_maximum_fusion.2), channel_id=1, source_target_pairs={{2,0},{3,1},{4,2},{5,3},{6,4},{7,5},{8,6},{9,7},{10,8},{11,9},{12,... | collective-permute-start | bytes 614408 | tf_op jit(solution)/shard_map/ppermute | solution.py:195
  147.1 8.6 %collective-permute-start.8 = (bf16[384,256]{1,0:T(8,128)(2,1)S(1)}, bf16[384,256]{1,0:T(8,128)(2,1)S(1)}, u32[]{:S(2)}, u32[]{:S(2)}) collective-permute-start(bf16[384,256]{1,0:T(8,128)(2,1)S(1)} %get-tuple-element.34), channel_id=1, source_target_pairs={{30,0},{31,1},{0,2},{1,3},{2,4},{3,5},{4,6},{5,7},{6,8},{7,9},{8,1... | collective-permute-start | bytes 589832 | tf_op jit(solution)/shard_map/ppermute | solution.py:195
  163.4 15.5 %collective-permute-start.13 = (bf16[784,256]{1,0:T(8,128)(2,1)S(1)}, bf16[784,256]{1,0:T(8,128)(2,1)S(1)}, u32[]{:S(2)}, u32[]{:S(2)}) collective-permute-start(bf16[784,256]{1,0:T(8,128)(2,1)S(1)} %get-tuple-element.46), channel_id=1, source_target_pairs={{2,0},{3,1},{4,2},{5,3},{6,4},{7,5},{8,6},{9,7},{10,8},{11,9},{12,... | collective-permute-start | bytes 1204232 | tf_op jit(solution)/shard_map/ppermute | solution.py:195
  165.3 13.6 %collective-permute-start.12 = (bf16[784,256]{1,0:T(8,128)(2,1)S(1)}, bf16[784,256]{1,0:T(8,128)(2,1)S(1)}, u32[]{:S(2)}, u32[]{:S(2)}) collective-permute-start(bf16[784,256]{1,0:T(8,128)(2,1)S(1)} %get-tuple-element.45), channel_id=1, source_target_pairs={{30,0},{31,1},{0,2},{1,3},{2,4},{3,5},{4,6},{5,7},{6,8},{7,9},{8,1... | collective-permute-start | bytes 1204232 | tf_op jit(solution)/shard_map/ppermute | solution.py:195
  168.7 10.2 %collective-permute-start.9 = (bf16[768,256]{1,0:T(8,128)(2,1)S(1)}, bf16[768,256]{1,0:T(8,128)(2,1)S(1)}, u32[]{:S(2)}, u32[]{:S(2)}) collective-permute-start(bf16[768,256]{1,0:T(8,128)(2,1)S(1)} %get-tuple-element.27), channel_id=1, source_target_pairs={{0,1},{1,0},{2,3},{3,2},{4,5},{5,4},{6,7},{7,6},{8,9},{9,8},{10,11... | collective-permute-start | bytes 1179656 | tf_op jit(solution)/shard_map/ppermute | solution.py:234
  179.1 9.6 %collective-permute-start.16 = (bf16[112,256]{1,0:T(8,128)(2,1)S(1)}, bf16[112,256]{1,0:T(8,128)(2,1)S(1)}, u32[]{:S(2)}, u32[]{:S(2)}) collective-permute-start(bf16[112,256]{1,0:T(8,128)(2,1)S(1)} %get-tuple-element.43), channel_id=1, source_target_pairs={{8,0},{9,1},{10,2},{11,3},{12,4},{13,5},{14,6},{15,7},{16,8},{17,9... | collective-permute-start | bytes 172040 | tf_op jit(solution)/shard_map/ppermute | solution.py:195
  184.4 8.8 %collective-permute-start.14 = (bf16[112,256]{1,0:T(8,128)(2,1)S(1)}, bf16[112,256]{1,0:T(8,128)(2,1)S(1)}, u32[]{:S(2)}, u32[]{:S(2)}) collective-permute-start(bf16[112,256]{1,0:T(8,128)(2,1)S(1)} %get-tuple-element.44), channel_id=1, source_target_pairs={{24,0},{25,1},{26,2},{27,3},{28,4},{29,5},{30,6},{31,7},{0,8},{1,9... | collective-permute-start | bytes 172040 | tf_op jit(solution)/shard_map/ppermute | solution.py:195
  193.2 10.9 %collective-permute-start.17 = (bf16[208,256]{1,0:T(8,128)(2,1)S(1)}, bf16[208,256]{1,0:T(8,128)(2,1)S(1)}, u32[]{:S(2)}, u32[]{:S(2)}) collective-permute-start(bf16[208,256]{1,0:T(8,128)(2,1)S(1)} %pad_maximum_fusion.3), channel_id=1, source_target_pairs={{8,0},{9,1},{10,2},{11,3},{12,4},{13,5},{14,6},{15,7},{16,8},{17,9... | collective-permute-start | bytes 319496 | tf_op jit(solution)/shard_map/ppermute | solution.py:195
  199.8 16.4 %collective-permute-start.15 = (bf16[192,256]{1,0:T(8,128)(2,1)S(1)}, bf16[192,256]{1,0:T(8,128)(2,1)S(1)}, u32[]{:S(2)}, u32[]{:S(2)}) collective-permute-start(bf16[192,256]{1,0:T(8,128)(2,1)S(1)} %get-tuple-element.40), channel_id=1, source_target_pairs={{24,0},{25,1},{26,2},{27,3},{28,4},{29,5},{30,6},{31,7},{0,8},{1,9... | collective-permute-start | bytes 294920 | tf_op jit(solution)/shard_map/ppermute | solution.py:195
  204.8 19.1 %all-to-all-start.2 = ((bf16[16,16,256]{2,1,0:T(8,128)(2,1)}), bf16[16,16,256]{2,1,0:T(8,128)(2,1)S(1)}, u32[]{:S(2)}, u32[]{:S(2)}) async-start(bf16[16,16,256]{2,1,0:T(8,128)(2,1)} %broadcast_in_dim.27), calls=%async_computation.2 | async-start | bytes 262144 | tf_op jit(solution)/shard_map/all_to_all | solution.py:258

commit v6 on v5

--- a/solution.py
+++ b/solution.py
@@ -31,7 +31,7 @@
 
 def each_slot(slot_count, one_slot):
     done = 0
-    for step in (16, 4, 1):
+    for step in (36, 12, 4, 1):
 
         def several(i, carry, step=step, done=done):
             one_slot([done + i * step + u for u in range(step)])
@@ -227,11 +227,11 @@
     swap2 = pair_swap(sent2, "dst", Y_GROUPS, y)
     swap13 = lax.ppermute(sent13, "dst", Y_SWAP)
     w = total_f32(w, swap2[full:])
-    low = shift(total_of(kept[2][:half], swap2[:half]), -1)
+    low = total_of(kept[2][:half], swap2[:half])
     high = jnp.concatenate([total_of(kept[2][half:], swap2[half:full]), w.astype(BF16)], 0)
-    high = shift(high, 1)
-    sent0, low = lax.optimization_barrier((sent0, low))
-    swap0 = lax.ppermute(sent0, "dst", Y_SWAP)
+    sent0, low, high = lax.optimization_barrier((sent0, low, high))
+    low, high = shift(low, -1), shift(high, 1)
+    swap0 = pair_swap(sent0, "dst", Y_GROUPS, y)
     w = total_of(w, high[half:])
     none = jnp.zeros_like(low[:ROWS])
     up = total_of(kept[1], swap13[:full], jnp.concatenate([none, low, none], 0))
@@ -258,6 +258,11 @@
     return lax.all_to_all(copies, "src", 0, 0, tiled=True).reshape(WIDTH, WIDTH).astype(F32)
 
 
+def staged(meta, values):
+    live = jnp.arange(values.shape[0], dtype=jnp.int32) < meta[0]
+    return jnp.where(live[:, None, None], values, jnp.zeros((), BF16))
+
+
 def shards(features, weight, values, coords, counts, cotangent):
     tile_values = values[0, 0]
     pairs = coords[0, 0].T.reshape(-1)
@@ -268,8 +273,7 @@
 
     parts = gather_sources(features)
     tile_values, _ = lax.optimization_barrier((tile_values, parts[0]))
-    live = jnp.arange(tile_values.shape[0], dtype=jnp.int32) < meta[0]
-    blocks = jnp.where(live[:, None, None], tile_values, jnp.zeros((), BF16))
+    blocks = staged(meta, tile_values)
     own, other = forward_sums(meta, pairs, blocks, parts, dest_rows)
     swapped = lax.ppermute(other, "src", CORE_SWAP)
     chip_sums = (own.astype(F32) + swapped.astype(F32)).astype(BF16)
@@ -279,7 +283,8 @@
     activations, message = middle(terms, weight, cotangent[0])
     mine = lax.all_to_all(message, "src", 0, 0, tiled=True, axis_index_groups=CORE_GROUPS)
     theirs = lax.ppermute(mine, "src", CORE_SWAP)
-    sums = backward_sums(meta, pairs, blocks, mine, theirs)
+    tile_values, mine = lax.optimization_barrier((values[0, 0], mine))
+    sums = backward_sums(meta, pairs, staged(meta, tile_values), mine, theirs)
     input_grad, weight_part = scatter_sources(*sums, y)
     weight_grad = gather_weight(weight_part)
     return (activations[None], input_grad, weight_grad)

time: 226 us -> 220 us (0.973)
  blocking collectives: 86 us -> 93.3 us
  starting transfers between devices: 72.5 us -> 66.1 us
  waiting for transfers between devices: 47.7 us -> 42.8 us
  other arithmetic: 5.19 us -> 7.93 us
  local copies, waits for them, and re-layouts: 3.88 us -> 1.54 us
    all_gather x1 -> x2, blocking collectives: 11.5 us -> 20.9 us  [pair_swap(): both = lax.all_gather(array, axis, axis=0, axis_index_groups=groups)]
    ppermute x1 -> x0, waiting for transfers between devices: 7.83 us -> none  [scatter_sources(): swap0 = lax.ppermute(sent0, 'dst', Y_SWAP)]
    ppermute x14, waiting for transfers between devices: 21.6 us -> 26.8 us  [shift(): return lax.ppermute(array, 'dst', from_z(step))]
    all_to_all x1, starting transfers between devices: 11.4 us -> 7.52 us  [gather_weight(): lax.all_to_all(copies, 'src', 0, 0, tiled=True).reshape(WIDTH, WIDTH)]
    select_n x1 -> x2, other arithmetic: 2.73 us -> 5.46 us  [staged(): return jnp.where(live[:, None, None], values, jnp.zeros((), BF16))]
    unnamed x8 -> x4, local copies, waits for them, and re-layouts: 2.35 us -> 0.01 us
    ppermute x1 -> x0, starting transfers between devices: 2.34 us -> none  [scatter_sources(): swap0 = lax.ppermute(sent0, 'dst', Y_SWAP)]
  transfers between devices with their start and end apart: 19 -> 18, of which waited for: 12 -> 12; matrix products, arithmetic and copies ran while one was open for 2% -> 4% of each run, Pallas kernels for 0% -> 0%
where the time goes in v6:
time: 220 us
  blocking collectives  93.3 us (42%)
  starting transfers between devices  66.1 us (30%)
  waiting for transfers between devices  42.8 us (19%)
  other arithmetic  7.93 us (4%)
  Pallas kernels  6.21 us (3%)
    ppermute x14, starting transfers between devices, shift(): return lax.ppermute(array, 'dst', from_z(step))  46.8 us
    all_gather x1, blocking collectives, gather_sources(): lax.all_gather(features, 'dst', axis=0, axis_index_groups=STRIDE_GROUPS)  28 us
    ppermute x14, waiting for transfers between devices, shift(): return lax.ppermute(array, 'dst', from_z(step))  26.8 us
    all_gather x2, blocking collectives, pair_swap(): both = lax.all_gather(array, axis, axis=0, axis_index_groups=groups)  20.9 us
    all_to_all x1, blocking collectives, shards(): lax.all_to_all(chip_sums.reshape(CHIPS, ROWS, WIDTH), 'src', 0, 0, tiled=...  20.6 us
    all_to_all x1, blocking collectives, shards(): lax.all_to_all(message, 'src', 0, 0, tiled=True, axis_index_groups=CORE_G...  16.6 us
    all_to_all x1, starting transfers between devices, gather_weight(): lax.all_to_all(copies, 'src', 0, 0, tiled=True).reshape(WIDTH, WIDTH)  7.52 us
    all_gather x1, blocking collectives, gather_sources(): lax.all_gather(own, 'dst', axis=1, tiled=True, axis_index_groups=Y_GROUPS)  7.29 us
  transfers between devices with their start and end apart: 18, of which 12 were waited for; matrix products, arithmetic and copies ran while one was open for 4% of the time, Pallas kernels for 0%

profile of v6, /device:TPU:1, one launch (start us, length us, event | category | flops | bytes accessed | tf_op | source)
XLA Modules:
  0.0 219.5 jit_solution(16807322604890680709)
XLA Ops:
  0.6 28.0 %all-gather = bf16[768,256]{1,0:T(8,128)(2,1)S(1)} all-gather(bf16[192,256]{1,0:T(8,128)(2,1)} %param.6), channel_id=2, replica_groups={{0,8,16,24},{1,9,17,25},{2,10,18,26},{3,11,19,27},{4,12,20,28},{5,13,21..., dimensions={0}, use_global_device_ids=true | all-gather | bytes 491520 | tf_op jit(solution)/shard_map/all_gather | solution.py:199
  28.6 7.3 %all_gather.23.g0 = bf16[4,384,256]{2,1,0:T(8,128)(2,1)S(1)} all-gather(bf16[4,192,256]{2,1,0:T(8,128)(2,1)S(1)} %bitcast.54), channel_id=1, replica_groups={{0,1},{2,3},{4,5},{6,7},{8,9},{10,11},{12,13},{14,15},{16,17},{18,19},{..., dimensions={1}, use_global_device_ids=true | all-gather | bytes 1179648 | tf_op jit(solution)/shard_map/all_gather | solution.py:200
  36.0 2.9 %collective-permute-start = (bf16[2,384,256]{2,1,0:T(8,128)(2,1)S(1)}, bf16[2,384,256]{2,1,0:T(8,128)(2,1)S(1)}, u32[]{:S(2)}, u32[]{:S(2)}) collective-permute-start(bf16[2,384,256]{2,1,0:T(8,128)(2,1)S(1)} %get-tuple-element.44), channel_id=1, source_target_pairs={{2,0},{3,1},{4,2},{5,3},{6,4},{7,5},{8,6},{9,7},{10,8},{11,9},{12,... | collective-permute-start | bytes 1179656 | tf_op jit(solution)/shard_map/ppermute | solution.py:195
  41.3 4.2 %collective-permute-start.1 = (bf16[2,384,256]{2,1,0:T(8,128)(2,1)S(1)}, bf16[2,384,256]{2,1,0:T(8,128)(2,1)S(1)}, u32[]{:S(2)}, u32[]{:S(2)}) collective-permute-start(bf16[2,384,256]{2,1,0:T(8,128)(2,1)S(1)} %get-tuple-element.43), channel_id=1, source_target_pairs={{2,0},{3,1},{4,2},{5,3},{6,4},{7,5},{8,6},{9,7},{10,8},{11,9},{12,... | collective-permute-start | bytes 1179656 | tf_op jit(solution)/shard_map/ppermute | solution.py:195
  48.9 4.6 %collective-permute-start.2 = (bf16[2,384,256]{2,1,0:T(8,128)(2,1)S(1)}, bf16[2,384,256]{2,1,0:T(8,128)(2,1)S(1)}, u32[]{:S(2)}, u32[]{:S(2)}) collective-permute-start(bf16[2,384,256]{2,1,0:T(8,128)(2,1)S(1)} %collective-permute-done.g1a), channel_id=1, source_target_pairs={{2,0},{3,1},{4,2},{5,3},{6,4},{7,5},{8,6},{9,7},{10,8},{11,9},{12,... | collective-permute-start | bytes 1179656 | tf_op jit(solution)/shard_map/ppermute | solution.py:195
  59.7 3.1 %collective-permute-done.2.g2a = bf16[2,384,256]{2,1,0:T(8,128)(2,1)S(1)} collective-permute-done((bf16[2,384,256]{2,1,0:T(8,128)(2,1)S(1)}, bf16[2,384,256]{2,1,0:T(8,128)(2,1)S(1)}, u32[]{:S(2)}, u32[]{:S(2)}) %collective-permute-start.2) | collective-permute-done | bytes 393248 | tf_op jit(solution)/shard_map/ppermute | solution.py:195
  62.8 5.3 %collective-permute-done.4.g2b = bf16[2,384,256]{2,1,0:T(8,128)(2,1)S(1)} collective-permute-done((bf16[2,384,256]{2,1,0:T(8,128)(2,1)S(1)}, bf16[2,384,256]{2,1,0:T(8,128)(2,1)S(1)}, u32[]{:S(2)}, u32[]{:S(2)}) %collective-permute-start.4) | collective-permute-done | bytes 393248 | tf_op jit(solution)/shard_map/ppermute | solution.py:195
  70.7 5.4 %collective-permute-start.6 = (bf16[1536,256]{1,0:T(8,128)(2,1)S(1)}, bf16[1536,256]{1,0:T(8,128)(2,1)S(1)}, u32[]{:S(2)}, u32[]{:S(2)}) collective-permute-start(bf16[1536,256]{1,0:T(8,128)(2,1)S(1)} %get-tuple-element.23), channel_id=1, source_target_pairs={{0,32},{32,0},{64,96},{96,64},{128,160},{160,128},{192,224},{224,1... | collective-permute-start | bytes 2359304 | tf_op jit(solution)/shard_map/ppermute | solution.py:278
  78.3 20.6 %all_to_all.15.terms = bf16[8,192,256]{2,1,0:T(8,128)(2,1)S(1)} all-to-all(bf16[8,192,256]{2,1,0:T(8,128)(2,1)S(1)} %bitcast.48), channel_id=1, replica_groups={{0,64,128,192,256,320,384,448},{32,96,160,224,288,352,416,480},{1,65,12..., dimensions={0} | all-to-all | bytes 1572864 | tf_op jit(solution)/shard_map/all_to_all | solution.py:280
  99.7 16.6 %all_to_all.16.mine = bf16[8,224,256]{2,1,0:T(8,128)(2,1)S(1)} all-to-all(bf16[8,224,256]{2,1,0:T(8,128)(2,1)S(1)} %get-tuple-element.25), channel_id=1, replica_groups={{0,64,128,192,256,320,384,448},{32,96,160,224,288,352,416,480},{1,65,12..., dimensions={0} | all-to-all | bytes 1835008 | tf_op jit(solution)/shard_map/all_to_all | solution.py:284
  116.3 4.4 %collective-permute-start.7 = (bf16[8,224,256]{2,1,0:T(8,128)(2,1)S(1)}, bf16[8,224,256]{2,1,0:T(8,128)(2,1)S(1)}, u32[]{:S(2)}, u32[]{:S(2)}) collective-permute-start(bf16[8,224,256]{2,1,0:T(8,128)(2,1)S(1)} %all_to_all.16.mine), channel_id=1, source_target_pairs={{0,32},{32,0},{64,96},{96,64},{128,160},{160,128},{192,224},{224,1... | collective-permute-start | bytes 2752520 | tf_op jit(solution)/shard_map/ppermute | solution.py:285
  126.2 11.7 %all-gather.1 = bf16[1568,256]{1,0:T(8,128)(2,1)S(1)} all-gather(bf16[784,256]{1,0:T(8,128)(2,1)S(1)} %get-tuple-element.31), channel_id=3, replica_groups={{0,1},{2,3},{4,5},{6,7},{8,9},{10,11},{12,13},{14,15},{16,17},{18,19},{..., dimensions={0}, use_global_device_ids=true | all-gather | bytes 1204224 | tf_op jit(solution)/shard_map/all_gather | solution.py:221
  142.5 2.8 %collective-permute-start.9 = (bf16[384,256]{1,0:T(8,128)(2,1)S(1)}, bf16[384,256]{1,0:T(8,128)(2,1)S(1)}, u32[]{:S(2)}, u32[]{:S(2)}) collective-permute-start(bf16[384,256]{1,0:T(8,128)(2,1)S(1)} %get-tuple-element.36), channel_id=1, source_target_pairs={{30,0},{31,1},{0,2},{1,3},{2,4},{3,5},{4,6},{5,7},{6,8},{7,9},{8,1... | collective-permute-start | bytes 589832 | tf_op jit(solution)/shard_map/ppermute | solution.py:195
  147.6 3.5 %collective-permute-done.9 = bf16[384,256]{1,0:T(8,128)(2,1)S(1)} collective-permute-done((bf16[384,256]{1,0:T(8,128)(2,1)S(1)}, bf16[384,256]{1,0:T(8,128)(2,1)S(1)}, u32[]{:S(2)}, u32[]{:S(2)}) %collective-permute-start.9) | collective-permute-done | bytes 196640 | tf_op jit(solution)/shard_map/ppermute | solution.py:195
  151.0 7.2 %collective-permute-done.8 = bf16[1536,256]{1,0:T(8,128)(2,1)S(1)} collective-permute-done((bf16[1536,256]{1,0:T(8,128)(2,1)S(1)}, bf16[1536,256]{1,0:T(8,128)(2,1)S(1)}, u32[]{:S(2)}, u32[]{:S(2)}) %collective-permute-start.8) | collective-permute-done | bytes 786464 | tf_op jit(solution)/shard_map/ppermute | solution.py:228
  158.6 2.8 %collective-permute-start.12 = (bf16[784,256]{1,0:T(8,128)(2,1)S(1)}, bf16[784,256]{1,0:T(8,128)(2,1)S(1)}, u32[]{:S(2)}, u32[]{:S(2)}) collective-permute-start(bf16[784,256]{1,0:T(8,128)(2,1)S(1)} %get-tuple-element.52), channel_id=1, source_target_pairs={{2,0},{3,1},{4,2},{5,3},{6,4},{7,5},{8,6},{9,7},{10,8},{11,9},{12,... | collective-permute-start | bytes 1204232 | tf_op jit(solution)/shard_map/ppermute | solution.py:195
  163.9 9.2 %all-gather.2 = bf16[1536,256]{1,0:T(8,128)(2,1)S(1)} all-gather(bf16[768,256]{1,0:T(8,128)(2,1)S(1)} %get-tuple-element.33), channel_id=4, replica_groups={{0,1},{2,3},{4,5},{6,7},{8,9},{10,11},{12,13},{14,15},{16,17},{18,19},{..., dimensions={0}, use_global_device_ids=true | all-gather | bytes 1179648 | tf_op jit(solution)/shard_map/all_gather | solution.py:221
  174.0 7.0 %collective-permute-start.15 = (bf16[112,256]{1,0:T(8,128)(2,1)S(1)}, bf16[112,256]{1,0:T(8,128)(2,1)S(1)}, u32[]{:S(2)}, u32[]{:S(2)}) collective-permute-start(bf16[112,256]{1,0:T(8,128)(2,1)S(1)} %get-tuple-element.49), channel_id=1, source_target_pairs={{8,0},{9,1},{10,2},{11,3},{12,4},{13,5},{14,6},{15,7},{16,8},{17,9... | collective-permute-start | bytes 172040 | tf_op jit(solution)/shard_map/ppermute | solution.py:195
  183.6 7.2 %collective-permute-done.13 = bf16[112,256]{1,0:T(8,128)(2,1)S(1)} collective-permute-done((bf16[112,256]{1,0:T(8,128)(2,1)S(1)}, bf16[112,256]{1,0:T(8,128)(2,1)S(1)}, u32[]{:S(2)}, u32[]{:S(2)}) %collective-permute-start.13) | collective-permute-done | bytes 57376 | tf_op jit(solution)/shard_map/ppermute | solution.py:195
  190.9 2.8 %collective-permute-start.16 = (bf16[208,256]{1,0:T(8,128)(2,1)S(1)}, bf16[208,256]{1,0:T(8,128)(2,1)S(1)}, u32[]{:S(2)}, u32[]{:S(2)}) collective-permute-start(bf16[208,256]{1,0:T(8,128)(2,1)S(1)} %pad_maximum_fusion.3), channel_id=1, source_target_pairs={{8,0},{9,1},{10,2},{11,3},{12,4},{13,5},{14,6},{15,7},{16,8},{17,9... | collective-permute-start | bytes 319496 | tf_op jit(solution)/shard_map/ppermute | solution.py:195
  193.6 6.4 %collective-permute-start.14 = (bf16[192,256]{1,0:T(8,128)(2,1)S(1)}, bf16[192,256]{1,0:T(8,128)(2,1)S(1)}, u32[]{:S(2)}, u32[]{:S(2)}) collective-permute-start(bf16[192,256]{1,0:T(8,128)(2,1)S(1)} %get-tuple-element.46), channel_id=1, source_target_pairs={{24,0},{25,1},{26,2},{27,3},{28,4},{29,5},{30,6},{31,7},{0,8},{1,9... | collective-permute-start | bytes 294920 | tf_op jit(solution)/shard_map/ppermute | solution.py:195
  200.1 2.9 %collective-permute-done.16 = bf16[208,256]{1,0:T(8,128)(2,1)S(1)} collective-permute-done((bf16[208,256]{1,0:T(8,128)(2,1)S(1)}, bf16[208,256]{1,0:T(8,128)(2,1)S(1)}, u32[]{:S(2)}, u32[]{:S(2)}) %collective-permute-start.16) | collective-permute-done | bytes 106528 | tf_op jit(solution)/shard_map/ppermute | solution.py:195
  203.6 7.5 %all-to-all-start.2 = ((bf16[16,16,256]{2,1,0:T(8,128)(2,1)}), bf16[16,16,256]{2,1,0:T(8,128)(2,1)S(1)}, u32[]{:S(2)}, u32[]{:S(2)}) async-start(bf16[16,16,256]{2,1,0:T(8,128)(2,1)} %broadcast_in_dim.32), calls=%async_computation.2 | async-start | bytes 262144 | tf_op jit(solution)/shard_map/all_to_all | solution.py:258
  211.8 7.0 %all-to-all-done.2 = bf16[16,16,256]{2,1,0:T(8,128)(2,1)S(1)} async-done(((bf16[16,16,256]{2,1,0:T(8,128)(2,1)}), bf16[16,16,256]{2,1,0:T(8,128)(2,1)S(1)}, u32[]{:S(2)}, u32[]{:S(2)}) %all-to-all-start.2) | async-done | bytes 131104 | tf_op jit(solution)/shard_map/all_to_all | solution.py:258
  (53 shorter events, 37.6 us)
Async XLA Ops:
  36.0 12.9 %collective-permute-start = (bf16[2,384,256]{2,1,0:T(8,128)(2,1)S(1)}, bf16[2,384,256]{2,1,0:T(8,128)(2,1)S(1)}, u32[]{:S(2)}, u32[]{:S(2)}) collective-permute-start(bf16[2,384,256]{2,1,0:T(8,128)(2,1)S(1)} %get-tuple-element.44), channel_id=1, source_target_pairs={{2,0},{3,1},{4,2},{5,3},{6,4},{7,5},{8,6},{9,7},{10,8},{11,9},{12,... | collective-permute-start | bytes 1179656 | tf_op jit(solution)/shard_map/ppermute | solution.py:195
  38.9 14.5 %collective-permute-start.3 = (bf16[2,384,256]{2,1,0:T(8,128)(2,1)S(1)}, bf16[2,384,256]{2,1,0:T(8,128)(2,1)S(1)}, u32[]{:S(2)}, u32[]{:S(2)}) collective-permute-start(bf16[2,384,256]{2,1,0:T(8,128)(2,1)S(1)} %get-tuple-element.43), channel_id=1, source_target_pairs={{30,0},{31,1},{0,2},{1,3},{2,4},{3,5},{4,6},{5,7},{6,8},{7,9},{8,1... | collective-permute-start | bytes 1179656 | tf_op jit(solution)/shard_map/ppermute | solution.py:195
  41.3 16.9 %collective-permute-start.1 = (bf16[2,384,256]{2,1,0:T(8,128)(2,1)S(1)}, bf16[2,384,256]{2,1,0:T(8,128)(2,1)S(1)}, u32[]{:S(2)}, u32[]{:S(2)}) collective-permute-start(bf16[2,384,256]{2,1,0:T(8,128)(2,1)S(1)} %get-tuple-element.43), channel_id=1, source_target_pairs={{2,0},{3,1},{4,2},{5,3},{6,4},{7,5},{8,6},{9,7},{10,8},{11,9},{12,... | collective-permute-start | bytes 1179656 | tf_op jit(solution)/shard_map/ppermute | solution.py:195
  45.5 14.2 %collective-permute-start.5 = (bf16[2,384,256]{2,1,0:T(8,128)(2,1)S(1)}, bf16[2,384,256]{2,1,0:T(8,128)(2,1)S(1)}, u32[]{:S(2)}, u32[]{:S(2)}) collective-permute-start(bf16[2,384,256]{2,1,0:T(8,128)(2,1)S(1)} %get-tuple-element.44), channel_id=1, source_target_pairs={{30,0},{31,1},{0,2},{1,3},{2,4},{3,5},{4,6},{5,7},{6,8},{7,9},{8,1... | collective-permute-start | bytes 1179656 | tf_op jit(solution)/shard_map/ppermute | solution.py:195
  48.9 13.9 %collective-permute-start.2 = (bf16[2,384,256]{2,1,0:T(8,128)(2,1)S(1)}, bf16[2,384,256]{2,1,0:T(8,128)(2,1)S(1)}, u32[]{:S(2)}, u32[]{:S(2)}) collective-permute-start(bf16[2,384,256]{2,1,0:T(8,128)(2,1)S(1)} %collective-permute-done.g1a), channel_id=1, source_target_pairs={{2,0},{3,1},{4,2},{5,3},{6,4},{7,5},{8,6},{9,7},{10,8},{11,9},{12,... | collective-permute-start | bytes 1179656 | tf_op jit(solution)/shard_map/ppermute | solution.py:195
  53.5 14.6 %collective-permute-start.4 = (bf16[2,384,256]{2,1,0:T(8,128)(2,1)S(1)}, bf16[2,384,256]{2,1,0:T(8,128)(2,1)S(1)}, u32[]{:S(2)}, u32[]{:S(2)}) collective-permute-start(bf16[2,384,256]{2,1,0:T(8,128)(2,1)S(1)} %collective-permute-done.3.g3b), channel_id=1, source_target_pairs={{30,0},{31,1},{0,2},{1,3},{2,4},{3,5},{4,6},{5,7},{6,8},{7,9},{8,1... | collective-permute-start | bytes 1179656 | tf_op jit(solution)/shard_map/ppermute | solution.py:195
  58.1 40.7 %copy-start = (bf16[256,256]{1,0:T(8,128)(2,1)S(1)}, bf16[256,256]{1,0:T(8,128)(2,1)}, u32[]{:S(2)}) copy-start(bf16[256,256]{1,0:T(8,128)(2,1)} %weight.1) | copy-start | bytes 393220
  58.2 40.7 %copy-start.1 = (bf16[1,192,256]{2,1,0:T(8,128)(2,1)S(1)}, bf16[1,192,256]{2,1,0:T(8,128)(2,1)}, u32[]{:S(2)}) copy-start(bf16[1,192,256]{2,1,0:T(8,128)(2,1)} %param.11) | copy-start | bytes 294916
  70.7 7.3 %collective-permute-start.6 = (bf16[1536,256]{1,0:T(8,128)(2,1)S(1)}, bf16[1536,256]{1,0:T(8,128)(2,1)S(1)}, u32[]{:S(2)}, u32[]{:S(2)}) collective-permute-start(bf16[1536,256]{1,0:T(8,128)(2,1)S(1)} %get-tuple-element.23), channel_id=1, source_target_pairs={{0,32},{32,0},{64,96},{96,64},{128,160},{160,128},{192,224},{224,1... | collective-permute-start | bytes 2359304 | tf_op jit(solution)/shard_map/ppermute | solution.py:278
  116.3 7.2 %collective-permute-start.7 = (bf16[8,224,256]{2,1,0:T(8,128)(2,1)S(1)}, bf16[8,224,256]{2,1,0:T(8,128)(2,1)S(1)}, u32[]{:S(2)}, u32[]{:S(2)}) collective-permute-start(bf16[8,224,256]{2,1,0:T(8,128)(2,1)S(1)} %all_to_all.16.mine), channel_id=1, source_target_pairs={{0,32},{32,0},{64,96},{96,64},{128,160},{160,128},{192,224},{224,1... | collective-permute-start | bytes 2752520 | tf_op jit(solution)/shard_map/ppermute | solution.py:285
  137.9 20.3 %collective-permute-start.8 = (bf16[1536,256]{1,0:T(8,128)(2,1)S(1)}, bf16[1536,256]{1,0:T(8,128)(2,1)S(1)}, u32[]{:S(2)}, u32[]{:S(2)}) collective-permute-start(bf16[1536,256]{1,0:T(8,128)(2,1)S(1)} %get-tuple-element.35), channel_id=1, source_target_pairs={{0,1},{1,0},{2,3},{3,2},{4,5},{5,4},{6,7},{7,6},{8,9},{9,8},{10,11... | collective-permute-start | bytes 2359304 | tf_op jit(solution)/shard_map/ppermute | solution.py:228
  140.0 7.5 %collective-permute-start.10 = (bf16[400,256]{1,0:T(8,128)(2,1)S(1)}, bf16[400,256]{1,0:T(8,128)(2,1)S(1)}, u32[]{:S(2)}, u32[]{:S(2)}) collective-permute-start(bf16[400,256]{1,0:T(8,128)(2,1)S(1)} %pad_maximum_fusion.2), channel_id=1, source_target_pairs={{2,0},{3,1},{4,2},{5,3},{6,4},{7,5},{8,6},{9,7},{10,8},{11,9},{12,... | collective-permute-start | bytes 614408 | tf_op jit(solution)/shard_map/ppermute | solution.py:195
  142.5 8.5 %collective-permute-start.9 = (bf16[384,256]{1,0:T(8,128)(2,1)S(1)}, bf16[384,256]{1,0:T(8,128)(2,1)S(1)}, u32[]{:S(2)}, u32[]{:S(2)}) collective-permute-start(bf16[384,256]{1,0:T(8,128)(2,1)S(1)} %get-tuple-element.36), channel_id=1, source_target_pairs={{30,0},{31,1},{0,2},{1,3},{2,4},{3,5},{4,6},{5,7},{6,8},{7,9},{8,1... | collective-permute-start | bytes 589832 | tf_op jit(solution)/shard_map/ppermute | solution.py:195
  158.6 14.5 %collective-permute-start.12 = (bf16[784,256]{1,0:T(8,128)(2,1)S(1)}, bf16[784,256]{1,0:T(8,128)(2,1)S(1)}, u32[]{:S(2)}, u32[]{:S(2)}) collective-permute-start(bf16[784,256]{1,0:T(8,128)(2,1)S(1)} %get-tuple-element.52), channel_id=1, source_target_pairs={{2,0},{3,1},{4,2},{5,3},{6,4},{7,5},{8,6},{9,7},{10,8},{11,9},{12,... | collective-permute-start | bytes 1204232 | tf_op jit(solution)/shard_map/ppermute | solution.py:195
  161.4 12.3 %collective-permute-start.11 = (bf16[784,256]{1,0:T(8,128)(2,1)S(1)}, bf16[784,256]{1,0:T(8,128)(2,1)S(1)}, u32[]{:S(2)}, u32[]{:S(2)}) collective-permute-start(bf16[784,256]{1,0:T(8,128)(2,1)S(1)} %get-tuple-element.51), channel_id=1, source_target_pairs={{30,0},{31,1},{0,2},{1,3},{2,4},{3,5},{4,6},{5,7},{6,8},{7,9},{8,1... | collective-permute-start | bytes 1204232 | tf_op jit(solution)/shard_map/ppermute | solution.py:195
  174.0 9.6 %collective-permute-start.15 = (bf16[112,256]{1,0:T(8,128)(2,1)S(1)}, bf16[112,256]{1,0:T(8,128)(2,1)S(1)}, u32[]{:S(2)}, u32[]{:S(2)}) collective-permute-start(bf16[112,256]{1,0:T(8,128)(2,1)S(1)} %get-tuple-element.49), channel_id=1, source_target_pairs={{8,0},{9,1},{10,2},{11,3},{12,4},{13,5},{14,6},{15,7},{16,8},{17,9... | collective-permute-start | bytes 172040 | tf_op jit(solution)/shard_map/ppermute | solution.py:195
  181.0 9.8 %collective-permute-start.13 = (bf16[112,256]{1,0:T(8,128)(2,1)S(1)}, bf16[112,256]{1,0:T(8,128)(2,1)S(1)}, u32[]{:S(2)}, u32[]{:S(2)}) collective-permute-start(bf16[112,256]{1,0:T(8,128)(2,1)S(1)} %get-tuple-element.50), channel_id=1, source_target_pairs={{24,0},{25,1},{26,2},{27,3},{28,4},{29,5},{30,6},{31,7},{0,8},{1,9... | collective-permute-start | bytes 172040 | tf_op jit(solution)/shard_map/ppermute | solution.py:195
  190.9 12.1 %collective-permute-start.16 = (bf16[208,256]{1,0:T(8,128)(2,1)S(1)}, bf16[208,256]{1,0:T(8,128)(2,1)S(1)}, u32[]{:S(2)}, u32[]{:S(2)}) collective-permute-start(bf16[208,256]{1,0:T(8,128)(2,1)S(1)} %pad_maximum_fusion.3), channel_id=1, source_target_pairs={{8,0},{9,1},{10,2},{11,3},{12,4},{13,5},{14,6},{15,7},{16,8},{17,9... | collective-permute-start | bytes 319496 | tf_op jit(solution)/shard_map/ppermute | solution.py:195
  193.6 17.5 %collective-permute-start.14 = (bf16[192,256]{1,0:T(8,128)(2,1)S(1)}, bf16[192,256]{1,0:T(8,128)(2,1)S(1)}, u32[]{:S(2)}, u32[]{:S(2)}) collective-permute-start(bf16[192,256]{1,0:T(8,128)(2,1)S(1)} %get-tuple-element.46), channel_id=1, source_target_pairs={{24,0},{25,1},{26,2},{27,3},{28,4},{29,5},{30,6},{31,7},{0,8},{1,9... | collective-permute-start | bytes 294920 | tf_op jit(solution)/shard_map/ppermute | solution.py:195
  203.6 15.2 %all-to-all-start.2 = ((bf16[16,16,256]{2,1,0:T(8,128)(2,1)}), bf16[16,16,256]{2,1,0:T(8,128)(2,1)S(1)}, u32[]{:S(2)}, u32[]{:S(2)}) async-start(bf16[16,16,256]{2,1,0:T(8,128)(2,1)} %broadcast_in_dim.32), calls=%async_computation.2 | async-start | bytes 262144 | tf_op jit(solution)/shard_map/all_to_all | solution.py:258

commit v7 on v6

--- a/solution.py
+++ b/solution.py
@@ -58,12 +58,12 @@
     def one_slot(ks):
         terms = [
             lax.dot_general(
-                blocks[k], block_of(rows, coords[k]), (((0,), (0,)), ((), ())), preferred_element_type=F32
+                blocks[k], block_of(rows, coords[0, k]), (((0,), (0,)), ((), ())), preferred_element_type=F32
             )
             for k in ks
         ]
         for k, term in zip(ks, terms):
-            add_block(total, coords[slots + k], term)
+            add_block(total, coords[1, k], term)
 
     pieces = ((0, g0, 0), (1, g1a, 0), (1, g1b, 2), (2, g2a, 0), (2, g2b, 2), (3, g3a, 0), (3, g3b, 2))
     for offset, ref, first in pieces:
@@ -137,11 +137,11 @@
 
     def one_slot(ks):
         terms = [
-            jnp.dot(blocks[k], block_of(rows, coords[slots + k]), preferred_element_type=F32)
+            jnp.dot(blocks[k], block_of(rows, coords[1, k]), preferred_element_type=F32)
             for k in ks
         ]
         for k, term in zip(ks, terms):
-            add_block(total, coords[k], term)
+            add_block(total, coords[0, k], term)
 
     share = wsum.shape[0]
     summed = jnp.zeros(wsum.shape, F32)
@@ -244,13 +244,12 @@
     part = ROWS // 2
     from_left = shift(jnp.concatenate([near[2, :part], w], 0), -4)
     from_right = shift(jnp.concatenate([near[2, part:], w], 0), 4)
-    w_left, w_right = from_left[part:], from_right[part:]
+    w_left, w_right, w_far = from_left[part:], from_right[part:], shift(w, 8)
     none = jnp.zeros((part, WIDTH), BF16)
     left = shift(total_of(near[1], jnp.concatenate([from_left[:part], none], 0)), -4)
     right = total_of(near[3], jnp.concatenate([none, from_right[:part]], 0))
-    right = shift(jnp.concatenate([right, w_right], 0), 4)
-    w = total_of(w, w_left, w_right, right[ROWS:])
-    return total_of(near[0], left, right[:ROWS]), w
+    right = shift(right, 4)
+    return total_of(near[0], left, right), total_of(w, w_left, w_right, w_far)
 
 
 def gather_weight(part):
@@ -265,7 +264,7 @@
 
 def shards(features, weight, values, coords, counts, cotangent):
     tile_values = values[0, 0]
-    pairs = coords[0, 0].T.reshape(-1)
+    pairs = coords[0, 0].T
     place = lax.axis_index("dst")
     z, y, core = place // NY, lax.rem(place, NY), lax.rem(lax.axis_index("src"), 2)
     meta = jnp.stack([counts[0, 0], z, y, core]).astype(jnp.int32)

time: 220 us -> 219 us (level)
  waiting for transfers between devices: 42.8 us -> 31.9 us
  starting transfers between devices: 66.1 us -> 75.5 us
  Pallas kernels: 6.21 us -> 9.91 us
  blocking collectives: 93.3 us -> 90.3 us
    ppermute x14 -> x15, waiting for transfers between devices: 26.8 us -> 14.8 us  [shift(): return lax.ppermute(array, 'dst', from_z(step))]
    ppermute x14 -> x15, starting transfers between devices: 46.8 us -> 55.1 us  [shift(): return lax.ppermute(array, 'dst', from_z(step))]
    all_to_all x1, blocking collectives: 20.6 us -> 17.8 us  [shards(): lax.all_to_all(chip_sums.reshape(CHIPS, ROWS, WIDTH), 'src', 0, 0, tiled=...]
  transfers between devices with their start and end apart: 18 -> 19, of which waited for: 12 -> 8; matrix products, arithmetic and copies ran while one was open for 4% -> 3% of each run, Pallas kernels for 0% -> 0%
where the time goes in v7:
time: 219 us; the launch traced here: 218 us
  blocking collectives  90.3 us (41%)
  starting transfers between devices  75.5 us (34%)
  waiting for transfers between devices  31.9 us (15%)
  Pallas kernels  9.91 us (5%)
  other arithmetic  7.92 us (4%)
    ppermute x15, starting transfers between devices, shift(): return lax.ppermute(array, 'dst', from_z(step))  55.1 us
    all_gather x1, blocking collectives, gather_sources(): lax.all_gather(features, 'dst', axis=0, axis_index_groups=STRIDE_GROUPS)  28 us
    all_gather x2, blocking collectives, pair_swap(): both = lax.all_gather(array, axis, axis=0, axis_index_groups=groups)  20.6 us
    all_to_all x1, blocking collectives, shards(): lax.all_to_all(chip_sums.reshape(CHIPS, ROWS, WIDTH), 'src', 0, 0, tiled=...  17.8 us
    all_to_all x1, blocking collectives, shards(): lax.all_to_all(message, 'src', 0, 0, tiled=True, axis_index_groups=CORE_G...  16.6 us
    ppermute x15, waiting for transfers between devices, shift(): return lax.ppermute(array, 'dst', from_z(step))  14.8 us
    ppermute x1, waiting for transfers between devices, scatter_sources(): swap13 = lax.ppermute(sent13, 'dst', Y_SWAP)  8.36 us
    all_to_all x1, starting transfers between devices, gather_weight(): lax.all_to_all(copies, 'src', 0, 0, tiled=True).reshape(WIDTH, WIDTH)  8.17 us
  transfers between devices with their start and end apart: 19, of which 8 were waited for; matrix products, arithmetic and copies ran while one was open for 3% of the time, Pallas kernels for 0%

profile of v7, /device:TPU:1, one launch (start us, length us, event | category | flops | bytes accessed | tf_op | source)
XLA Modules:
  0.0 218.0 jit_solution(14684123970032368908)
XLA Ops:
  0.6 28.0 %all-gather = bf16[768,256]{1,0:T(8,128)(2,1)S(1)} all-gather(bf16[192,256]{1,0:T(8,128)(2,1)} %param.6), channel_id=2, replica_groups={{0,8,16,24},{1,9,17,25},{2,10,18,26},{3,11,19,27},{4,12,20,28},{5,13,21..., dimensions={0}, use_global_device_ids=true | all-gather | bytes 491520 | tf_op jit(solution)/shard_map/all_gather | solution.py:199
  28.6 7.3 %all_gather.23.g0 = bf16[4,384,256]{2,1,0:T(8,128)(2,1)S(1)} all-gather(bf16[4,192,256]{2,1,0:T(8,128)(2,1)S(1)} %bitcast.56), channel_id=1, replica_groups={{0,1},{2,3},{4,5},{6,7},{8,9},{10,11},{12,13},{14,15},{16,17},{18,19},{..., dimensions={1}, use_global_device_ids=true | all-gather | bytes 1179648 | tf_op jit(solution)/shard_map/all_gather | solution.py:200
  41.3 4.2 %collective-permute-start.1 = (bf16[2,384,256]{2,1,0:T(8,128)(2,1)S(1)}, bf16[2,384,256]{2,1,0:T(8,128)(2,1)S(1)}, u32[]{:S(2)}, u32[]{:S(2)}) collective-permute-start(bf16[2,384,256]{2,1,0:T(8,128)(2,1)S(1)} %get-tuple-element.43), channel_id=1, source_target_pairs={{2,0},{3,1},{4,2},{5,3},{6,4},{7,5},{8,6},{9,7},{10,8},{11,9},{12,... | collective-permute-start | bytes 1179656 | tf_op jit(solution)/shard_map/ppermute | solution.py:195
  48.1 4.7 %collective-permute-start.2 = (bf16[2,384,256]{2,1,0:T(8,128)(2,1)S(1)}, bf16[2,384,256]{2,1,0:T(8,128)(2,1)S(1)}, u32[]{:S(2)}, u32[]{:S(2)}) collective-permute-start(bf16[2,384,256]{2,1,0:T(8,128)(2,1)S(1)} %collective-permute-done.g1a), channel_id=1, source_target_pairs={{2,0},{3,1},{4,2},{5,3},{6,4},{7,5},{8,6},{9,7},{10,8},{11,9},{12,... | collective-permute-start | bytes 1179656 | tf_op jit(solution)/shard_map/ppermute | solution.py:195
  59.7 3.1 %collective-permute-done.2.g2a = bf16[2,384,256]{2,1,0:T(8,128)(2,1)S(1)} collective-permute-done((bf16[2,384,256]{2,1,0:T(8,128)(2,1)S(1)}, bf16[2,384,256]{2,1,0:T(8,128)(2,1)S(1)}, u32[]{:S(2)}, u32[]{:S(2)}) %collective-permute-start.2) | collective-permute-done | bytes 393248 | tf_op jit(solution)/shard_map/ppermute | solution.py:195
  62.8 5.3 %collective-permute-done.4.g2b = bf16[2,384,256]{2,1,0:T(8,128)(2,1)S(1)} collective-permute-done((bf16[2,384,256]{2,1,0:T(8,128)(2,1)S(1)}, bf16[2,384,256]{2,1,0:T(8,128)(2,1)S(1)}, u32[]{:S(2)}, u32[]{:S(2)}) %collective-permute-start.4) | collective-permute-done | bytes 393248 | tf_op jit(solution)/shard_map/ppermute | solution.py:195
  68.1 4.4 %forward_sums.1 = (bf16[1536,256]{1,0:T(8,128)(2,1)S(1)}, bf16[1536,256]{1,0:T(8,128)(2,1)S(1)}) custom-call(s32[4]{0:T(128)S(1)} %pad_add_fusion.meta, s32[2,144]{1,0:T(2,128)S(1)} %bitcast.46, bf16[144,128,128]{2,1,0:T(8,128)(2,1)S(1)} %broadcast_select_fusion.1.blocks, bf16[4,384,256]{2,1,0:T(8,128)(2,1)S(1)} %all_gather.23.g0, ...), custom_call_target="tpu_custom_call" | custom-call | tf_op jit(solution)/shard_map/forward_sums/pallas_call | solution.py:87
  72.6 5.7 %collective-permute-start.6 = (bf16[1536,256]{1,0:T(8,128)(2,1)S(1)}, bf16[1536,256]{1,0:T(8,128)(2,1)S(1)}, u32[]{:S(2)}, u32[]{:S(2)}) collective-permute-start(bf16[1536,256]{1,0:T(8,128)(2,1)S(1)} %get-tuple-element.23), channel_id=1, source_target_pairs={{0,32},{32,0},{64,96},{96,64},{128,160},{160,128},{192,224},{224,1... | collective-permute-start | bytes 2359304 | tf_op jit(solution)/shard_map/ppermute | solution.py:277
  80.3 17.8 %all_to_all.15.terms = bf16[8,192,256]{2,1,0:T(8,128)(2,1)S(1)} all-to-all(bf16[8,192,256]{2,1,0:T(8,128)(2,1)S(1)} %bitcast.50), channel_id=1, replica_groups={{0,64,128,192,256,320,384,448},{32,96,160,224,288,352,416,480},{1,65,12..., dimensions={0} | all-to-all | bytes 1572864 | tf_op jit(solution)/shard_map/all_to_all | solution.py:279
  99.0 16.6 %all_to_all.16.mine = bf16[8,224,256]{2,1,0:T(8,128)(2,1)S(1)} all-to-all(bf16[8,224,256]{2,1,0:T(8,128)(2,1)S(1)} %get-tuple-element.25), channel_id=1, replica_groups={{0,64,128,192,256,320,384,448},{32,96,160,224,288,352,416,480},{1,65,12..., dimensions={0} | all-to-all | bytes 1835008 | tf_op jit(solution)/shard_map/all_to_all | solution.py:283
  115.6 4.4 %collective-permute-start.7 = (bf16[8,224,256]{2,1,0:T(8,128)(2,1)S(1)}, bf16[8,224,256]{2,1,0:T(8,128)(2,1)S(1)}, u32[]{:S(2)}, u32[]{:S(2)}) collective-permute-start(bf16[8,224,256]{2,1,0:T(8,128)(2,1)S(1)} %all_to_all.16.mine), channel_id=1, source_target_pairs={{0,32},{32,0},{64,96},{96,64},{128,160},{160,128},{192,224},{224,1... | collective-permute-start | bytes 2752520 | tf_op jit(solution)/shard_map/ppermute | solution.py:284
  122.8 4.6 %backward_sums.1 = (bf16[768,256]{1,0:T(8,128)(2,1)S(1)}, bf16[768,256]{1,0:T(8,128)(2,1)S(1)}, bf16[768,256]{1,0:T(8,128)(2,1)S(1)}, bf16[768,256]{1,0:T(8,128)...) custom-call(s32[4]{0:T(128)S(1)} %pad_add_fusion.meta, ...), custom_call_target="tpu_custom_call" | custom-call | tf_op jit(solution)/shard_map/backward_sums/pallas_call | solution.py:181
  127.4 11.6 %all-gather.1 = bf16[1568,256]{1,0:T(8,128)(2,1)S(1)} all-gather(bf16[784,256]{1,0:T(8,128)(2,1)S(1)} %get-tuple-element.31), channel_id=3, replica_groups={{0,1},{2,3},{4,5},{6,7},{8,9},{10,11},{12,13},{14,15},{16,17},{18,19},{..., dimensions={0}, use_global_device_ids=true | all-gather | bytes 1204224 | tf_op jit(solution)/shard_map/all_gather | solution.py:221
  143.2 3.4 %collective-permute-start.9 = (bf16[384,256]{1,0:T(8,128)(2,1)S(1)}, bf16[384,256]{1,0:T(8,128)(2,1)S(1)}, u32[]{:S(2)}, u32[]{:S(2)}) collective-permute-start(bf16[384,256]{1,0:T(8,128)(2,1)S(1)} %get-tuple-element.36), channel_id=1, source_target_pairs={{30,0},{31,1},{0,2},{1,3},{2,4},{3,5},{4,6},{5,7},{6,8},{7,9},{8,1... | collective-permute-start | bytes 589832 | tf_op jit(solution)/shard_map/ppermute | solution.py:195
  150.8 8.4 %collective-permute-done.8 = bf16[1536,256]{1,0:T(8,128)(2,1)S(1)} collective-permute-done((bf16[1536,256]{1,0:T(8,128)(2,1)S(1)}, bf16[1536,256]{1,0:T(8,128)(2,1)S(1)}, u32[]{:S(2)}, u32[]{:S(2)}) %collective-permute-start.8) | collective-permute-done | bytes 786464 | tf_op jit(solution)/shard_map/ppermute | solution.py:228
  161.4 3.4 %collective-permute-start.11 = (bf16[784,256]{1,0:T(8,128)(2,1)S(1)}, bf16[784,256]{1,0:T(8,128)(2,1)S(1)}, u32[]{:S(2)}, u32[]{:S(2)}) collective-permute-start(bf16[784,256]{1,0:T(8,128)(2,1)S(1)} %get-tuple-element.51), channel_id=1, source_target_pairs={{30,0},{31,1},{0,2},{1,3},{2,4},{3,5},{4,6},{5,7},{6,8},{7,9},{8,1... | collective-permute-start | bytes 1204232 | tf_op jit(solution)/shard_map/ppermute | solution.py:195
  164.8 9.0 %all-gather.2 = bf16[1536,256]{1,0:T(8,128)(2,1)S(1)} all-gather(bf16[768,256]{1,0:T(8,128)(2,1)S(1)} %get-tuple-element.33), channel_id=4, replica_groups={{0,1},{2,3},{4,5},{6,7},{8,9},{10,11},{12,13},{14,15},{16,17},{18,19},{..., dimensions={0}, use_global_device_ids=true | all-gather | bytes 1179648 | tf_op jit(solution)/shard_map/all_gather | solution.py:221
  174.1 6.6 %collective-permute-start.13 = (bf16[112,256]{1,0:T(8,128)(2,1)S(1)}, bf16[112,256]{1,0:T(8,128)(2,1)S(1)}, u32[]{:S(2)}, u32[]{:S(2)}) collective-permute-start(bf16[112,256]{1,0:T(8,128)(2,1)S(1)} %get-tuple-element.49), channel_id=1, source_target_pairs={{24,0},{25,1},{26,2},{27,3},{28,4},{29,5},{30,6},{31,7},{0,8},{1,9... | collective-permute-start | bytes 172040 | tf_op jit(solution)/shard_map/ppermute | solution.py:195
  180.7 3.7 %collective-permute-start.15 = (bf16[112,256]{1,0:T(8,128)(2,1)S(1)}, bf16[112,256]{1,0:T(8,128)(2,1)S(1)}, u32[]{:S(2)}, u32[]{:S(2)}) collective-permute-start(bf16[112,256]{1,0:T(8,128)(2,1)S(1)} %get-tuple-element.50), channel_id=1, source_target_pairs={{8,0},{9,1},{10,2},{11,3},{12,4},{13,5},{14,6},{15,7},{16,8},{17,9... | collective-permute-start | bytes 172040 | tf_op jit(solution)/shard_map/ppermute | solution.py:195
  184.4 7.1 %collective-permute-start.17 = (bf16[16,256]{1,0:T(8,128)(2,1)S(1)}, bf16[16,256]{1,0:T(8,128)(2,1)S(1)}, u32[]{:S(2)}, u32[]{:S(2)}) collective-permute-start(bf16[16,256]{1,0:T(8,128)(2,1)S(1)} %add_convert_fusion.7), channel_id=1, source_target_pairs={{16,0},{17,1},{18,2},{19,3},{20,4},{21,5},{22,6},{23,7},{24,8},{25... | collective-permute-start | bytes 24584 | tf_op jit(solution)/shard_map/ppermute | solution.py:195
  191.6 5.4 %collective-permute-start.16 = (bf16[192,256]{1,0:T(8,128)(2,1)S(1)}, bf16[192,256]{1,0:T(8,128)(2,1)S(1)}, u32[]{:S(2)}, u32[]{:S(2)}) collective-permute-start(bf16[192,256]{1,0:T(8,128)(2,1)S(1)} %get-tuple-element.46), channel_id=1, source_target_pairs={{8,0},{9,1},{10,2},{11,3},{12,4},{13,5},{14,6},{15,7},{16,8},{17,9... | collective-permute-start | bytes 294920 | tf_op jit(solution)/shard_map/ppermute | solution.py:195
  197.0 3.8 %collective-permute-start.14 = (bf16[192,256]{1,0:T(8,128)(2,1)S(1)}, bf16[192,256]{1,0:T(8,128)(2,1)S(1)}, u32[]{:S(2)}, u32[]{:S(2)}) collective-permute-start(bf16[192,256]{1,0:T(8,128)(2,1)S(1)} %get-tuple-element.45), channel_id=1, source_target_pairs={{24,0},{25,1},{26,2},{27,3},{28,4},{29,5},{30,6},{31,7},{0,8},{1,9... | collective-permute-start | bytes 294920 | tf_op jit(solution)/shard_map/ppermute | solution.py:195
  201.5 8.2 %all-to-all-start.2 = ((bf16[16,16,256]{2,1,0:T(8,128)(2,1)}), bf16[16,16,256]{2,1,0:T(8,128)(2,1)S(1)}, u32[]{:S(2)}, u32[]{:S(2)}) async-start(bf16[16,16,256]{2,1,0:T(8,128)(2,1)} %broadcast_in_dim.32), calls=%async_computation.2 | async-start | bytes 262144 | tf_op jit(solution)/shard_map/all_to_all | solution.py:257
  210.4 6.9 %all-to-all-done.2 = bf16[16,16,256]{2,1,0:T(8,128)(2,1)S(1)} async-done(((bf16[16,16,256]{2,1,0:T(8,128)(2,1)}), bf16[16,16,256]{2,1,0:T(8,128)(2,1)S(1)}, u32[]{:S(2)}, u32[]{:S(2)}) %all-to-all-start.2) | async-done | bytes 131104 | tf_op jit(solution)/shard_map/all_to_all | solution.py:257
  (54 shorter events, 32.9 us)
Async XLA Ops:
  36.0 12.2 %collective-permute-start = (bf16[2,384,256]{2,1,0:T(8,128)(2,1)S(1)}, bf16[2,384,256]{2,1,0:T(8,128)(2,1)S(1)}, u32[]{:S(2)}, u32[]{:S(2)}) collective-permute-start(bf16[2,384,256]{2,1,0:T(8,128)(2,1)S(1)} %get-tuple-element.44), channel_id=1, source_target_pairs={{2,0},{3,1},{4,2},{5,3},{6,4},{7,5},{8,6},{9,7},{10,8},{11,9},{12,... | collective-permute-start | bytes 1179656 | tf_op jit(solution)/shard_map/ppermute | solution.py:195
  38.9 13.9 %collective-permute-start.3 = (bf16[2,384,256]{2,1,0:T(8,128)(2,1)S(1)}, bf16[2,384,256]{2,1,0:T(8,128)(2,1)S(1)}, u32[]{:S(2)}, u32[]{:S(2)}) collective-permute-start(bf16[2,384,256]{2,1,0:T(8,128)(2,1)S(1)} %get-tuple-element.43), channel_id=1, source_target_pairs={{30,0},{31,1},{0,2},{1,3},{2,4},{3,5},{4,6},{5,7},{6,8},{7,9},{8,1... | collective-permute-start | bytes 1179656 | tf_op jit(solution)/shard_map/ppermute | solution.py:195
  41.3 16.2 %collective-permute-start.1 = (bf16[2,384,256]{2,1,0:T(8,128)(2,1)S(1)}, bf16[2,384,256]{2,1,0:T(8,128)(2,1)S(1)}, u32[]{:S(2)}, u32[]{:S(2)}) collective-permute-start(bf16[2,384,256]{2,1,0:T(8,128)(2,1)S(1)} %get-tuple-element.43), channel_id=1, source_target_pairs={{2,0},{3,1},{4,2},{5,3},{6,4},{7,5},{8,6},{9,7},{10,8},{11,9},{12,... | collective-permute-start | bytes 1179656 | tf_op jit(solution)/shard_map/ppermute | solution.py:195
  45.5 14.2 %collective-permute-start.5 = (bf16[2,384,256]{2,1,0:T(8,128)(2,1)S(1)}, bf16[2,384,256]{2,1,0:T(8,128)(2,1)S(1)}, u32[]{:S(2)}, u32[]{:S(2)}) collective-permute-start(bf16[2,384,256]{2,1,0:T(8,128)(2,1)S(1)} %get-tuple-element.44), channel_id=1, source_target_pairs={{30,0},{31,1},{0,2},{1,3},{2,4},{3,5},{4,6},{5,7},{6,8},{7,9},{8,1... | collective-permute-start | bytes 1179656 | tf_op jit(solution)/shard_map/ppermute | solution.py:195
  48.1 20.0 %copy-start.2 = (s32[1,1,144,2]{2,3,1,0:T(2,128)S(1)}, s32[1,1,144,2]{2,3,1,0:T(2,128)}, u32[]{:S(2)}) copy-start(s32[1,1,144,2]{2,3,1,0:T(2,128)} %param.9) | copy-start | bytes 3460
  48.1 14.7 %collective-permute-start.2 = (bf16[2,384,256]{2,1,0:T(8,128)(2,1)S(1)}, bf16[2,384,256]{2,1,0:T(8,128)(2,1)S(1)}, u32[]{:S(2)}, u32[]{:S(2)}) collective-permute-start(bf16[2,384,256]{2,1,0:T(8,128)(2,1)S(1)} %collective-permute-done.g1a), channel_id=1, source_target_pairs={{2,0},{3,1},{4,2},{5,3},{6,4},{7,5},{8,6},{9,7},{10,8},{11,9},{12,... | collective-permute-start | bytes 1179656 | tf_op jit(solution)/shard_map/ppermute | solution.py:195
  52.9 15.2 %collective-permute-start.4 = (bf16[2,384,256]{2,1,0:T(8,128)(2,1)S(1)}, bf16[2,384,256]{2,1,0:T(8,128)(2,1)S(1)}, u32[]{:S(2)}, u32[]{:S(2)}) collective-permute-start(bf16[2,384,256]{2,1,0:T(8,128)(2,1)S(1)} %collective-permute-done.3.g3b), channel_id=1, source_target_pairs={{30,0},{31,1},{0,2},{1,3},{2,4},{3,5},{4,6},{5,7},{6,8},{7,9},{8,1... | collective-permute-start | bytes 1179656 | tf_op jit(solution)/shard_map/ppermute | solution.py:195
  68.1 30.0 %copy-start = (bf16[256,256]{1,0:T(8,128)(2,1)S(1)}, bf16[256,256]{1,0:T(8,128)(2,1)}, u32[]{:S(2)}) copy-start(bf16[256,256]{1,0:T(8,128)(2,1)} %weight.1) | copy-start | bytes 393220
  68.1 30.0 %copy-start.1 = (bf16[1,192,256]{2,1,0:T(8,128)(2,1)S(1)}, bf16[1,192,256]{2,1,0:T(8,128)(2,1)}, u32[]{:S(2)}) copy-start(bf16[1,192,256]{2,1,0:T(8,128)(2,1)} %param.11) | copy-start | bytes 294916
  72.6 7.6 %collective-permute-start.6 = (bf16[1536,256]{1,0:T(8,128)(2,1)S(1)}, bf16[1536,256]{1,0:T(8,128)(2,1)S(1)}, u32[]{:S(2)}, u32[]{:S(2)}) collective-permute-start(bf16[1536,256]{1,0:T(8,128)(2,1)S(1)} %get-tuple-element.23), channel_id=1, source_target_pairs={{0,32},{32,0},{64,96},{96,64},{128,160},{160,128},{192,224},{224,1... | collective-permute-start | bytes 2359304 | tf_op jit(solution)/shard_map/ppermute | solution.py:277
  115.6 7.2 %collective-permute-start.7 = (bf16[8,224,256]{2,1,0:T(8,128)(2,1)S(1)}, bf16[8,224,256]{2,1,0:T(8,128)(2,1)S(1)}, u32[]{:S(2)}, u32[]{:S(2)}) collective-permute-start(bf16[8,224,256]{2,1,0:T(8,128)(2,1)S(1)} %all_to_all.16.mine), channel_id=1, source_target_pairs={{0,32},{32,0},{64,96},{96,64},{128,160},{160,128},{192,224},{224,1... | collective-permute-start | bytes 2752520 | tf_op jit(solution)/shard_map/ppermute | solution.py:284
  139.0 20.2 %collective-permute-start.8 = (bf16[1536,256]{1,0:T(8,128)(2,1)S(1)}, bf16[1536,256]{1,0:T(8,128)(2,1)S(1)}, u32[]{:S(2)}, u32[]{:S(2)}) collective-permute-start(bf16[1536,256]{1,0:T(8,128)(2,1)S(1)} %get-tuple-element.35), channel_id=1, source_target_pairs={{0,1},{1,0},{2,3},{3,2},{4,5},{5,4},{6,7},{7,6},{8,9},{9,8},{10,11... | collective-permute-start | bytes 2359304 | tf_op jit(solution)/shard_map/ppermute | solution.py:228
  141.2 7.6 %collective-permute-start.10 = (bf16[400,256]{1,0:T(8,128)(2,1)S(1)}, bf16[400,256]{1,0:T(8,128)(2,1)S(1)}, u32[]{:S(2)}, u32[]{:S(2)}) collective-permute-start(bf16[400,256]{1,0:T(8,128)(2,1)S(1)} %pad_maximum_fusion.2), channel_id=1, source_target_pairs={{2,0},{3,1},{4,2},{5,3},{6,4},{7,5},{8,6},{9,7},{10,8},{11,9},{12,... | collective-permute-start | bytes 614408 | tf_op jit(solution)/shard_map/ppermute | solution.py:195
  143.2 7.6 %collective-permute-start.9 = (bf16[384,256]{1,0:T(8,128)(2,1)S(1)}, bf16[384,256]{1,0:T(8,128)(2,1)S(1)}, u32[]{:S(2)}, u32[]{:S(2)}) collective-permute-start(bf16[384,256]{1,0:T(8,128)(2,1)S(1)} %get-tuple-element.36), channel_id=1, source_target_pairs={{30,0},{31,1},{0,2},{1,3},{2,4},{3,5},{4,6},{5,7},{6,8},{7,9},{8,1... | collective-permute-start | bytes 589832 | tf_op jit(solution)/shard_map/ppermute | solution.py:195
  159.5 14.3 %collective-permute-start.12 = (bf16[784,256]{1,0:T(8,128)(2,1)S(1)}, bf16[784,256]{1,0:T(8,128)(2,1)S(1)}, u32[]{:S(2)}, u32[]{:S(2)}) collective-permute-start(bf16[784,256]{1,0:T(8,128)(2,1)S(1)} %get-tuple-element.52), channel_id=1, source_target_pairs={{2,0},{3,1},{4,2},{5,3},{6,4},{7,5},{8,6},{9,7},{10,8},{11,9},{12,... | collective-permute-start | bytes 1204232 | tf_op jit(solution)/shard_map/ppermute | solution.py:195
  161.4 12.4 %collective-permute-start.11 = (bf16[784,256]{1,0:T(8,128)(2,1)S(1)}, bf16[784,256]{1,0:T(8,128)(2,1)S(1)}, u32[]{:S(2)}, u32[]{:S(2)}) collective-permute-start(bf16[784,256]{1,0:T(8,128)(2,1)S(1)} %get-tuple-element.51), channel_id=1, source_target_pairs={{30,0},{31,1},{0,2},{1,3},{2,4},{3,5},{4,6},{5,7},{6,8},{7,9},{8,1... | collective-permute-start | bytes 1204232 | tf_op jit(solution)/shard_map/ppermute | solution.py:195
  174.1 17.4 %collective-permute-start.13 = (bf16[112,256]{1,0:T(8,128)(2,1)S(1)}, bf16[112,256]{1,0:T(8,128)(2,1)S(1)}, u32[]{:S(2)}, u32[]{:S(2)}) collective-permute-start(bf16[112,256]{1,0:T(8,128)(2,1)S(1)} %get-tuple-element.49), channel_id=1, source_target_pairs={{24,0},{25,1},{26,2},{27,3},{28,4},{29,5},{30,6},{31,7},{0,8},{1,9... | collective-permute-start | bytes 172040 | tf_op jit(solution)/shard_map/ppermute | solution.py:195
  180.7 10.8 %collective-permute-start.15 = (bf16[112,256]{1,0:T(8,128)(2,1)S(1)}, bf16[112,256]{1,0:T(8,128)(2,1)S(1)}, u32[]{:S(2)}, u32[]{:S(2)}) collective-permute-start(bf16[112,256]{1,0:T(8,128)(2,1)S(1)} %get-tuple-element.50), channel_id=1, source_target_pairs={{8,0},{9,1},{10,2},{11,3},{12,4},{13,5},{14,6},{15,7},{16,8},{17,9... | collective-permute-start | bytes 172040 | tf_op jit(solution)/shard_map/ppermute | solution.py:195
  184.4 16.4 %collective-permute-start.17 = (bf16[16,256]{1,0:T(8,128)(2,1)S(1)}, bf16[16,256]{1,0:T(8,128)(2,1)S(1)}, u32[]{:S(2)}, u32[]{:S(2)}) collective-permute-start(bf16[16,256]{1,0:T(8,128)(2,1)S(1)} %add_convert_fusion.7), channel_id=1, source_target_pairs={{16,0},{17,1},{18,2},{19,3},{20,4},{21,5},{22,6},{23,7},{24,8},{25... | collective-permute-start | bytes 24584 | tf_op jit(solution)/shard_map/ppermute | solution.py:195
  191.6 18.1 %collective-permute-start.16 = (bf16[192,256]{1,0:T(8,128)(2,1)S(1)}, bf16[192,256]{1,0:T(8,128)(2,1)S(1)}, u32[]{:S(2)}, u32[]{:S(2)}) collective-permute-start(bf16[192,256]{1,0:T(8,128)(2,1)S(1)} %get-tuple-element.46), channel_id=1, source_target_pairs={{8,0},{9,1},{10,2},{11,3},{12,4},{13,5},{14,6},{15,7},{16,8},{17,9... | collective-permute-start | bytes 294920 | tf_op jit(solution)/shard_map/ppermute | solution.py:195
  197.0 12.7 %collective-permute-start.14 = (bf16[192,256]{1,0:T(8,128)(2,1)S(1)}, bf16[192,256]{1,0:T(8,128)(2,1)S(1)}, u32[]{:S(2)}, u32[]{:S(2)}) collective-permute-start(bf16[192,256]{1,0:T(8,128)(2,1)S(1)} %get-tuple-element.45), channel_id=1, source_target_pairs={{24,0},{25,1},{26,2},{27,3},{28,4},{29,5},{30,6},{31,7},{0,8},{1,9... | collective-permute-start | bytes 294920 | tf_op jit(solution)/shard_map/ppermute | solution.py:195
  201.5 15.8 %all-to-all-start.2 = ((bf16[16,16,256]{2,1,0:T(8,128)(2,1)}), bf16[16,16,256]{2,1,0:T(8,128)(2,1)S(1)}, u32[]{:S(2)}, u32[]{:S(2)}) async-start(bf16[16,16,256]{2,1,0:T(8,128)(2,1)} %broadcast_in_dim.32), calls=%async_computation.2 | async-start | bytes 262144 | tf_op jit(solution)/shard_map/all_to_all | solution.py:257

commit v8 on v7

--- a/solution.py
+++ b/solution.py
@@ -31,7 +31,7 @@
 
 def each_slot(slot_count, one_slot):
     done = 0
-    for step in (36, 12, 4, 1):
+    for step in (48, 16, 4, 1):
 
         def several(i, carry, step=step, done=done):
             one_slot([done + i * step + u for u in range(step)])

time: 219 us -> 218 us (level)
  blocking collectives: 90.3 us -> 94.1 us
  starting transfers between devices: 75.5 us -> 72.1 us
    all_to_all x1, blocking collectives: 17.8 us -> 21.2 us  [shards(): lax.all_to_all(chip_sums.reshape(CHIPS, ROWS, WIDTH), 'src', 0, 0, tiled=...]
    ppermute x15, starting transfers between devices: 55.1 us -> 52.1 us  [shift(): return lax.ppermute(array, 'dst', from_z(step))]
  transfers between devices with their start and end apart: 19 -> 19, of which waited for: 8 -> 9; matrix products, arithmetic and copies ran while one was open for 3% -> 3% of each run, Pallas kernels for 0% -> 0%
where the time goes in v8:
time: 218 us; the launch traced here: 217 us
  blocking collectives  94.1 us (43%)
  starting transfers between devices  72.1 us (33%)
  waiting for transfers between devices  32.8 us (15%)
  Pallas kernels  7.96 us (4%)
  other arithmetic  7.92 us (4%)
    ppermute x15, starting transfers between devices, shift(): return lax.ppermute(array, 'dst', from_z(step))  52.1 us
    all_gather x1, blocking collectives, gather_sources(): lax.all_gather(features, 'dst', axis=0, axis_index_groups=STRIDE_GROUPS)  28 us
    all_to_all x1, blocking collectives, shards(): lax.all_to_all(chip_sums.reshape(CHIPS, ROWS, WIDTH), 'src', 0, 0, tiled=...  21.2 us
    all_gather x2, blocking collectives, pair_swap(): both = lax.all_gather(array, axis, axis=0, axis_index_groups=groups)  21 us
    ppermute x15, waiting for transfers between devices, shift(): return lax.ppermute(array, 'dst', from_z(step))  16.6 us
    all_to_all x1, blocking collectives, shards(): lax.all_to_all(message, 'src', 0, 0, tiled=True, axis_index_groups=CORE_G...  16.6 us
    all_to_all x1, starting transfers between devices, gather_weight(): lax.all_to_all(copies, 'src', 0, 0, tiled=True).reshape(WIDTH, WIDTH)  8.07 us
    ppermute x1, waiting for transfers between devices, scatter_sources(): swap13 = lax.ppermute(sent13, 'dst', Y_SWAP)  7.37 us
  transfers between devices with their start and end apart: 19, of which 9 were waited for; matrix products, arithmetic and copies ran while one was open for 3% of the time, Pallas kernels for 0%

profile of v8, /device:TPU:1, one launch (start us, length us, event | category | flops | bytes accessed | tf_op | source)
XLA Modules:
  0.0 217.3 jit_solution(6892622532188826073)
XLA Ops:
  0.6 28.0 %all-gather = bf16[768,256]{1,0:T(8,128)(2,1)S(1)} all-gather(bf16[192,256]{1,0:T(8,128)(2,1)} %param.6), channel_id=2, replica_groups={{0,8,16,24},{1,9,17,25},{2,10,18,26},{3,11,19,27},{4,12,20,28},{5,13,21..., dimensions={0}, use_global_device_ids=true | all-gather | bytes 491520 | tf_op jit(solution)/shard_map/all_gather | solution.py:199
  28.6 7.3 %all_gather.23.g0 = bf16[4,384,256]{2,1,0:T(8,128)(2,1)S(1)} all-gather(bf16[4,192,256]{2,1,0:T(8,128)(2,1)S(1)} %bitcast.56), channel_id=1, replica_groups={{0,1},{2,3},{4,5},{6,7},{8,9},{10,11},{12,13},{14,15},{16,17},{18,19},{..., dimensions={1}, use_global_device_ids=true | all-gather | bytes 1179648 | tf_op jit(solution)/shard_map/all_gather | solution.py:200
  41.3 4.2 %collective-permute-start.1 = (bf16[2,384,256]{2,1,0:T(8,128)(2,1)S(1)}, bf16[2,384,256]{2,1,0:T(8,128)(2,1)S(1)}, u32[]{:S(2)}, u32[]{:S(2)}) collective-permute-start(bf16[2,384,256]{2,1,0:T(8,128)(2,1)S(1)} %get-tuple-element.43), channel_id=1, source_target_pairs={{2,0},{3,1},{4,2},{5,3},{6,4},{7,5},{8,6},{9,7},{10,8},{11,9},{12,... | collective-permute-start | bytes 1179656 | tf_op jit(solution)/shard_map/ppermute | solution.py:195
  48.1 4.7 %collective-permute-start.2 = (bf16[2,384,256]{2,1,0:T(8,128)(2,1)S(1)}, bf16[2,384,256]{2,1,0:T(8,128)(2,1)S(1)}, u32[]{:S(2)}, u32[]{:S(2)}) collective-permute-start(bf16[2,384,256]{2,1,0:T(8,128)(2,1)S(1)} %collective-permute-done.g1a), channel_id=1, source_target_pairs={{2,0},{3,1},{4,2},{5,3},{6,4},{7,5},{8,6},{9,7},{10,8},{11,9},{12,... | collective-permute-start | bytes 1179656 | tf_op jit(solution)/shard_map/ppermute | solution.py:195
  59.7 3.1 %collective-permute-done.2.g2a = bf16[2,384,256]{2,1,0:T(8,128)(2,1)S(1)} collective-permute-done((bf16[2,384,256]{2,1,0:T(8,128)(2,1)S(1)}, bf16[2,384,256]{2,1,0:T(8,128)(2,1)S(1)}, u32[]{:S(2)}, u32[]{:S(2)}) %collective-permute-start.2) | collective-permute-done | bytes 393248 | tf_op jit(solution)/shard_map/ppermute | solution.py:195
  62.8 5.3 %collective-permute-done.4.g2b = bf16[2,384,256]{2,1,0:T(8,128)(2,1)S(1)} collective-permute-done((bf16[2,384,256]{2,1,0:T(8,128)(2,1)S(1)}, bf16[2,384,256]{2,1,0:T(8,128)(2,1)S(1)}, u32[]{:S(2)}, u32[]{:S(2)}) %collective-permute-start.4) | collective-permute-done | bytes 393248 | tf_op jit(solution)/shard_map/ppermute | solution.py:195
  68.1 3.5 %forward_sums.1 = (bf16[1536,256]{1,0:T(8,128)(2,1)S(1)}, bf16[1536,256]{1,0:T(8,128)(2,1)S(1)}) custom-call(s32[4]{0:T(128)S(1)} %pad_add_fusion.meta, s32[2,144]{1,0:T(2,128)S(1)} %bitcast.46, bf16[144,128,128]{2,1,0:T(8,128)(2,1)S(1)} %broadcast_select_fusion.1.blocks, bf16[4,384,256]{2,1,0:T(8,128)(2,1)S(1)} %all_gather.23.g0, ...), custom_call_target="tpu_custom_call" | custom-call | tf_op jit(solution)/shard_map/forward_sums/pallas_call | solution.py:87
  71.6 5.5 %collective-permute-start.6 = (bf16[1536,256]{1,0:T(8,128)(2,1)S(1)}, bf16[1536,256]{1,0:T(8,128)(2,1)S(1)}, u32[]{:S(2)}, u32[]{:S(2)}) collective-permute-start(bf16[1536,256]{1,0:T(8,128)(2,1)S(1)} %get-tuple-element.23), channel_id=1, source_target_pairs={{0,32},{32,0},{64,96},{96,64},{128,160},{160,128},{192,224},{224,1... | collective-permute-start | bytes 2359304 | tf_op jit(solution)/shard_map/ppermute | solution.py:277
  79.2 21.2 %all_to_all.15.terms = bf16[8,192,256]{2,1,0:T(8,128)(2,1)S(1)} all-to-all(bf16[8,192,256]{2,1,0:T(8,128)(2,1)S(1)} %bitcast.50), channel_id=1, replica_groups={{0,64,128,192,256,320,384,448},{32,96,160,224,288,352,416,480},{1,65,12..., dimensions={0} | all-to-all | bytes 1572864 | tf_op jit(solution)/shard_map/all_to_all | solution.py:279
  101.3 16.6 %all_to_all.16.mine = bf16[8,224,256]{2,1,0:T(8,128)(2,1)S(1)} all-to-all(bf16[8,224,256]{2,1,0:T(8,128)(2,1)S(1)} %get-tuple-element.25), channel_id=1, replica_groups={{0,64,128,192,256,320,384,448},{32,96,160,224,288,352,416,480},{1,65,12..., dimensions={0} | all-to-all | bytes 1835008 | tf_op jit(solution)/shard_map/all_to_all | solution.py:283
  117.9 4.4 %collective-permute-start.7 = (bf16[8,224,256]{2,1,0:T(8,128)(2,1)S(1)}, bf16[8,224,256]{2,1,0:T(8,128)(2,1)S(1)}, u32[]{:S(2)}, u32[]{:S(2)}) collective-permute-start(bf16[8,224,256]{2,1,0:T(8,128)(2,1)S(1)} %all_to_all.16.mine), channel_id=1, source_target_pairs={{0,32},{32,0},{64,96},{96,64},{128,160},{160,128},{192,224},{224,1... | collective-permute-start | bytes 2752520 | tf_op jit(solution)/shard_map/ppermute | solution.py:284
  125.1 3.6 %backward_sums.1 = (bf16[768,256]{1,0:T(8,128)(2,1)S(1)}, bf16[768,256]{1,0:T(8,128)(2,1)S(1)}, bf16[768,256]{1,0:T(8,128)(2,1)S(1)}, bf16[768,256]{1,0:T(8,128)...) custom-call(s32[4]{0:T(128)S(1)} %pad_add_fusion.meta, ...), custom_call_target="tpu_custom_call" | custom-call | tf_op jit(solution)/shard_map/backward_sums/pallas_call | solution.py:181
  128.6 11.8 %all-gather.1 = bf16[1568,256]{1,0:T(8,128)(2,1)S(1)} all-gather(bf16[784,256]{1,0:T(8,128)(2,1)S(1)} %get-tuple-element.31), channel_id=3, replica_groups={{0,1},{2,3},{4,5},{6,7},{8,9},{10,11},{12,13},{14,15},{16,17},{18,19},{..., dimensions={0}, use_global_device_ids=true | all-gather | bytes 1204224 | tf_op jit(solution)/shard_map/all_gather | solution.py:221
  144.5 3.4 %collective-permute-start.9 = (bf16[384,256]{1,0:T(8,128)(2,1)S(1)}, bf16[384,256]{1,0:T(8,128)(2,1)S(1)}, u32[]{:S(2)}, u32[]{:S(2)}) collective-permute-start(bf16[384,256]{1,0:T(8,128)(2,1)S(1)} %get-tuple-element.36), channel_id=1, source_target_pairs={{30,0},{31,1},{0,2},{1,3},{2,4},{3,5},{4,6},{5,7},{6,8},{7,9},{8,1... | collective-permute-start | bytes 589832 | tf_op jit(solution)/shard_map/ppermute | solution.py:195
  153.4 7.4 %collective-permute-done.8 = bf16[1536,256]{1,0:T(8,128)(2,1)S(1)} collective-permute-done((bf16[1536,256]{1,0:T(8,128)(2,1)S(1)}, bf16[1536,256]{1,0:T(8,128)(2,1)S(1)}, u32[]{:S(2)}, u32[]{:S(2)}) %collective-permute-start.8) | collective-permute-done | bytes 786464 | tf_op jit(solution)/shard_map/ppermute | solution.py:228
  163.1 3.4 %collective-permute-start.11 = (bf16[784,256]{1,0:T(8,128)(2,1)S(1)}, bf16[784,256]{1,0:T(8,128)(2,1)S(1)}, u32[]{:S(2)}, u32[]{:S(2)}) collective-permute-start(bf16[784,256]{1,0:T(8,128)(2,1)S(1)} %get-tuple-element.51), channel_id=1, source_target_pairs={{30,0},{31,1},{0,2},{1,3},{2,4},{3,5},{4,6},{5,7},{6,8},{7,9},{8,1... | collective-permute-start | bytes 1204232 | tf_op jit(solution)/shard_map/ppermute | solution.py:195
  166.4 9.2 %all-gather.2 = bf16[1536,256]{1,0:T(8,128)(2,1)S(1)} all-gather(bf16[768,256]{1,0:T(8,128)(2,1)S(1)} %get-tuple-element.33), channel_id=4, replica_groups={{0,1},{2,3},{4,5},{6,7},{8,9},{10,11},{12,13},{14,15},{16,17},{18,19},{..., dimensions={0}, use_global_device_ids=true | all-gather | bytes 1179648 | tf_op jit(solution)/shard_map/all_gather | solution.py:221
  175.9 4.9 %collective-permute-start.13 = (bf16[112,256]{1,0:T(8,128)(2,1)S(1)}, bf16[112,256]{1,0:T(8,128)(2,1)S(1)}, u32[]{:S(2)}, u32[]{:S(2)}) collective-permute-start(bf16[112,256]{1,0:T(8,128)(2,1)S(1)} %get-tuple-element.49), channel_id=1, source_target_pairs={{24,0},{25,1},{26,2},{27,3},{28,4},{29,5},{30,6},{31,7},{0,8},{1,9... | collective-permute-start | bytes 172040 | tf_op jit(solution)/shard_map/ppermute | solution.py:195
  180.8 4.3 %collective-permute-start.15 = (bf16[112,256]{1,0:T(8,128)(2,1)S(1)}, bf16[112,256]{1,0:T(8,128)(2,1)S(1)}, u32[]{:S(2)}, u32[]{:S(2)}) collective-permute-start(bf16[112,256]{1,0:T(8,128)(2,1)S(1)} %get-tuple-element.50), channel_id=1, source_target_pairs={{8,0},{9,1},{10,2},{11,3},{12,4},{13,5},{14,6},{15,7},{16,8},{17,9... | collective-permute-start | bytes 172040 | tf_op jit(solution)/shard_map/ppermute | solution.py:195
  185.1 5.2 %collective-permute-start.17 = (bf16[16,256]{1,0:T(8,128)(2,1)S(1)}, bf16[16,256]{1,0:T(8,128)(2,1)S(1)}, u32[]{:S(2)}, u32[]{:S(2)}) collective-permute-start(bf16[16,256]{1,0:T(8,128)(2,1)S(1)} %add_convert_fusion.7), channel_id=1, source_target_pairs={{16,0},{17,1},{18,2},{19,3},{20,4},{21,5},{22,6},{23,7},{24,8},{25... | collective-permute-start | bytes 24584 | tf_op jit(solution)/shard_map/ppermute | solution.py:195
  191.0 6.1 %collective-permute-start.16 = (bf16[192,256]{1,0:T(8,128)(2,1)S(1)}, bf16[192,256]{1,0:T(8,128)(2,1)S(1)}, u32[]{:S(2)}, u32[]{:S(2)}) collective-permute-start(bf16[192,256]{1,0:T(8,128)(2,1)S(1)} %get-tuple-element.46), channel_id=1, source_target_pairs={{8,0},{9,1},{10,2},{11,3},{12,4},{13,5},{14,6},{15,7},{16,8},{17,9... | collective-permute-start | bytes 294920 | tf_op jit(solution)/shard_map/ppermute | solution.py:195
  197.1 3.1 %collective-permute-start.14 = (bf16[192,256]{1,0:T(8,128)(2,1)S(1)}, bf16[192,256]{1,0:T(8,128)(2,1)S(1)}, u32[]{:S(2)}, u32[]{:S(2)}) collective-permute-start(bf16[192,256]{1,0:T(8,128)(2,1)S(1)} %get-tuple-element.45), channel_id=1, source_target_pairs={{24,0},{25,1},{26,2},{27,3},{28,4},{29,5},{30,6},{31,7},{0,8},{1,9... | collective-permute-start | bytes 294920 | tf_op jit(solution)/shard_map/ppermute | solution.py:195
  200.9 8.1 %all-to-all-start.2 = ((bf16[16,16,256]{2,1,0:T(8,128)(2,1)}), bf16[16,16,256]{2,1,0:T(8,128)(2,1)S(1)}, u32[]{:S(2)}, u32[]{:S(2)}) async-start(bf16[16,16,256]{2,1,0:T(8,128)(2,1)} %broadcast_in_dim.32), calls=%async_computation.2 | async-start | bytes 262144 | tf_op jit(solution)/shard_map/all_to_all | solution.py:257
  209.6 7.0 %all-to-all-done.2 = bf16[16,16,256]{2,1,0:T(8,128)(2,1)S(1)} async-done(((bf16[16,16,256]{2,1,0:T(8,128)(2,1)}), bf16[16,16,256]{2,1,0:T(8,128)(2,1)S(1)}, u32[]{:S(2)}, u32[]{:S(2)}) %all-to-all-start.2) | async-done | bytes 131104 | tf_op jit(solution)/shard_map/all_to_all | solution.py:257
  (54 shorter events, 34.6 us)
Async XLA Ops:
  36.0 12.2 %collective-permute-start = (bf16[2,384,256]{2,1,0:T(8,128)(2,1)S(1)}, bf16[2,384,256]{2,1,0:T(8,128)(2,1)S(1)}, u32[]{:S(2)}, u32[]{:S(2)}) collective-permute-start(bf16[2,384,256]{2,1,0:T(8,128)(2,1)S(1)} %get-tuple-element.44), channel_id=1, source_target_pairs={{2,0},{3,1},{4,2},{5,3},{6,4},{7,5},{8,6},{9,7},{10,8},{11,9},{12,... | collective-permute-start | bytes 1179656 | tf_op jit(solution)/shard_map/ppermute | solution.py:195
  38.9 13.9 %collective-permute-start.3 = (bf16[2,384,256]{2,1,0:T(8,128)(2,1)S(1)}, bf16[2,384,256]{2,1,0:T(8,128)(2,1)S(1)}, u32[]{:S(2)}, u32[]{:S(2)}) collective-permute-start(bf16[2,384,256]{2,1,0:T(8,128)(2,1)S(1)} %get-tuple-element.43), channel_id=1, source_target_pairs={{30,0},{31,1},{0,2},{1,3},{2,4},{3,5},{4,6},{5,7},{6,8},{7,9},{8,1... | collective-permute-start | bytes 1179656 | tf_op jit(solution)/shard_map/ppermute | solution.py:195
  41.3 16.2 %collective-permute-start.1 = (bf16[2,384,256]{2,1,0:T(8,128)(2,1)S(1)}, bf16[2,384,256]{2,1,0:T(8,128)(2,1)S(1)}, u32[]{:S(2)}, u32[]{:S(2)}) collective-permute-start(bf16[2,384,256]{2,1,0:T(8,128)(2,1)S(1)} %get-tuple-element.43), channel_id=1, source_target_pairs={{2,0},{3,1},{4,2},{5,3},{6,4},{7,5},{8,6},{9,7},{10,8},{11,9},{12,... | collective-permute-start | bytes 1179656 | tf_op jit(solution)/shard_map/ppermute | solution.py:195
  45.5 14.2 %collective-permute-start.5 = (bf16[2,384,256]{2,1,0:T(8,128)(2,1)S(1)}, bf16[2,384,256]{2,1,0:T(8,128)(2,1)S(1)}, u32[]{:S(2)}, u32[]{:S(2)}) collective-permute-start(bf16[2,384,256]{2,1,0:T(8,128)(2,1)S(1)} %get-tuple-element.44), channel_id=1, source_target_pairs={{30,0},{31,1},{0,2},{1,3},{2,4},{3,5},{4,6},{5,7},{6,8},{7,9},{8,1... | collective-permute-start | bytes 1179656 | tf_op jit(solution)/shard_map/ppermute | solution.py:195
  48.1 20.0 %copy-start.2 = (s32[1,1,144,2]{2,3,1,0:T(2,128)S(1)}, s32[1,1,144,2]{2,3,1,0:T(2,128)}, u32[]{:S(2)}) copy-start(s32[1,1,144,2]{2,3,1,0:T(2,128)} %param.9) | copy-start | bytes 3460
  48.1 14.7 %collective-permute-start.2 = (bf16[2,384,256]{2,1,0:T(8,128)(2,1)S(1)}, bf16[2,384,256]{2,1,0:T(8,128)(2,1)S(1)}, u32[]{:S(2)}, u32[]{:S(2)}) collective-permute-start(bf16[2,384,256]{2,1,0:T(8,128)(2,1)S(1)} %collective-permute-done.g1a), channel_id=1, source_target_pairs={{2,0},{3,1},{4,2},{5,3},{6,4},{7,5},{8,6},{9,7},{10,8},{11,9},{12,... | collective-permute-start | bytes 1179656 | tf_op jit(solution)/shard_map/ppermute | solution.py:195
  52.9 15.2 %collective-permute-start.4 = (bf16[2,384,256]{2,1,0:T(8,128)(2,1)S(1)}, bf16[2,384,256]{2,1,0:T(8,128)(2,1)S(1)}, u32[]{:S(2)}, u32[]{:S(2)}) collective-permute-start(bf16[2,384,256]{2,1,0:T(8,128)(2,1)S(1)} %collective-permute-done.3.g3b), channel_id=1, source_target_pairs={{30,0},{31,1},{0,2},{1,3},{2,4},{3,5},{4,6},{5,7},{6,8},{7,9},{8,1... | collective-permute-start | bytes 1179656 | tf_op jit(solution)/shard_map/ppermute | solution.py:195
  68.1 32.3 %copy-start = (bf16[256,256]{1,0:T(8,128)(2,1)S(1)}, bf16[256,256]{1,0:T(8,128)(2,1)}, u32[]{:S(2)}) copy-start(bf16[256,256]{1,0:T(8,128)(2,1)} %weight.1) | copy-start | bytes 393220
  68.1 32.3 %copy-start.1 = (bf16[1,192,256]{2,1,0:T(8,128)(2,1)S(1)}, bf16[1,192,256]{2,1,0:T(8,128)(2,1)}, u32[]{:S(2)}) copy-start(bf16[1,192,256]{2,1,0:T(8,128)(2,1)} %param.11) | copy-start | bytes 294916
  71.6 7.4 %collective-permute-start.6 = (bf16[1536,256]{1,0:T(8,128)(2,1)S(1)}, bf16[1536,256]{1,0:T(8,128)(2,1)S(1)}, u32[]{:S(2)}, u32[]{:S(2)}) collective-permute-start(bf16[1536,256]{1,0:T(8,128)(2,1)S(1)} %get-tuple-element.23), channel_id=1, source_target_pairs={{0,32},{32,0},{64,96},{96,64},{128,160},{160,128},{192,224},{224,1... | collective-permute-start | bytes 2359304 | tf_op jit(solution)/shard_map/ppermute | solution.py:277
  117.9 7.2 %collective-permute-start.7 = (bf16[8,224,256]{2,1,0:T(8,128)(2,1)S(1)}, bf16[8,224,256]{2,1,0:T(8,128)(2,1)S(1)}, u32[]{:S(2)}, u32[]{:S(2)}) collective-permute-start(bf16[8,224,256]{2,1,0:T(8,128)(2,1)S(1)} %all_to_all.16.mine), channel_id=1, source_target_pairs={{0,32},{32,0},{64,96},{96,64},{128,160},{160,128},{192,224},{224,1... | collective-permute-start | bytes 2752520 | tf_op jit(solution)/shard_map/ppermute | solution.py:284
  140.4 20.4 %collective-permute-start.8 = (bf16[1536,256]{1,0:T(8,128)(2,1)S(1)}, bf16[1536,256]{1,0:T(8,128)(2,1)S(1)}, u32[]{:S(2)}, u32[]{:S(2)}) collective-permute-start(bf16[1536,256]{1,0:T(8,128)(2,1)S(1)} %get-tuple-element.35), channel_id=1, source_target_pairs={{0,1},{1,0},{2,3},{3,2},{4,5},{5,4},{6,7},{7,6},{8,9},{9,8},{10,11... | collective-permute-start | bytes 2359304 | tf_op jit(solution)/shard_map/ppermute | solution.py:228
  142.6 7.8 %collective-permute-start.10 = (bf16[400,256]{1,0:T(8,128)(2,1)S(1)}, bf16[400,256]{1,0:T(8,128)(2,1)S(1)}, u32[]{:S(2)}, u32[]{:S(2)}) collective-permute-start(bf16[400,256]{1,0:T(8,128)(2,1)S(1)} %pad_maximum_fusion.2), channel_id=1, source_target_pairs={{2,0},{3,1},{4,2},{5,3},{6,4},{7,5},{8,6},{9,7},{10,8},{11,9},{12,... | collective-permute-start | bytes 614408 | tf_op jit(solution)/shard_map/ppermute | solution.py:195
  144.5 8.9 %collective-permute-start.9 = (bf16[384,256]{1,0:T(8,128)(2,1)S(1)}, bf16[384,256]{1,0:T(8,128)(2,1)S(1)}, u32[]{:S(2)}, u32[]{:S(2)}) collective-permute-start(bf16[384,256]{1,0:T(8,128)(2,1)S(1)} %get-tuple-element.36), channel_id=1, source_target_pairs={{30,0},{31,1},{0,2},{1,3},{2,4},{3,5},{4,6},{5,7},{6,8},{7,9},{8,1... | collective-permute-start | bytes 589832 | tf_op jit(solution)/shard_map/ppermute | solution.py:195
  161.1 14.5 %collective-permute-start.12 = (bf16[784,256]{1,0:T(8,128)(2,1)S(1)}, bf16[784,256]{1,0:T(8,128)(2,1)S(1)}, u32[]{:S(2)}, u32[]{:S(2)}) collective-permute-start(bf16[784,256]{1,0:T(8,128)(2,1)S(1)} %get-tuple-element.52), channel_id=1, source_target_pairs={{2,0},{3,1},{4,2},{5,3},{6,4},{7,5},{8,6},{9,7},{10,8},{11,9},{12,... | collective-permute-start | bytes 1204232 | tf_op jit(solution)/shard_map/ppermute | solution.py:195
  163.1 12.6 %collective-permute-start.11 = (bf16[784,256]{1,0:T(8,128)(2,1)S(1)}, bf16[784,256]{1,0:T(8,128)(2,1)S(1)}, u32[]{:S(2)}, u32[]{:S(2)}) collective-permute-start(bf16[784,256]{1,0:T(8,128)(2,1)S(1)} %get-tuple-element.51), channel_id=1, source_target_pairs={{30,0},{31,1},{0,2},{1,3},{2,4},{3,5},{4,6},{5,7},{6,8},{7,9},{8,1... | collective-permute-start | bytes 1204232 | tf_op jit(solution)/shard_map/ppermute | solution.py:195
  175.9 14.4 %collective-permute-start.13 = (bf16[112,256]{1,0:T(8,128)(2,1)S(1)}, bf16[112,256]{1,0:T(8,128)(2,1)S(1)}, u32[]{:S(2)}, u32[]{:S(2)}) collective-permute-start(bf16[112,256]{1,0:T(8,128)(2,1)S(1)} %get-tuple-element.49), channel_id=1, source_target_pairs={{24,0},{25,1},{26,2},{27,3},{28,4},{29,5},{30,6},{31,7},{0,8},{1,9... | collective-permute-start | bytes 172040 | tf_op jit(solution)/shard_map/ppermute | solution.py:195
  180.8 10.1 %collective-permute-start.15 = (bf16[112,256]{1,0:T(8,128)(2,1)S(1)}, bf16[112,256]{1,0:T(8,128)(2,1)S(1)}, u32[]{:S(2)}, u32[]{:S(2)}) collective-permute-start(bf16[112,256]{1,0:T(8,128)(2,1)S(1)} %get-tuple-element.50), channel_id=1, source_target_pairs={{8,0},{9,1},{10,2},{11,3},{12,4},{13,5},{14,6},{15,7},{16,8},{17,9... | collective-permute-start | bytes 172040 | tf_op jit(solution)/shard_map/ppermute | solution.py:195
  185.1 15.0 %collective-permute-start.17 = (bf16[16,256]{1,0:T(8,128)(2,1)S(1)}, bf16[16,256]{1,0:T(8,128)(2,1)S(1)}, u32[]{:S(2)}, u32[]{:S(2)}) collective-permute-start(bf16[16,256]{1,0:T(8,128)(2,1)S(1)} %add_convert_fusion.7), channel_id=1, source_target_pairs={{16,0},{17,1},{18,2},{19,3},{20,4},{21,5},{22,6},{23,7},{24,8},{25... | collective-permute-start | bytes 24584 | tf_op jit(solution)/shard_map/ppermute | solution.py:195
  191.0 18.0 %collective-permute-start.16 = (bf16[192,256]{1,0:T(8,128)(2,1)S(1)}, bf16[192,256]{1,0:T(8,128)(2,1)S(1)}, u32[]{:S(2)}, u32[]{:S(2)}) collective-permute-start(bf16[192,256]{1,0:T(8,128)(2,1)S(1)} %get-tuple-element.46), channel_id=1, source_target_pairs={{8,0},{9,1},{10,2},{11,3},{12,4},{13,5},{14,6},{15,7},{16,8},{17,9... | collective-permute-start | bytes 294920 | tf_op jit(solution)/shard_map/ppermute | solution.py:195
  197.1 11.8 %collective-permute-start.14 = (bf16[192,256]{1,0:T(8,128)(2,1)S(1)}, bf16[192,256]{1,0:T(8,128)(2,1)S(1)}, u32[]{:S(2)}, u32[]{:S(2)}) collective-permute-start(bf16[192,256]{1,0:T(8,128)(2,1)S(1)} %get-tuple-element.45), channel_id=1, source_target_pairs={{24,0},{25,1},{26,2},{27,3},{28,4},{29,5},{30,6},{31,7},{0,8},{1,9... | collective-permute-start | bytes 294920 | tf_op jit(solution)/shard_map/ppermute | solution.py:195
  200.9 15.7 %all-to-all-start.2 = ((bf16[16,16,256]{2,1,0:T(8,128)(2,1)}), bf16[16,16,256]{2,1,0:T(8,128)(2,1)S(1)}, u32[]{:S(2)}, u32[]{:S(2)}) async-start(bf16[16,16,256]{2,1,0:T(8,128)(2,1)} %broadcast_in_dim.32), calls=%async_computation.2 | async-start | bytes 262144 | tf_op jit(solution)/shard_map/all_to_all | solution.py:257
